TPU v7x, 32 devices: a whole 2x2x4 slice. The times are simulated.
32 devices in a mesh: grp: 4 (over y, core), tile: 8 (over z, x).
Axes of the slice: x: 2, y: 2, z: 4, core: 2. Of those that a mesh axis runs over, the one named last changes fastest.
Arguments:
- members: float32 [32, 32, 64, 128], P(None, 'grp', 'tile'), may hold values from -6 to 6
- courant: float32 [3, 32, 64, 128], P(None, 'grp', 'tile'), may hold values from -0.08 to 0.08
- turb_energy: float32 [32, 64, 128], P('grp', 'tile'), may hold values from 0.3 to 1
- dissipation: float32 [32, 64, 128], P('grp', 'tile'), may hold values from 1 to 10
- sensor_cells: int32 [8, 32768], P(None, ('grp', 'tile')), may hold values from 0 to 8191, as said below
- sensor_frac: float32 [3, 32768], P(None, ('grp', 'tile')), may hold values from 0 to 1
- sensor_count: int32 [32], P(('grp', 'tile')), may hold values from 1 to 1024, 16384 in all
- obs_var: float32 [16384], P('tile'), may hold values from 0.2 to 1
Outputs:
- trailing: float32 [16384, 16384], P('grp', 'tile')
- factor: float32 [16384, 512], P(('grp', 'tile'))
Inputs may be any that keep to these rules, and one draw needn't show every extreme that they name: `sensor_cells`: slot q lists the eight cells of a cube of 2 x 2 x 2 cells inside its grid block, as local indices (x 8 + y) * 128 + z; entry j is the corner offset by the bits of j (first dimension most significant), entry 0 the lowest corner. `sensor_count`: the counts sum to 16384.
All inputs are finite; a program needn't handle non-finite values. No bound on the sum of `sensor_count` on one device may be relied on, other than what follows from the above.
Results may differ from a plain program's by a relative error of at most 0.0025.
Values sent between devices are 32-bit elements; how exact they have to be, the bound alone decides.
No kernel may reach another device: no remote copies, remote signals or barrier semaphores. Data moves between devices by JAX's collectives and lax.ppermute only.
A program may use at most 192 MiB of HBM per device.

v0:
```python
import jax
import jax.numpy as jnp
from jax import lax
from jax.sharding import PartitionSpec as P

NS = 16384
PANEL = 128
PANELS = 4
SWEEPS = 2
LOC = 8


diffuse_rate = 0.06


def extended(value, sides, width):
    for axis, dim in sides:
        size, length = (lax.axis_size(axis), value.shape[dim])
        up = [(i, (i + 1) % size) for i in range(size - 1)]
        down = [(j, i) for i, j in up]
        last = lax.slice_in_dim(value, length - width, length, axis=dim)
        initial = lax.slice_in_dim(value, 0, width, axis=dim)
        before = lax.ppermute(last, axis, up)
        after = lax.ppermute(initial, axis, down)
        value = jnp.concatenate([before, value, after], axis=dim)
    return value


def spread(value, axis, root):
    mine = lax.axis_index(axis) == root
    return lax.psum(jnp.where(mine, value, jnp.zeros_like(value)), axis)


def window(array_in, spatial, lower_cut, upper_cut):
    pieces = []
    for dimension in range(3):
        extent = array_in.shape[array_in.ndim - 3 + dimension]
        if dimension == spatial:
            pieces.append(slice(lower_cut, extent - upper_cut))
        else:
            pieces.append(slice(1, extent - 1))
    return array_in[(slice(None),) * (array_in.ndim - 3) + tuple(pieces)]


def advance(padded, coefs):
    interior = window(padded, 0, 1, 1)
    change = jnp.zeros_like(interior)
    for spatial in range(3):
        lower_cells = window(padded, spatial, 0, 1)
        upper_cells = window(padded, spatial, 1, 0)
        speed_face = 0.5 * (
            window(coefs[spatial], spatial, 0, 1) + window(coefs[spatial], spatial, 1, 0)
        )
        spread_face = 0.5 * (window(coefs[3], spatial, 0, 1) + window(coefs[3], spatial, 1, 0))
        flux_face = (
            jnp.maximum(speed_face, 0.0) * lower_cells
            + jnp.minimum(speed_face, 0.0) * upper_cells
            + spread_face * (lower_cells - upper_cells)
        )
        dimension = flux_face.ndim - 3 + spatial
        extent = flux_face.shape[dimension]
        change = (
            change
            + lax.slice_in_dim(flux_face, 1, extent, axis=dimension)
            - lax.slice_in_dim(flux_face, 0, extent - 1, axis=dimension)
        )
    return interior - change


def corner_weights(fractions):
    rows_out = []
    for corner in range(8):
        weight_now = jnp.ones_like(fractions[0])
        for spatial in range(3):
            if corner >> 2 - spatial & 1:
                weight_now = weight_now * fractions[spatial]
            else:
                weight_now = weight_now * (1.0 - fractions[spatial])
        rows_out.append(weight_now)
    return jnp.stack(rows_out, 0)


def assemble(left_data, right_data, left_ids, right_ids, right_noise, members_n):
    left_resp = left_data[:members_n].astype(jnp.bfloat16)
    right_resp = right_data[:members_n].astype(jnp.bfloat16)
    covar = lax.dot_general(
        left_resp, right_resp, (((0,), (0,)), ((), ())), preferred_element_type=jnp.float32
    )
    dist_sq = jnp.zeros((left_data.shape[1], right_data.shape[1]), jnp.float32)
    for spatial in range(3):
        gap_now = left_data[members_n + spatial][:, None] - right_data[members_n + spatial][None, :]
        dist_sq = dist_sq + gap_now * gap_now
    taper = 1.0 / (1.0 + dist_sq / (LOC * LOC))
    return taper * covar / (members_n - 1) + jnp.where(
        left_ids[:, None] == right_ids[None, :], right_noise[None, :], 0.0
    )


def per_device(
    members, courant, turb_energy, dissipation, sensor_cells, sensor_frac, sensor_count, obs_var
):
    grp_size = lax.axis_size("grp")
    tile_size = lax.axis_size("tile")
    grp_index = lax.axis_index("grp")
    tile_index = lax.axis_index("tile")
    members_n, cells_x, cells_y, cells_z = members.shape
    slot_count = sensor_cells.shape[1]
    diffusion = diffuse_rate * turb_energy * turb_energy / dissipation
    coefs = jnp.concatenate([courant, diffusion[None]], 0)
    coefs = extended(coefs, (("grp", 1), ("tile", 2)), 1)
    coefs = jnp.pad(coefs, ((0, 0), (0, 0), (0, 0), (1, 1)))
    state = members
    for sweep_index in range(SWEEPS):
        padded = extended(state, (("grp", 1), ("tile", 2)), 1)
        state = advance(jnp.pad(padded, ((0, 0), (0, 0), (0, 0), (1, 1))), coefs)
    anomaly = state - jnp.mean(state, axis=0, keepdims=True)
    picked = jnp.take(anomaly.reshape(members_n, -1), sensor_cells, axis=1)
    response = jnp.sum(picked * corner_weights(sensor_frac)[None], axis=1).astype(jnp.bfloat16)
    base_cells = sensor_cells[0]
    local_x = base_cells // (cells_y * cells_z)
    local_y = base_cells // cells_z % cells_y
    local_z = base_cells % cells_z
    position = jnp.stack(
        [
            (grp_index * cells_x + local_x).astype(jnp.float32) + sensor_frac[0],
            (tile_index * cells_y + local_y).astype(jnp.float32) + sensor_frac[1],
            local_z.astype(jnp.float32) + sensor_frac[2],
        ],
        0,
    )
    message = jnp.concatenate([lax.optimization_barrier(response).astype(jnp.float32), position], 0)
    slot_iota = jnp.arange(slot_count, dtype=jnp.int32)
    blank = jnp.zeros((members_n + 3, NS), jnp.float32)
    counts_all = lax.all_gather(sensor_count, ("grp", "tile"), axis=0, tiled=True)
    offsets = jnp.cumsum(counts_all) - counts_all
    block_total = counts_all.shape[0]
    slot_offsets = jnp.repeat(offsets, slot_count, total_repeat_length=block_total * slot_count)
    slot_limits = jnp.repeat(counts_all, slot_count, total_repeat_length=block_total * slot_count)
    local_slot = jnp.tile(slot_iota, block_total)
    packed = jnp.where(local_slot < slot_limits, slot_offsets + local_slot, NS)
    everything = lax.all_gather(message, ("grp", "tile"), axis=1, tiled=True)
    full = blank.at[:, packed].set(everything, mode="drop")
    row_span = NS // grp_size
    col_span = NS // tile_size
    row_data = lax.dynamic_slice_in_dim(full, grp_index * row_span, row_span, 1)
    col_data = lax.dynamic_slice_in_dim(full, tile_index * col_span, col_span, 1)
    row_ids = grp_index * row_span + jnp.arange(row_span, dtype=jnp.int32)
    col_ids = tile_index * col_span + jnp.arange(col_span, dtype=jnp.int32)
    matrix = assemble(row_data, col_data, row_ids, col_ids, obs_var, members_n)
    share_rows = row_span // tile_size
    columns_out = []
    for panel_index in range(PANELS):
        start = panel_index * PANEL
        tile_root = start // col_span
        col_start = start % col_span
        grp_root = start // row_span
        row_start = start % row_span
        rows_block = spread(matrix[:, col_start : col_start + PANEL], "tile", tile_root)
        diag_part = spread(rows_block[row_start : row_start + PANEL], "grp", grp_root)
        lower_block = jnp.linalg.cholesky(diag_part)
        factor_rows = lax.linalg.triangular_solve(
            lower_block, rows_block, left_side=False, lower=True, transpose_a=True
        )
        factor_rows = jnp.where((row_ids >= start)[:, None], factor_rows, 0.0)
        source_rows = lax.dynamic_slice_in_dim(
            factor_rows, tile_index * col_span % row_span, col_span, 0
        )
        factor_cols = spread(source_rows, "grp", tile_index * col_span // row_span)
        matrix = matrix - jnp.dot(
            factor_rows,
            factor_cols.T,
            preferred_element_type=jnp.float32,
            precision=lax.Precision.HIGHEST,
        )
        columns_out.append(
            lax.dynamic_slice_in_dim(factor_rows, tile_index * share_rows, share_rows, 0)
        )
    return (matrix, jnp.concatenate(columns_out, 1))


def solution(mesh):
    return jax.shard_map(
        per_device,
        mesh=mesh,
        in_specs=(
            P(None, "grp", "tile", None),
            P(None, "grp", "tile", None),
            P("grp", "tile", None),
            P("grp", "tile", None),
            P(None, ("grp", "tile")),
            P(None, ("grp", "tile")),
            P(("grp", "tile")),
            P("tile"),
        ),
        out_specs=(P("grp", "tile"), P(("grp", "tile"), None)),
        check_vma=False,
    )
```

profile of v0, /device:TPU:0, one launch (start us, length us, event | category | flops | bytes accessed | tf_op | source)
XLA Modules:
  0.0 1334.3 jit_solution(16394799693329458357)
XLA Ops:
  13.4 5.2 collective-permute-start.4
  22.8 3.4 collective-permute-start.2
  28.4 3.4 collective-permute-done.3
  34.4 4.4 collective-permute-start.6
  40.5 6.3 collective-permute-done.6
  53.7 4.3 collective-permute-done.9
  58.0 3.4 collective-permute-start.10
  64.2 4.4 collective-permute-done.11
  75.2 29.9 %gather_fusion = f32[8192,32]{1,0:T(8,128)} fusion(f32[32,8192]{0,1:T(8,128)} %bitcast.291, s32[8192]{0:T(1024)S(1)} %bitcast_clamp_fusion), kind=kCustom, calls=%fused_computation | custom fusion | bytes 2129920 | tf_op jit(solution)/shard_map/jit(_take)/gather | solution.py:117
  105.1 6.1 multiply_reduce_fusion
  112.9 43.4 %all-reduce.4 = s32[32]{0:T(128)S(1)} all-reduce(s32[32]{0:T(128)S(1)} %dynamic-update-slice.6), channel_id=1, replica_groups=mesh['grp'=4,'tile'=8] {'grp','tile'}, use_global_device_ids=true, to_apply=%add.4 | all-reduce | flops 32 | bytes 256
  159.6 40.5 %compare_select_fusion.1 = s32[32768]{0:T(1024)S(1)} fusion(s32[32768]{0:T(1024)S(1)} %bitcast.295, s32[256,128]{1,0:T(8,128)S(1)} %copy-done.7, s32[]{:T(128)} %bitcast.66, s32[]{:T(128)} %bitcast.65, s32[]{:T(128)} %bitcast.64, s32[]{:T(128)} %bitcast.63, s32[]{:T(128)} %bitcast.62, s32[]{:T(128)} %bitcast.61, s32[]{:T(128)} %bitcast.60, s32[]{:T(128)} %bitcast.59, ...), kind=kLoop, calls=%fused_computation.82 | loop fusion | flops 3571712 | bytes 394496 | tf_op jit(solution)/shard_map/select_n | solution.py:142
  200.1 11.1 copy.92
  211.2 84.0 %scatter_custom_fusion = f32[35,16384]{0,1:T(8,128)} fusion(s32[32768]{0:T(1024)S(1)} %compare_select_fusion.1, f32[32768,35]{1,0:T(8,128)} %copy.92, f32[]{:T(128)} %constant.240.clone.1), kind=kCustom, calls=%fused_computation.18 | custom fusion | bytes 2294272 | tf_op jit(solution)/shard_map/scatter | solution.py:142
  295.2 3.8 dynamic-slice_reduce_fusion.5
  299.0 6.3 dynamic-slice_reduce_fusion.2
  305.3 20.7 %select_add_fusion = f32[4096,2048]{0,1:T(8,128)S(1)} fusion(f32[2048]{0:T(1024)S(1)} %copy-done.9, s32[4096]{0:T(1024)S(1)} %iota_add_fusion, f32[2048]{0:T(1024)S(1)} %get-tuple-element.40, f32[4096]{0:T(1024)S(1)} %get-tuple-element.36, f32[2048]{0:T(1024)S(1)} %get-tuple-element.39, f32[4096]{0:T(1024)S(1)} %get-tuple-element.37, ...), kind=kOutput, calls=%fused_computation.2 | convolution fusion | flops 671088640 | bytes 35233800 | tf_op jit(solution)/shard_map/dot_general | solution.py:86
  326.0 11.7 copy-done
  339.2 101.2 %all-reduce.18.cloned.1.call-done = f32[4096,128]{0,1:T(8,128)} async-done(((f32[4096,128]{0,1:T(8,128)}), f32[4096,128]{0,1:T(8,128)}) %all-reduce.18.cloned.1.call-update) | async-done | bytes 2097168 | tf_op jit(solution)/shard_map/psum | solution.py:31
  442.2 31.9 %all-reduce.20.cloned.1.call-done = f32[128,128]{0,1:T(8,128)} async-done(((f32[128,128]{0,1:T(8,128)}), f32[128,128]{0,1:T(8,128)}) %all-reduce.20.cloned.1.call-update) | async-done | bytes 65552 | tf_op jit(solution)/shard_map/psum | solution.py:31
  475.9 11.7 cholesky.74
  489.0 9.8 custom-call.8
  498.8 3.5 fusion.3
  503.8 35.8 %all-reduce.22.cloned.1.call-done = f32[2048,128]{0,1:T(8,128)} async-done(((f32[2048,128]{0,1:T(8,128)}), f32[2048,128]{0,1:T(8,128)}) %all-reduce.22.cloned.1.call-update) | async-done | bytes 1048592 | tf_op jit(solution)/shard_map/psum | solution.py:31
  539.6 34.1 %convolution_subtract_fusion.3 = f32[4096,2048]{0,1:T(8,128)} fusion(f32[4096,2048]{0,1:T(8,128)} %copy-done, f32[4096,128]{0,1:T(8,128)S(1)} %fusion.3, f32[2048,128]{0,1:T(8,128)} %all-reduce.22.cloned.1.call-done), kind=kOutput, calls=%fused_computation.6 | convolution fusion | flops 12893290496 | bytes 70254592 | tf_op jit(solution)/shard_map/dot_general | solution.py:169
  576.8 102.3 %all-reduce.24.cloned.1.call-done = f32[4096,128]{0,1:T(8,128)} async-done(((f32[4096,128]{0,1:T(8,128)}), f32[4096,128]{0,1:T(8,128)}) %all-reduce.24.cloned.1.call-update) | async-done | bytes 2097168 | tf_op jit(solution)/shard_map/psum | solution.py:31
  680.9 31.8 %all-reduce.26.cloned.1.call-done = f32[128,128]{0,1:T(8,128)} async-done(((f32[128,128]{0,1:T(8,128)}), f32[128,128]{0,1:T(8,128)}) %all-reduce.26.cloned.1.call-update) | async-done | bytes 65552 | tf_op jit(solution)/shard_map/psum | solution.py:31
  714.5 11.7 cholesky.85
  727.6 9.8 custom-call.9
  737.4 3.5 fusion.2
  743.6 36.0 %all-reduce.28.cloned.1.call-done = f32[2048,128]{0,1:T(8,128)} async-done(((f32[2048,128]{0,1:T(8,128)}), f32[2048,128]{0,1:T(8,128)}) %all-reduce.28.cloned.1.call-update) | async-done | bytes 1048592 | tf_op jit(solution)/shard_map/psum | solution.py:31
  779.6 34.4 %convolution_subtract_fusion.2 = f32[4096,2048]{0,1:T(8,128)} fusion(f32[4096,2048]{0,1:T(8,128)} %convolution_subtract_fusion.3, f32[4096,128]{0,1:T(8,128)} %copy-done.1, f32[2048,128]{0,1:T(8,128)} %all-reduce.28.cloned.1.call-done), kind=kOutput, calls=%fused_computation.5 | convolution fusion | flops 12893290496 | bytes 70254592 | tf_op jit(solution)/shard_map/dot_general | solution.py:169
  817.1 102.3 %all-reduce.30.cloned.1.call-done = f32[4096,128]{0,1:T(8,128)} async-done(((f32[4096,128]{0,1:T(8,128)}), f32[4096,128]{0,1:T(8,128)}) %all-reduce.30.cloned.1.call-update) | async-done | bytes 2097168 | tf_op jit(solution)/shard_map/psum | solution.py:31
  921.3 31.9 %all-reduce.32.cloned.1.call-done = f32[128,128]{0,1:T(8,128)} async-done(((f32[128,128]{0,1:T(8,128)}), f32[128,128]{0,1:T(8,128)}) %all-reduce.32.cloned.1.call-update) | async-done | bytes 65552 | tf_op jit(solution)/shard_map/psum | solution.py:31
  955.0 11.7 cholesky.96
  968.0 9.8 custom-call.10
  977.8 3.5 fusion.1
  984.2 35.7 %all-reduce.34.cloned.1.call-done = f32[2048,128]{0,1:T(8,128)} async-done(((f32[2048,128]{0,1:T(8,128)}), f32[2048,128]{0,1:T(8,128)}) %all-reduce.34.cloned.1.call-update) | async-done | bytes 1048592 | tf_op jit(solution)/shard_map/psum | solution.py:31
  1020.0 34.4 %convolution_subtract_fusion.1 = f32[4096,2048]{0,1:T(8,128)} fusion(f32[4096,2048]{0,1:T(8,128)} %convolution_subtract_fusion.2, f32[4096,128]{0,1:T(8,128)} %copy-done.2, f32[2048,128]{0,1:T(8,128)} %all-reduce.34.cloned.1.call-done), kind=kOutput, calls=%fused_computation.4 | convolution fusion | flops 12893290496 | bytes 70254592 | tf_op jit(solution)/shard_map/dot_general | solution.py:169
  1054.3 3.1 slice_select_fusion
  1057.5 102.2 %all-reduce.36.cloned.1.call-done = f32[4096,128]{0,1:T(8,128)} async-done(((f32[4096,128]{0,1:T(8,128)}), f32[4096,128]{0,1:T(8,128)}) %all-reduce.36.cloned.1.call-update) | async-done | bytes 2097168 | tf_op jit(solution)/shard_map/psum | solution.py:31
  1161.5 31.8 %all-reduce.38.cloned.1.call-done = f32[128,128]{0,1:T(8,128)} async-done(((f32[128,128]{0,1:T(8,128)}), f32[128,128]{0,1:T(8,128)}) %all-reduce.38.cloned.1.call-update) | async-done | bytes 65552 | tf_op jit(solution)/shard_map/psum | solution.py:31
  1195.1 11.7 cholesky.107
  1208.2 9.8 custom-call.11
  1218.0 3.5 fusion
  1228.3 31.8 %all-reduce.40.cloned.1.call-done = f32[2048,128]{0,1:T(8,128)} async-done(((f32[2048,128]{0,1:T(8,128)}), f32[2048,128]{0,1:T(8,128)}) %all-reduce.40.cloned.1.call-update) | async-done | bytes 1048592 | tf_op jit(solution)/shard_map/psum | solution.py:31
  1260.1 34.1 %convolution_subtract_fusion = f32[4096,2048]{0,1:T(8,128)} fusion(f32[4096,2048]{0,1:T(8,128)} %convolution_subtract_fusion.1, f32[4096,128]{0,1:T(8,128)S(1)} %copy-done.4, f32[2048,128]{0,1:T(8,128)} %all-reduce.40.cloned.1.call-done), kind=kOutput, calls=%fused_computation.3 | convolution fusion | flops 12893290496 | bytes 70254592 | tf_op jit(solution)/shard_map/dot_general | solution.py:169
  1294.2 33.3 %copy.102 = f32[4096,2048]{1,0:T(8,128)} copy(f32[4096,2048]{0,1:T(8,128)} %convolution_subtract_fusion) | data formatting | bytes 67108864
  (159 shorter events, 78.5 us)
Async XLA Ops:
  7.2 193.0 %all-gather.2.cloned.1.call-start = ((), (), s32[]{:S(2)}) async-start(), calls=%async_computation | async-start | bytes 5406720 | tf_op jit(solution)/shard_map/all_gather | solution.py:141
  8.8 13.0 collective-permute-start
  11.1 10.6 collective-permute-start.1
  13.4 20.1 %collective-permute-start.4 = (f32[32,1,8,128]{3,0,2,1:T(8,128)S(1)}, f32[32,1,8,128]{3,0,2,1:T(8,128)S(1)}, u32[]{:S(2)}, u32[]{:S(2)}) collective-permute-start(f32[32,1,8,128]{3,0,2,1:T(8,128)S(1)} %copy.116), channel_id=1, source_target_pairs={{0,8},{8,16},{16,24},{1,9},{9,17},{17,25},{2,10},{10,18},{18,26},{... | collective-permute-start | bytes 393224 | tf_op jit(solution)/shard_map/ppermute | solution.py:23
  18.7 15.6 %collective-permute-start.5 = (f32[32,1,8,128]{3,0,2,1:T(8,128)S(1)}, f32[32,1,8,128]{3,0,2,1:T(8,128)S(1)}, u32[]{:S(2)}, u32[]{:S(2)}) collective-permute-start(f32[32,1,8,128]{3,0,2,1:T(8,128)S(1)} %copy.117), channel_id=1, source_target_pairs={{8,0},{16,8},{24,16},{9,1},{17,9},{25,17},{10,2},{18,10},{26,18},{... | collective-permute-start | bytes 393224 | tf_op jit(solution)/shard_map/ppermute | solution.py:24
  20.7 12.9 copy-start.5
  22.8 5.6 collective-permute-start.2
  26.2 5.7 collective-permute-start.3
  34.4 12.4 collective-permute-start.6
  38.7 8.6 collective-permute-start.7
  49.5 4.1 copy-start.6
  50.6 3.0 collective-permute-start.8
  52.4 5.6 collective-permute-start.9
  58.0 6.2 collective-permute-start.10
  61.4 7.2 collective-permute-start.11
  105.1 51.5 %copy-start.8 = (s32[2,128]{1,0:T(2,128)S(1)}, s32[2,128]{1,0:T(2,128)}, u32[]{:S(2)}) copy-start(s32[2,128]{1,0:T(2,128)} %constant.242.clone.1) | copy-start | bytes 3076
  105.1 54.5 %copy-start.7 = (s32[256,128]{1,0:T(8,128)S(1)}, s32[256,128]{1,0:T(8,128)}, u32[]{:S(2)}) copy-start(s32[256,128]{1,0:T(8,128)} %constant.244.clone.1) | copy-start | bytes 393220
  112.1 328.3 %all-reduce.18.cloned.1.call-start = ((), (), s32[]{:S(2)}) async-start(), calls=%async_computation.1 | async-start | bytes 4194304 | tf_op jit(solution)/shard_map/psum | solution.py:31
  299.0 6.3 copy-start.9
  326.0 11.7 copy-start
  339.1 135.0 %all-reduce.20.cloned.1.call-start = ((), (), s32[]{:S(2)}) async-start(), calls=%async_computation.2 | async-start | bytes 131072 | tf_op jit(solution)/shard_map/psum | solution.py:31
  441.9 97.7 %all-reduce.22.cloned.1.call-start = ((), (), s32[]{:S(2)}) async-start(), calls=%async_computation.3 | async-start | bytes 2097152 | tf_op jit(solution)/shard_map/psum | solution.py:31
  503.4 175.8 %all-reduce.24.cloned.1.call-start = ((), (), s32[]{:S(2)}) async-start(), calls=%async_computation.4 | async-start | bytes 4194304 | tf_op jit(solution)/shard_map/psum | solution.py:31
  576.8 136.0 %all-reduce.26.cloned.1.call-start = ((), (), s32[]{:S(2)}) async-start(), calls=%async_computation.5 | async-start | bytes 131072 | tf_op jit(solution)/shard_map/psum | solution.py:31
  680.6 98.9 %all-reduce.28.cloned.1.call-start = ((), (), s32[]{:S(2)}) async-start(), calls=%async_computation.6 | async-start | bytes 2097152 | tf_op jit(solution)/shard_map/psum | solution.py:31
  740.9 1.4 copy-start.1
  743.3 176.1 %all-reduce.30.cloned.1.call-start = ((), (), s32[]{:S(2)}) async-start(), calls=%async_computation.7 | async-start | bytes 4194304 | tf_op jit(solution)/shard_map/psum | solution.py:31
  817.1 136.1 %all-reduce.32.cloned.1.call-start = ((), (), s32[]{:S(2)}) async-start(), calls=%async_computation.8 | async-start | bytes 131072 | tf_op jit(solution)/shard_map/psum | solution.py:31
  921.0 99.0 %all-reduce.34.cloned.1.call-start = ((), (), s32[]{:S(2)}) async-start(), calls=%async_computation.9 | async-start | bytes 2097152 | tf_op jit(solution)/shard_map/psum | solution.py:31
  981.3 1.3 copy-start.2
  983.7 176.0 %all-reduce.36.cloned.1.call-start = ((), (), s32[]{:S(2)}) async-start(), calls=%async_computation.10 | async-start | bytes 4194304 | tf_op jit(solution)/shard_map/psum | solution.py:31
  1057.5 135.8 %all-reduce.38.cloned.1.call-start = ((), (), s32[]{:S(2)}) async-start(), calls=%async_computation.11 | async-start | bytes 131072 | tf_op jit(solution)/shard_map/psum | solution.py:31
  1161.3 98.9 %all-reduce.40.cloned.1.call-start = ((), (), s32[]{:S(2)}) async-start(), calls=%async_computation.12 | async-start | bytes 2097152 | tf_op jit(solution)/shard_map/psum | solution.py:31
  1221.5 1.3 copy-start.3
  1226.9 33.2 %copy-start.4 = (f32[4096,128]{0,1:T(8,128)S(1)}, f32[4096,128]{0,1:T(8,128)}, u32[]{:S(2)}) copy-start(f32[4096,128]{0,1:T(8,128)} %copy-done.3) | copy-start | bytes 6291460
Sparse Core Ops, SparseCore 0:
  112.2 67.8 all-gather.1
  339.3 101.1 all-reduce.17
  443.3 30.7 all-reduce.19
  503.5 36.0 all-reduce.21
  576.9 102.2 all-reduce.23
  681.9 30.7 all-reduce.25
  743.4 36.0 all-reduce.27
  817.2 102.2 all-reduce.29
  922.3 30.7 all-reduce.31
  983.9 36.0 all-reduce.33
  1057.6 102.1 all-reduce.35
  1162.5 30.7 all-reduce.37
  1224.1 36.0 all-reduce.39
where the time goes:
time: 1340 us; the launch traced here: 1330 us
  waiting for transfers between devices  695 us (52%)
  local copies, waits for them, and re-layouts  200 us (15%)
  other arithmetic  178 us (13%)
  matrix products  171 us (13%)
  blocking collectives  43.4 us (3%)
  starting transfers between devices  30.6 us (2%)
  between operations  15.5 us (1%)
    psum x12, waiting for transfers between devices, spread(): return lax.psum(jnp.where(mine, value, jnp.zeros_like(value)), axis)  675 us
    dot_general x4, matrix products, per_device(): jnp.dot(factor_rows, factor_cols.T, preferred_element_type=jnp.float32, p...  137 us
    scatter x1, local copies, waits for them, and re-layouts, per_device(): full = blank.at[:, packed].set(everything, mode='drop')  84 us
    unnamed x30, local copies, waits for them, and re-layouts  51.2 us
    another operation x12, other arithmetic, per_device(): lower_block = jnp.linalg.cholesky(diag_part)  49.6 us
    unnamed x1, blocking collectives  43.4 us
    another operation x8, other arithmetic, per_device(): lax.linalg.triangular_solve(lower_block, rows_block, left_side=False, low...  41.9 us
    select_n x1, other arithmetic, per_device(): full = blank.at[:, packed].set(everything, mode='drop')  40.5 us
  transfers between devices with their start and end apart: 25, of which 18 were waited for; matrix products, arithmetic and copies ran while one was open for 4% of the time, Pallas kernels for 0%

commit v1 on v0

v1 whole, which is shorter than its diff:
```python
import jax
import jax.numpy as jnp
from jax import lax
from jax.experimental import pallas as pl
from jax.experimental.pallas import tpu as pltpu
from jax.sharding import PartitionSpec as P

NS = 16384
PANEL = 128
PANELS = 4
SWEEPS = 2
LOC = 8
HEAD = PANEL * PANELS
ROWS = 40
LANES = 128

diffuse_rate = 0.06

HIGH = lax.Precision.HIGHEST
F32 = jnp.float32
BF16 = jnp.bfloat16
VMEM_LIMIT = 56 * 1024 * 1024


def split(value):
    hi = value.astype(BF16)
    lo = (value - hi.astype(F32)).astype(BF16)
    return hi, lo


def forecast_kernel(
    place_ref, count_ref, mem, cour, turb, diss, xlo, xhi, ylo, yhi, own_lo, own_hi,
    c_ll, c_lh, c_hl, c_hh, cells, frac, obs, out, kc, state,
):
    members_n = mem.shape[0]
    slots = cells.shape[1]
    grp, tile = place_ref[0], place_ref[1]
    last_grp, last_tile = place_ref[2], place_ref[3]
    sub = lax.broadcasted_iota(jnp.int32, (8, LANES), 0)
    lane = lax.broadcasted_iota(jnp.int32, (8, LANES), 1)

    def after(v, row):
        return jnp.where(sub == 0, jnp.broadcast_to(row, (8, LANES)), pltpu.roll(v, 1, 0))

    def before(v, row):
        return jnp.where(sub == 7, jnp.broadcast_to(row, (8, LANES)), pltpu.roll(v, 7, 0))

    def zlow(v):
        return jnp.where(lane == 0, 0.0, pltpu.roll(v, 1, 1))

    def zhigh(v):
        return jnp.where(lane == LANES - 1, 0.0, pltpu.roll(v, LANES - 1, 1))

    def diffusion(x):
        t = turb[x]
        return diffuse_rate * t * t / diss[x]

    def xplane(f, x):
        if x < 0:
            return xlo[f, x + 2]
        if x > 7:
            return xhi[f, x - 8]
        if isinstance(f, int) and f >= members_n:
            return cour[f - members_n, x] if f < members_n + 3 else diffusion(x)
        return mem[f, x]

    def row(ref, f):
        return ref[pl.ds(f, 1), :]

    def xends(f, x):
        if x < 0:
            return row(c_ll, f), row(c_lh, f)
        if x > 7:
            return row(c_hl, f), row(c_hh, f)
        return ylo[f, 1, x : x + 1, :], yhi[f, 0, x : x + 1, :]

    def face(cp, ep, cq, eq):
        c = 0.5 * (cp + cq)
        e = 0.5 * (ep + eq)
        return jnp.maximum(c, 0.0) + e, jnp.minimum(c, 0.0) - e

    def coefs(index, keep, depth, tangent, planes, ends):
        e_prev, e_now, e_next = planes(members_n + 3)
        e_lo, e_hi = ends(members_n + 3)
        d_prev, d_now, d_next = planes(members_n + depth)
        t_now = planes(members_n + tangent)[1]
        t_lo, t_hi = ends(members_n + tangent)
        z_now = planes(members_n + 2)[1]
        pairs = [
            face(d_prev, e_prev, d_now, e_now),
            face(d_now, e_now, d_next, e_next),
            face(after(t_now, t_lo), after(e_now, e_lo), t_now, e_now),
            face(t_now, e_now, before(t_now, t_hi), before(e_now, e_hi)),
            face(zlow(z_now), zlow(e_now), z_now, e_now),
            face(z_now, e_now, zhigh(z_now), zhigh(e_now)),
        ]
        middle = jnp.ones((8, LANES), F32)
        for axis in range(3):
            (a_lo, b_lo), (a_hi, b_hi) = pairs[2 * axis], pairs[2 * axis + 1]
            middle = middle - (a_hi - b_lo)
            kc[index, 1 + 2 * axis] = keep * a_lo
            kc[index, 2 + 2 * axis] = -(keep * b_hi)
        kc[index, 0] = keep * middle

    def kept(flag):
        return jnp.where(flag, 1.0, 0.0).astype(F32)

    for x in range(-1, 9):
        keep = 1.0
        if x < 0:
            keep = kept(grp > 0)
        if x > 7:
            keep = kept(grp < last_grp)
        coefs(
            x + 1, keep, 0, 1,
            lambda f, x=x: tuple(xplane(f, x + s) for s in (-1, 0, 1)),
            lambda f, x=x: xends(f, x),
        )

    def yplanes_lo(f):
        return ylo[f, 0], ylo[f, 1], own_lo[f, 0]

    def yplanes_hi(f):
        return own_hi[f, 1], yhi[f, 0], yhi[f, 1]

    def yends_lo(f):
        return row(c_ll, f), row(c_hl, f)

    def yends_hi(f):
        return row(c_lh, f), row(c_hh, f)

    coefs(10, kept(tile > 0), 1, 0, yplanes_lo, yends_lo)
    coefs(11, kept(tile < last_tile), 1, 0, yplanes_hi, yends_hi)

    def update(index, v_prev, v, v_next, r_lo, r_hi):
        return (
            kc[index, 0] * v
            + kc[index, 1] * v_prev
            + kc[index, 2] * v_next
            + kc[index, 3] * after(v, r_lo)
            + kc[index, 4] * before(v, r_hi)
            + kc[index, 5] * zlow(v)
            + kc[index, 6] * zhigh(v)
        )

    def one_member(m, total):
        planes = [xplane(m, x) for x in range(-2, 10)]
        new = [
            update(x + 1, planes[x + 1], planes[x + 2], planes[x + 3], *xends(m, x))
            for x in range(-1, 9)
        ]
        new_lo = update(10, *yplanes_lo(m), *yends_lo(m))
        new_hi = update(11, *yplanes_hi(m), *yends_hi(m))
        sums = []
        for x in range(8):
            v = update(
                x + 1, new[x], new[x + 1], new[x + 2], new_lo[x : x + 1, :], new_hi[x : x + 1, :]
            )
            state[m, x * 8 : (x + 1) * 8, :] = v
            sums.append(total[x] + v)
        return tuple(sums)

    zero = jnp.zeros((8, LANES), F32)
    total = lax.fori_loop(0, members_n, one_member, (zero,) * 8)
    mean = jnp.concatenate(total, 0) * (1.0 / members_n)

    base = cells[0:1, :]
    z0 = lax.rem(base, LANES)
    xy0 = lax.div(base, LANES)
    y0 = lax.rem(xy0, 8)
    x0 = lax.div(xy0, 8)
    fx, fy, fz = frac[0:1, :], frac[1:2, :], frac[2:3, :]

    def hat(size, at, f):
        iota = lax.broadcasted_iota(jnp.int32, (size, slots), 0)
        return jnp.where(iota == at, 1.0 - f, jnp.where(iota == at + 1, f, 0.0))

    wz_hi, wz_lo = split(hat(LANES, z0, fz))
    wz = jnp.concatenate([wz_hi, wz_hi, wz_lo], 0)
    wx = hat(8, x0, fx)
    wy = hat(8, y0, fy)
    wxy = jnp.concatenate([wx[x : x + 1, :] * wy for x in range(8)], 0)

    group = 8

    def some_members(step, carry):
        field = state[pl.ds(step * group, group)] - mean[None]
        hi, lo = split(field.reshape(group * 64, LANES))
        along = jnp.dot(
            jnp.concatenate([hi, lo, hi], 1), wz, preferred_element_type=F32
        ).reshape(group, 64, slots)
        picked = jnp.sum(along * wxy[None], axis=1)
        out[pl.ds(pl.multiple_of(step * group, group), group), :] = picked.astype(BF16).astype(F32)
        return carry

    lax.fori_loop(0, members_n // group, some_members, 0)
    tail = jnp.concatenate(
        [
            (grp * 8 + x0).astype(F32) + fx,
            (tile * 8 + y0).astype(F32) + fy,
            z0.astype(F32) + fz,
            jnp.full((1, slots), count_ref[0], jnp.int32).astype(F32),
            obs[...],
            jnp.zeros((3, slots), F32),
        ],
        0,
    )
    out[members_n : members_n + 8, :] = tail


def taper_cov(left, right, members_n):
    cov = jnp.dot(
        left[:, :members_n].astype(BF16), right[:members_n].astype(BF16), preferred_element_type=F32
    )
    dist = None
    for d in range(3):
        at = members_n + d
        gap = left[:, at : at + 1] - right[at : at + 1, :]
        dist = gap * gap if dist is None else dist + gap * gap
    scale = 1.0 / (members_n - 1.0)
    return cov * (scale / (1.0 + dist * (1.0 / (LOC * LOC))))


def eliminate(a):
    groups = len(a)
    sub = lax.broadcasted_iota(jnp.int32, (8, LANES), 0)
    lane = lax.broadcasted_iota(jnp.int32, (8, LANES), 1)
    m = [jnp.where(lane == sub + 8 * g, 1.0, 0.0).astype(F32) for g in range(groups)]
    done = []

    def down(v, j):
        return jnp.broadcast_to(v[j : j + 1, :], (8, LANES))

    def across(v, k):
        return jnp.broadcast_to(v[:, k : k + 1], (8, LANES))

    for gk in range(groups):
        k0 = 8 * gk
        col = [across(a[gk], k0 + j) for j in range(8)]
        ra, rm = a[gk], m[gk]
        rows_a, rows_m, inv, u = [], [], [], []
        diag = jnp.ones((8, LANES), F32)
        for j in range(8):
            pivot = down(col[j], j)
            r = 1.0 / pivot
            diag = jnp.where(sub == j, pivot, diag)
            row_a, row_m = down(ra, j), down(rm, j)
            uj = [down(col[i], j) if i > j else None for i in range(8)]
            f = jnp.where(sub > j, col[j] * r, 0.0)
            for i in range(j + 1, 8):
                col[i] = col[i] - f * uj[i]
            ra = ra - f * row_a
            rm = rm - f * row_m
            rows_a.append(row_a)
            rows_m.append(row_m)
            inv.append(r)
            u.append(uj)
        done.append(rm * lax.rsqrt(diag))
        for g in range(gk + 1, groups):
            c = [across(a[g], k0 + j) for j in range(8)]
            ag, mg = a[g], m[g]
            for j in range(8):
                f = c[j] * inv[j]
                for i in range(j + 1, 8):
                    c[i] = c[i] - f * u[j][i]
                ag = ag - f * rows_a[j]
                mg = mg - f * rows_m[j]
            a[g], m[g] = ag, mg
    return jnp.concatenate(done, 0)


def head_kernel(
    offset_ref, place_ref, everything, obs_head, rows_out, cols_out, head_out, linv_out, fcols_out,
    full, work,
):
    blocks, _, slots = everything.shape
    row_chunks = rows_out.shape[0] // LANES
    col_chunks = cols_out.shape[1] // LANES
    members_n = ROWS - 8
    grp, tile = place_ref[0], place_ref[1]
    lane = lax.broadcasted_iota(jnp.int32, (ROWS, LANES), 1)
    parts = slots // LANES

    def pack(b, carry):
        at = offset_ref[b]
        chunk = lax.div(at, LANES)
        shift = lax.rem(at, LANES)
        early = lane < shift
        last = full[chunk]
        for j in range(parts):
            now = pltpu.roll(everything[b, :, j * LANES : (j + 1) * LANES], shift, 1)
            full[chunk + j] = jnp.where(early, last, now)
            last = now
        full[chunk + parts] = last
        return carry

    lax.fori_loop(0, blocks, pack, 0)

    def turn(c, carry):
        piece = jnp.concatenate([full[grp * row_chunks + c], jnp.zeros((LANES - ROWS, LANES), F32)], 0)
        rows_out[pl.ds(pl.multiple_of(c * LANES, LANES), LANES), :] = piece.T
        return carry

    lax.fori_loop(0, row_chunks, turn, 0)
    for c in range(col_chunks):
        cols_out[:, c * LANES : (c + 1) * LANES] = full[tile * col_chunks + c]
    for c in range(PANELS):
        head_out[:, c * LANES : (c + 1) * LANES] = full[c]

    head = head_out[...]
    down = []
    for c in range(PANELS):
        piece = jnp.concatenate([full[c], jnp.zeros((LANES - ROWS, LANES), F32)], 0)
        down.append(piece.T)
    down = jnp.concatenate(down, 0)
    rid = lax.broadcasted_iota(jnp.int32, (HEAD, HEAD), 0)
    cid = lax.broadcasted_iota(jnp.int32, (HEAD, HEAD), 1)
    same = rid == cid
    work[:HEAD, :HEAD] = taper_cov(down, head, members_n) + jnp.where(same, obs_head[...], 0.0)
    work[:HEAD, HEAD:] = jnp.where(same, 1.0, 0.0).astype(F32)

    def panel(p, carry):
        at = pl.multiple_of(p * PANEL, PANEL)
        for q in range(PANELS):
            @pl.when(p == q)
            def _(q=q):
                for g in range(16):
                    work[HEAD + 8 * g : HEAD + 8 * g + 8, :PANEL] = work[
                        q * PANEL + 8 * g : q * PANEL + 8 * g + 8, q * PANEL : (q + 1) * PANEL
                    ]
        inverse = eliminate([work[HEAD + 8 * g : HEAD + 8 * g + 8, :PANEL] for g in range(16)])
        done = jnp.dot(inverse, work[pl.ds(at, PANEL), :], precision=HIGH, preferred_element_type=F32)
        work[pl.ds(at, PANEL), :] = done
        for q in range(PANELS - 1):
            @pl.when(p == q)
            def _(q=q):
                rest = (q + 1) * PANEL
                upper = done[:, rest:HEAD]
                work[rest:HEAD, :] = work[rest:HEAD, :] - lax.dot_general(
                    upper, done, (((0,), (0,)), ((), ())), precision=HIGH, preferred_element_type=F32
                )
        return carry

    lax.fori_loop(0, PANELS, panel, 0)
    linv = work[:HEAD, HEAD:]
    hi, lo = split(linv)
    linv_out[:, :HEAD] = hi
    linv_out[:, HEAD : 2 * HEAD] = hi
    linv_out[:, 2 * HEAD :] = lo
    left = jnp.concatenate([hi, lo, hi], 1)
    width = 256
    pr = lax.broadcasted_iota(jnp.int32, (HEAD, width), 0)
    pc = lax.broadcasted_iota(jnp.int32, (HEAD, width), 1)

    def some_cols(c, carry):
        at = pl.multiple_of(c * width, width)
        first = tile * col_chunks * LANES + c * width
        right = cols_out[:, pl.ds(at, width)]
        ids = pc + first
        cross = taper_cov(down, right, members_n)
        cross = cross + jnp.where(pr == ids, carry, 0.0)
        hi, lo = split(cross)
        f = jnp.dot(left, jnp.concatenate([hi, hi, lo], 0), preferred_element_type=F32)
        f = jnp.where(ids >= lax.div(pr, PANEL) * PANEL, f, 0.0)
        hi, lo = split(f)
        fcols_out[:HEAD, pl.ds(at, width)] = hi
        fcols_out[HEAD : 2 * HEAD, pl.ds(at, width)] = lo
        fcols_out[2 * HEAD :, pl.ds(at, width)] = hi
        return carry

    noise_down = jnp.sum(jnp.where(same, obs_head[...], 0.0), axis=1, keepdims=True)
    lax.fori_loop(0, cols_out.shape[1] // width, some_cols, jnp.broadcast_to(noise_down, (HEAD, width)))


def final_kernel(place_ref, rows, cols, head, linv, fcols, obs_head, obs, trailing, factor, keep):
    members_n = ROWS - 8
    step = pl.program_id(0)
    grp, tile = place_ref[0], place_ref[1]
    height = rows.shape[0]
    steps = pl.num_programs(0)
    col_span = cols.shape[1]
    first_row = (grp * steps + step) * height
    first_col = tile * col_span
    left = rows[...]
    rid = lax.broadcasted_iota(jnp.int32, (height, HEAD), 0) + first_row
    cid = lax.broadcasted_iota(jnp.int32, (height, HEAD), 1)
    cross = taper_cov(left, head[...], members_n) + jnp.where(rid == cid, obs_head[...], 0.0)
    hi, lo = split(cross)
    f = lax.dot_general(
        jnp.concatenate([hi, lo, hi], 1), linv[...], (((1,), (1,)), ((), ())), preferred_element_type=F32
    )
    f = jnp.where(rid >= lax.div(cid, PANEL) * PANEL, f, 0.0)
    keep[pl.ds(pl.multiple_of(step * height, height), height), :] = f
    hi, lo = split(f)
    f3 = jnp.concatenate([hi, hi, lo], 1)
    width = min(512, col_span)
    for c in range(0, col_span, width):
        part = cols[:, c : c + width]
        value = taper_cov(left, part, members_n)
        trailing[:, c : c + width] = value - jnp.dot(
            f3, fcols[:, c : c + width], preferred_element_type=F32
        )

    @pl.when((first_row < first_col + col_span) & (first_col < first_row + height))
    def _():
        for c in range(0, col_span, width):
            rid = lax.broadcasted_iota(jnp.int32, (height, width), 0) + first_row
            cid = lax.broadcasted_iota(jnp.int32, (height, width), 1) + (first_col + c)
            trailing[:, c : c + width] = trailing[:, c : c + width] + jnp.where(
                rid == cid, obs[:, c : c + width], 0.0
            )

    @pl.when(step == steps - 1)
    def _():
        share = factor.shape[0]
        factor[...] = keep[pl.ds(pl.multiple_of(tile * share, share), share), :]


def spec(space=pltpu.VMEM):
    return pl.BlockSpec(memory_space=space)


def per_device(
    members, courant, turb_energy, dissipation, sensor_cells, sensor_frac, sensor_count, obs_var
):
    grp_size = lax.axis_size("grp")
    tile_size = lax.axis_size("tile")
    grp = lax.axis_index("grp")
    tile = lax.axis_index("tile")
    members_n = members.shape[0]
    slots = sensor_cells.shape[1]
    blocks = grp_size * tile_size
    place = jnp.stack([grp, tile, jnp.int32(grp_size - 1), jnp.int32(tile_size - 1)]).astype(jnp.int32)

    diffusion = diffuse_rate * turb_energy * turb_energy / dissipation

    def cut(xs, ys):
        return jnp.concatenate([members[:, xs, ys], courant[:, xs, ys], diffusion[None, xs, ys]], 0)

    every = slice(None)
    x_first, x_last = cut(slice(0, 2), every), cut(slice(6, 8), every)
    y_first = jnp.swapaxes(cut(every, slice(0, 2)), 1, 2)
    y_last = jnp.swapaxes(cut(every, slice(6, 8)), 1, 2)

    def move(value, dg, dt):
        pairs = []
        for g in range(grp_size):
            for t in range(tile_size):
                if 0 <= g + dg < grp_size and 0 <= t + dt < tile_size:
                    pairs.append((g * tile_size + t, (g + dg) * tile_size + t + dt))
        return lax.ppermute(value, ("grp", "tile"), pairs)

    xlo, xhi = move(x_last, 1, 0), move(x_first, -1, 0)
    ylo, yhi = move(y_last, 0, 1), move(y_first, 0, -1)
    c_ll, c_lh = move(cut(7, 7), 1, 1), move(cut(7, 0), 1, -1)
    c_hl, c_hh = move(cut(0, 7), -1, 1), move(cut(0, 0), -1, -1)

    obs_at = jnp.minimum(grp * slots, obs_var.shape[0] - slots)
    obs_part = lax.dynamic_slice_in_dim(obs_var, obs_at, slots, 0)[None]

    message = pl.pallas_call(
        forecast_kernel,
        out_shape=jax.ShapeDtypeStruct((ROWS, slots), F32),
        in_specs=[spec(pltpu.SMEM)] * 2 + [spec()] * 17,
        out_specs=spec(),
        scratch_shapes=[pltpu.VMEM((12, 7, 8, LANES), F32), pltpu.VMEM((members_n, 64, LANES), F32)],
        compiler_params=pltpu.CompilerParams(vmem_limit_bytes=VMEM_LIMIT),
        name="forecast",
    )(
        place, sensor_count, members, courant, turb_energy, dissipation, xlo, xhi, ylo, yhi,
        y_first, y_last, c_ll, c_lh, c_hl, c_hh, sensor_cells, sensor_frac, obs_part,
    )

    everything = lax.all_gather(message, ("grp", "tile"), axis=0)
    counts = everything[:, members_n + 3, 0].astype(jnp.int32)
    offsets = jnp.cumsum(counts) - counts
    holders = -(-HEAD // slots)
    obs_head = everything[: holders * tile_size : tile_size, members_n + 4].reshape(1, -1)[:, :HEAD]

    row_span = NS // grp_size
    col_span = NS // tile_size
    rows, cols, head, linv, fcols = pl.pallas_call(
        head_kernel,
        out_shape=[
            jax.ShapeDtypeStruct((row_span, LANES), F32),
            jax.ShapeDtypeStruct((ROWS, col_span), F32),
            jax.ShapeDtypeStruct((ROWS, HEAD), F32),
            jax.ShapeDtypeStruct((HEAD, 3 * HEAD), BF16),
            jax.ShapeDtypeStruct((3 * HEAD, col_span), BF16),
        ],
        in_specs=[spec(pltpu.SMEM)] * 2 + [spec()] * 2,
        out_specs=[spec()] * 5,
        scratch_shapes=[
            pltpu.VMEM((NS // LANES + slots // LANES + 1, ROWS, LANES), F32),
            pltpu.VMEM((HEAD + PANEL, 2 * HEAD), F32),
        ],
        compiler_params=pltpu.CompilerParams(vmem_limit_bytes=VMEM_LIMIT),
        name="head",
    )(offsets, place, everything, obs_head)

    height = 256
    share = row_span // tile_size
    whole = lambda shape: pl.BlockSpec(shape, lambda i: (0, 0))
    trailing, factor = pl.pallas_call(
        final_kernel,
        grid=(row_span // height,),
        out_shape=[
            jax.ShapeDtypeStruct((row_span, col_span), F32),
            jax.ShapeDtypeStruct((share, HEAD), F32),
        ],
        in_specs=[
            spec(pltpu.SMEM),
            pl.BlockSpec((height, LANES), lambda i: (i, 0)),
            whole((ROWS, col_span)),
            whole((ROWS, HEAD)),
            whole((HEAD, 3 * HEAD)),
            whole((3 * HEAD, col_span)),
            whole((1, HEAD)),
            whole((1, col_span)),
        ],
        out_specs=[pl.BlockSpec((height, col_span), lambda i: (i, 0)), whole((share, HEAD))],
        scratch_shapes=[pltpu.VMEM((row_span, HEAD), F32)],
        compiler_params=pltpu.CompilerParams(vmem_limit_bytes=VMEM_LIMIT),
        name="final",
    )(place, rows, cols, head, linv, fcols, obs_head, obs_var[None])
    return trailing, factor


def solution(mesh):
    return jax.shard_map(
        per_device,
        mesh=mesh,
        in_specs=(
            P(None, "grp", "tile", None),
            P(None, "grp", "tile", None),
            P("grp", "tile", None),
            P("grp", "tile", None),
            P(None, ("grp", "tile")),
            P(None, ("grp", "tile")),
            P(("grp", "tile")),
            P("tile"),
        ),
        out_specs=(P("grp", "tile"), P(("grp", "tile"), None)),
        check_vma=False,
    )
```

time: 1340 us -> 239 us (0.18)
  waiting for transfers between devices: 695 us -> 81 us
  local copies, waits for them, and re-layouts: 200 us -> 9.53 us
  other arithmetic: 178 us -> 4.66 us
  matrix products: 171 us -> 0 us
  Pallas kernels: 0 us -> 109 us
  blocking collectives: 43.4 us -> 0 us
    psum x12 -> x0, waiting for transfers between devices: 675 us -> none  [spread(): return lax.psum(jnp.where(mine, value, jnp.zeros_like(value)), axis)]
    dot_general x5 -> x0, matrix products: 157 us -> none  [the longest x4 137 us: per_device(): jnp.dot(factor_rows, factor_cols.T, preferred_element_type=jnp.float32, p...]
    pallas_call x0 -> x3, Pallas kernels: none -> 109 us  [the longest x1 54.7 us: per_device(): pl.pallas_call(final_kernel, grid=(row_span // height,), out_shape=[jax.S...]
    another operation x24 -> x3, other arithmetic: 91.7 us -> 0.73 us  [the longest x1 0.56 us: per_device(): jnp.stack([grp, tile, jnp.int32(grp_size - 1), jnp.int32(tile_size - 1)])]
    scatter x1 -> x0, local copies, waits for them, and re-layouts: 84 us -> none  [per_device(): full = blank.at[:, packed].set(everything, mode='drop')]
    all_gather x1, waiting for transfers between devices: 0.02 us -> 71.6 us  [per_device(): everything = lax.all_gather(message, ('grp', 'tile'), axis=0)]
    select_n x13 -> x0, other arithmetic: 61.4 us -> none  [the longest x1 40.5 us: per_device(): full = blank.at[:, packed].set(everything, mode='drop')]
    unnamed x30, local copies, waits for them, and re-layouts: 51.2 us -> 1 us
  transfers between devices with their start and end apart: 25 -> 9, of which waited for: 18 -> 2; matrix products, arithmetic and copies ran while one was open for 4% -> 3% of each run, Pallas kernels for 0% -> 0%
where the time goes in v1:
time: 239 us; the launch traced here: 238 us
  Pallas kernels  109 us (46%)
  waiting for transfers between devices  81 us (34%)
  starting transfers between devices  18.7 us (8%)
  between operations  15.1 us (6%)
  local copies, waits for them, and re-layouts  9.53 us (4%)
  other arithmetic  4.66 us (2%)
    all_gather x1, waiting for transfers between devices, per_device(): everything = lax.all_gather(message, ('grp', 'tile'), axis=0)  71.6 us
    pallas_call x1, Pallas kernels, per_device(): pl.pallas_call(final_kernel, grid=(row_span // height,), out_shape=[jax.S...  54.7 us
    pallas_call x1, Pallas kernels, per_device(): pl.pallas_call(head_kernel, out_shape=[jax.ShapeDtypeStruct((row_span, LA...  42.9 us
    ppermute x8, starting transfers between devices, move(): return lax.ppermute(value, ('grp', 'tile'), pairs)  18.6 us
    pallas_call x1, Pallas kernels, per_device(): pl.pallas_call(forecast_kernel, out_shape=jax.ShapeDtypeStruct((ROWS, slo...  11.3 us
    ppermute x8, waiting for transfers between devices, move(): return lax.ppermute(value, ('grp', 'tile'), pairs)  9.35 us
  transfers between devices with their start and end apart: 9, of which 2 were waited for; matrix products, arithmetic and copies ran while one was open for 3% of the time, Pallas kernels for 0%

profile of v1, /device:TPU:0, one launch (start us, length us, event | category | flops | bytes accessed | tf_op | source)
XLA Modules:
  0.0 237.8 jit_solution(15816320779999012281)
XLA Ops:
  7.2 0.0 copy-start.10
  7.2 0.0 all-gather.3.cloned.1.call-start
  7.2 0.8 fusion.5
  8.0 0.8 fusion
  8.8 1.2 fusion.2
  10.0 0.7 collective-permute-start.6
  10.7 7.4 %collective-permute-start.4 = (f32[36,128]{1,0:T(8,128)S(1)}, f32[36,128]{1,0:T(8,128)S(1)}, u32[]{:S(2)}, u32[]{:S(2)}) collective-permute-start(f32[36,128]{1,0:T(8,128)S(1)} %pad_maximum_fusion.2), channel_id=1, source_target_pairs={{0,9},{1,10},{2,11},{3,12},{4,13},{5,14},{6,15},{8,17},{9,18},{10,... | collective-permute-start | bytes 55304 | tf_op jit(solution)/shard_map/ppermute | solution.py:451
  18.1 0.8 fusion.7
  18.8 1.1 fusion.4
  20.0 2.7 %collective-permute-start = (f32[36,2,8,128]{3,2,1,0:T(8,128)S(1)}, f32[36,2,8,128]{3,2,1,0:T(8,128)S(1)}, u32[]{:S(2)}, u32[]{:S(2)}) collective-permute-start(f32[36,2,8,128]{3,2,1,0:T(8,128)S(1)} %pad_maximum_fusion), channel_id=1, source_target_pairs={{0,8},{1,9},{2,10},{3,11},{4,12},{5,13},{6,14},{7,15},{8,16},{9,17... | collective-permute-start | bytes 884744 | tf_op jit(solution)/shard_map/ppermute | solution.py:451
  22.7 1.3 collective-permute-start.1
  24.0 1.0 fusion.6
  25.0 1.8 fusion.3
  26.8 3.4 %collective-permute-start.2 = (f32[36,2,8,128]{3,2,1,0:T(8,128)S(1)}, f32[36,2,8,128]{3,2,1,0:T(8,128)S(1)}, u32[]{:S(2)}, u32[]{:S(2)}) collective-permute-start(f32[36,2,8,128]{3,2,1,0:T(8,128)S(1)} %maximum_bitcast_fusion.own_hi), channel_id=1, source_target_pairs={{0,1},{1,2},{2,3},{3,4},{4,5},{5,6},{6,7},{8,9},{9,10},{10,11},{11... | collective-permute-start | bytes 884744 | tf_op jit(solution)/shard_map/ppermute | solution.py:451
  30.3 0.0 copy-start.1
  30.3 0.0 collective-permute-done.6.c_hl
  30.4 1.3 collective-permute-start.3
  31.7 0.0 collective-permute-done.4.c_ll
  31.7 1.3 collective-permute-start.7
  33.0 9.3 %collective-permute-done.7.c_hh = f32[36,128]{1,0:T(8,128)S(1)} collective-permute-done((f32[36,128]{1,0:T(8,128)S(1)}, f32[36,128]{1,0:T(8,128)S(1)}, u32[]{:S(2)}, u32[]{:S(2)}) %collective-permute-start.7) | collective-permute-done | bytes 18464 | tf_op jit(solution)/shard_map/ppermute | solution.py:451
  42.4 0.7 collective-permute-start.5
  43.0 0.6 pad_add_fusion.place_ref
  44.2 0.7 dynamic_slice.3
  44.9 0.0 collective-permute-done.5.c_lh
  44.9 0.0 collective-permute-done.xlo
  44.9 0.0 copy-start.2
  44.9 0.0 collective-permute-done.1.xhi
  44.9 0.0 copy-start.3
  45.0 0.0 collective-permute-done.2.ylo
  45.0 0.0 copy-start.4
  45.0 0.0 collective-permute-done.3.yhi
  45.0 0.5 copy-done.9
  45.5 0.1 copy-done.2
  45.6 0.1 copy-done.3
  45.7 0.1 copy-done.4
  45.8 0.1 copy-done.5
  45.9 11.3 %forecast.1 = f32[40,1024]{1,0:T(8,128)} custom-call(s32[4]{0:T(128)} %pad_add_fusion.place_ref, s32[1]{0:T(128)S(6)} %copy.68.count_ref, f32[32,8,8,128]{3,2,1,0:T(8,128)} %mem.1, f32[3,8,8,128]{3,2,1,0:T(8,128)} %cour.1, f32[8,8,128]{2,1,0:T(8,128)} %turb.1, f32[8,8,128]{2,1,0:T(8,128)} %diss.1, f32[36,2,8,128]{3,2,1,0:T(8,128)} %copy-done.2, ...), custom_call_target="tpu_custom_call" | custom-call | tf_op jit(solution)/shard_map/forecast/pallas_call | solution.py:461
  57.3 0.0 all-gather.3.cloned.1.call-update
  57.3 71.6 %all-gather.3.cloned.1.call-done = f32[1280,1024]{1,0:T(8,128)} async-done(((f32[40,1024]{1,0:T(8,128)}), f32[1280,1024]{1,0:T(8,128)}) %all-gather.3.cloned.1.call-update) | async-done | bytes 5242896 | tf_op jit(solution)/shard_map/all_gather | solution.py:474
  129.0 1.6 fusion.1
  130.5 0.8 slice_bitcast_fusion.4
  131.3 0.9 slice_convert_fusion
  132.2 0.5 slice.119.obs_head
  132.7 0.1 reduce-window.9
  132.8 0.1 reduce
  132.9 0.5 sub.3.offset_ref
  133.4 42.9 %head.1 = (f32[4096,128]{1,0:T(8,128)}, f32[40,2048]{1,0:T(8,128)}, f32[40,512]{1,0:T(8,128)}, bf16[512,1536]{1,0:T(8,128)(2,1)}, bf16[1536,2048]{1,0:T(8,128)(2,1)}) custom-call(s32[32]{0:T(128)} %sub.3.offset_ref, s32[4]{0:T(128)} %pad_add_fusion.place_ref, f32[32,40,1024]{2,1,0:T(8,128)} %bitcast.55, f32[1,512]{1,0:T(1,128)} %slice.119.obs_head), custom_call_target="tpu_custom_call" | custom-call | tf_op jit(solution)/shard_map/head/pallas_call | solution.py:482
  176.3 54.7 %final.1 = (f32[4096,2048]{1,0:T(8,128)}, f32[512,512]{1,0:T(8,128)}) custom-call(s32[4]{0:T(128)} %pad_add_fusion.place_ref, f32[4096,128]{1,0:T(8,128)} %get-tuple-element.7.rows, f32[40,2048]{1,0:T(8,128)} %get-tuple-element.8.cols, f32[40,512]{1,0:T(8,128)} %get-tuple-element.9.head, bf16[512,1536]{1,0:T(8,128)(2,1)} %get-tuple-element.10.linv, ...), custom_call_target="tpu_custom_call" | custom-call | tf_op jit(solution)/shard_map/final/pallas_call | solution.py:504
  (33 shorter events, 0.2 us)
Async XLA Ops:
  7.2 37.1 %copy-start.10 = (f32[2048]{0:T(1024)S(1)}, f32[2048]{0:T(1024)}, u32[]{:S(2)}) copy-start(f32[2048]{0:T(1024)} %param.15) | copy-start | bytes 24580
  7.2 121.8 %all-gather.3.cloned.1.call-start = ((), (), s32[]{:S(2)}) async-start(), calls=%async_computation | async-start | bytes 5406720 | tf_op jit(solution)/shard_map/all_gather | solution.py:474
  10.0 20.3 %collective-permute-start.6 = (f32[36,128]{1,0:T(8,128)S(1)}, f32[36,128]{1,0:T(8,128)S(1)}, u32[]{:S(2)}, u32[]{:S(2)}) collective-permute-start(f32[36,128]{1,0:T(8,128)S(1)} %pad_maximum_fusion.4), channel_id=1, source_target_pairs={{8,1},{9,2},{10,3},{11,4},{12,5},{13,6},{14,7},{16,9},{17,10},{18,... | collective-permute-start | bytes 55304 | tf_op jit(solution)/shard_map/ppermute | solution.py:451
  10.7 21.0 %collective-permute-start.4 = (f32[36,128]{1,0:T(8,128)S(1)}, f32[36,128]{1,0:T(8,128)S(1)}, u32[]{:S(2)}, u32[]{:S(2)}) collective-permute-start(f32[36,128]{1,0:T(8,128)S(1)} %pad_maximum_fusion.2), channel_id=1, source_target_pairs={{0,9},{1,10},{2,11},{3,12},{4,13},{5,14},{6,15},{8,17},{9,18},{10,... | collective-permute-start | bytes 55304 | tf_op jit(solution)/shard_map/ppermute | solution.py:451
  20.0 25.0 %collective-permute-start = (f32[36,2,8,128]{3,2,1,0:T(8,128)S(1)}, f32[36,2,8,128]{3,2,1,0:T(8,128)S(1)}, u32[]{:S(2)}, u32[]{:S(2)}) collective-permute-start(f32[36,2,8,128]{3,2,1,0:T(8,128)S(1)} %pad_maximum_fusion), channel_id=1, source_target_pairs={{0,8},{1,9},{2,10},{3,11},{4,12},{5,13},{6,14},{7,15},{8,16},{9,17... | collective-permute-start | bytes 884744 | tf_op jit(solution)/shard_map/ppermute | solution.py:451
  22.7 22.3 %collective-permute-start.1 = (f32[36,2,8,128]{3,2,1,0:T(8,128)S(1)}, f32[36,2,8,128]{3,2,1,0:T(8,128)S(1)}, u32[]{:S(2)}, u32[]{:S(2)}) collective-permute-start(f32[36,2,8,128]{3,2,1,0:T(8,128)S(1)} %pad_maximum_fusion.1), channel_id=1, source_target_pairs={{8,0},{9,1},{10,2},{11,3},{12,4},{13,5},{14,6},{15,7},{16,8},{17,9... | collective-permute-start | bytes 884744 | tf_op jit(solution)/shard_map/ppermute | solution.py:451
  26.8 18.2 %copy-start = (f32[36,2,8,128]{3,2,1,0:T(8,128)}, f32[36,2,8,128]{3,2,1,0:T(8,128)S(1)}, u32[]{:S(2)}) copy-start(f32[36,2,8,128]{3,2,1,0:T(8,128)S(1)} %maximum_bitcast_fusion.own_hi) | copy-start | bytes 884740
  26.8 18.1 %collective-permute-start.2 = (f32[36,2,8,128]{3,2,1,0:T(8,128)S(1)}, f32[36,2,8,128]{3,2,1,0:T(8,128)S(1)}, u32[]{:S(2)}, u32[]{:S(2)}) collective-permute-start(f32[36,2,8,128]{3,2,1,0:T(8,128)S(1)} %maximum_bitcast_fusion.own_hi), channel_id=1, source_target_pairs={{0,1},{1,2},{2,3},{3,4},{4,5},{5,6},{6,7},{8,9},{9,10},{10,11},{11... | collective-permute-start | bytes 884744 | tf_op jit(solution)/shard_map/ppermute | solution.py:451
  30.3 14.7 %copy-start.1 = (f32[36,2,8,128]{3,2,1,0:T(8,128)}, f32[36,2,8,128]{3,2,1,0:T(8,128)S(1)}, u32[]{:S(2)}) copy-start(f32[36,2,8,128]{3,2,1,0:T(8,128)S(1)} %maximum_bitcast_fusion.1.own_lo) | copy-start | bytes 884740
  30.3 14.7 %copy-start.6 = (f32[36,128]{1,0:T(8,128)}, f32[36,128]{1,0:T(8,128)S(1)}, u32[]{:S(2)}) copy-start(f32[36,128]{1,0:T(8,128)S(1)} %collective-permute-done.6.c_hl) | copy-start | bytes 55300
  30.4 14.6 %collective-permute-start.3 = (f32[36,2,8,128]{3,2,1,0:T(8,128)S(1)}, f32[36,2,8,128]{3,2,1,0:T(8,128)S(1)}, u32[]{:S(2)}, u32[]{:S(2)}) collective-permute-start(f32[36,2,8,128]{3,2,1,0:T(8,128)S(1)} %maximum_bitcast_fusion.1.own_lo), channel_id=1, source_target_pairs={{1,0},{2,1},{3,2},{4,3},{5,4},{6,5},{7,6},{9,8},{10,9},{11,10},{12... | collective-permute-start | bytes 884744 | tf_op jit(solution)/shard_map/ppermute | solution.py:451
  31.7 13.3 %copy-start.7 = (f32[36,128]{1,0:T(8,128)}, f32[36,128]{1,0:T(8,128)S(1)}, u32[]{:S(2)}) copy-start(f32[36,128]{1,0:T(8,128)S(1)} %collective-permute-done.4.c_ll) | copy-start | bytes 55300
  31.7 10.7 %collective-permute-start.7 = (f32[36,128]{1,0:T(8,128)S(1)}, f32[36,128]{1,0:T(8,128)S(1)}, u32[]{:S(2)}, u32[]{:S(2)}) collective-permute-start(f32[36,128]{1,0:T(8,128)S(1)} %pad_maximum_fusion.5), channel_id=1, source_target_pairs={{9,0},{10,1},{11,2},{12,3},{13,4},{14,5},{15,6},{17,8},{18,9},{19,... | collective-permute-start | bytes 55304 | tf_op jit(solution)/shard_map/ppermute | solution.py:451
  42.4 2.7 %copy-start.8 = (f32[36,128]{1,0:T(8,128)}, f32[36,128]{1,0:T(8,128)S(1)}, u32[]{:S(2)}) copy-start(f32[36,128]{1,0:T(8,128)S(1)} %collective-permute-done.7.c_hh) | copy-start | bytes 55300
  42.4 2.6 %collective-permute-start.5 = (f32[36,128]{1,0:T(8,128)S(1)}, f32[36,128]{1,0:T(8,128)S(1)}, u32[]{:S(2)}, u32[]{:S(2)}) collective-permute-start(f32[36,128]{1,0:T(8,128)S(1)} %pad_maximum_fusion.3), channel_id=1, source_target_pairs={{1,8},{2,9},{3,10},{4,11},{5,12},{6,13},{7,14},{9,16},{10,17},{11,... | collective-permute-start | bytes 55304 | tf_op jit(solution)/shard_map/ppermute | solution.py:451
  44.9 0.6 copy-start.9
  44.9 0.7 copy-start.2
  44.9 0.8 copy-start.3
  45.0 0.9 copy-start.4
  45.0 1.0 copy-start.5
Sparse Core Ops, SparseCore 0:
  57.4 71.4 all-gather.2

commit v2 on v1

--- a/solution.py
+++ b/solution.py
@@ -1,3 +1,6 @@
+import functools
+import math
+
 import jax
 import jax.numpy as jnp
 from jax import lax
@@ -28,11 +31,51 @@
     return hi, lo
 
 
+def cut_kernel(
+    mem, cour, turb, diss, x_first, x_last, y_first, y_last, diff
+):
+    members_n = mem.shape[0]
+    t = turb[...]
+    diff[0] = diffuse_rate * t * t / diss[...]
+
+    def one(ref, i, f):
+        x_first[f, 0] = ref[i, 0:8, :]
+        x_first[f, 1] = ref[i, 8:16, :]
+        x_last[f, 0] = ref[i, 48:56, :]
+        x_last[f, 1] = ref[i, 56:64, :]
+        for k in range(2):
+            y_first[f, k] = ref[i, pl.ds(k, 8, stride=8), :]
+            y_last[f, k] = ref[i, pl.ds(6 + k, 8, stride=8), :]
+
+    def members_loop(i, carry):
+        one(mem, i, i)
+        return carry
+
+    lax.fori_loop(0, members_n, members_loop, 0)
+    for d in range(3):
+        one(cour, d, members_n + d)
+    one(diff, 0, members_n + 3)
+
+
+def edge_kernel(xlo, xhi, last, first):
+    fields = xlo.shape[0]
+
+    def one(f, carry):
+        last[pl.ds(f, 1), :] = xlo[f, 1, 7:8, :]
+        last[pl.ds(fields + f, 1), :] = xhi[f, 0, 7:8, :]
+        first[pl.ds(f, 1), :] = xlo[f, 1, 0:1, :]
+        first[pl.ds(fields + f, 1), :] = xhi[f, 0, 0:1, :]
+        return carry
+
+    lax.fori_loop(0, fields, one, 0, unroll=4)
+
+
 def forecast_kernel(
     place_ref, count_ref, mem, cour, turb, diss, xlo, xhi, ylo, yhi, own_lo, own_hi,
-    c_ll, c_lh, c_hl, c_hh, cells, frac, obs, out, kc, state,
+    edge_lo, edge_hi, cells, frac, obs, out, kc, state,
 ):
     members_n = mem.shape[0]
+    fields = members_n + 4
     slots = cells.shape[1]
     grp, tile = place_ref[0], place_ref[1]
     last_grp, last_tile = place_ref[2], place_ref[3]
@@ -69,9 +112,9 @@
 
     def xends(f, x):
         if x < 0:
-            return row(c_ll, f), row(c_lh, f)
+            return row(edge_lo, f), row(edge_hi, f)
         if x > 7:
-            return row(c_hl, f), row(c_hh, f)
+            return row(edge_lo, fields + f), row(edge_hi, fields + f)
         return ylo[f, 1, x : x + 1, :], yhi[f, 0, x : x + 1, :]
 
     def face(cp, ep, cq, eq):
@@ -124,10 +167,10 @@
         return own_hi[f, 1], yhi[f, 0], yhi[f, 1]
 
     def yends_lo(f):
-        return row(c_ll, f), row(c_hl, f)
+        return row(edge_lo, f), row(edge_lo, fields + f)
 
     def yends_hi(f):
-        return row(c_lh, f), row(c_hh, f)
+        return row(edge_hi, f), row(edge_hi, fields + f)
 
     coefs(10, kept(tile > 0), 1, 0, yplanes_lo, yends_lo)
     coefs(11, kept(tile < last_tile), 1, 0, yplanes_hi, yends_hi)
@@ -161,7 +204,7 @@
         return tuple(sums)
 
     zero = jnp.zeros((8, LANES), F32)
-    total = lax.fori_loop(0, members_n, one_member, (zero,) * 8)
+    total = lax.fori_loop(0, members_n, one_member, (zero,) * 8, unroll=4)
     mean = jnp.concatenate(total, 0) * (1.0 / members_n)
 
     base = cells[0:1, :]
@@ -182,6 +225,7 @@
     wxy = jnp.concatenate([wx[x : x + 1, :] * wy for x in range(8)], 0)
 
     group = 8
+    parts = slots // LANES
 
     def some_members(step, carry):
         field = state[pl.ds(step * group, group)] - mean[None]
@@ -190,35 +234,40 @@
             jnp.concatenate([hi, lo, hi], 1), wz, preferred_element_type=F32
         ).reshape(group, 64, slots)
         picked = jnp.sum(along * wxy[None], axis=1)
-        out[pl.ds(pl.multiple_of(step * group, group), group), :] = picked.astype(BF16).astype(F32)
+        picked = picked.astype(BF16).astype(F32)
+        for c in range(parts):
+            out[pl.ds(pl.multiple_of(c * members_n + step * group, group), group), :] = picked[
+                :, c * LANES : (c + 1) * LANES
+            ]
         return carry
 
-    lax.fori_loop(0, members_n // group, some_members, 0)
-    tail = jnp.concatenate(
-        [
-            (grp * 8 + x0).astype(F32) + fx,
-            (tile * 8 + y0).astype(F32) + fy,
-            z0.astype(F32) + fz,
-            jnp.full((1, slots), count_ref[0], jnp.int32).astype(F32),
-            obs[...],
-            jnp.zeros((3, slots), F32),
-        ],
-        0,
+    lax.fori_loop(0, members_n // group, some_members, 0, unroll=True)
+    extras = (
+        (grp * 8 + x0).astype(F32) + fx,
+        (tile * 8 + y0).astype(F32) + fy,
+        z0.astype(F32) + fz,
+        jnp.full((1, slots), count_ref[0], jnp.int32).astype(F32),
+        obs[...],
     )
-    out[members_n : members_n + 8, :] = tail
+    for e, value in enumerate(extras):
+        for c in range(parts):
+            at = (members_n + e) * parts + c
+            out[at : at + 1, :] = value[:, c * LANES : (c + 1) * LANES]
+    used = (members_n + len(extras)) * parts
+    if used < out.shape[0]:
+        out[used:, :] = jnp.zeros((out.shape[0] - used, LANES), F32)
 
 
 def taper_cov(left, right, members_n):
     cov = jnp.dot(
         left[:, :members_n].astype(BF16), right[:members_n].astype(BF16), preferred_element_type=F32
     )
-    dist = None
+    dist = members_n - 1.0
     for d in range(3):
         at = members_n + d
         gap = left[:, at : at + 1] - right[at : at + 1, :]
-        dist = gap * gap if dist is None else dist + gap * gap
-    scale = 1.0 / (members_n - 1.0)
-    return cov * (scale / (1.0 + dist * (1.0 / (LOC * LOC))))
+        dist = dist + gap * gap
+    return cov * pl.reciprocal(dist, approx=True)
 
 
 def eliminate(a):
@@ -237,24 +286,29 @@
     for gk in range(groups):
         k0 = 8 * gk
         col = [across(a[gk], k0 + j) for j in range(8)]
+        u = [[down(col[j], i) if i >= j else None for i in range(8)] for j in range(8)]
+        inv = []
+        for j in range(8):
+            inv.append(pl.reciprocal(u[j][j], approx=True))
+            for i in range(j + 1, 8):
+                f = u[j][i] * inv[j]
+                for k in range(i, 8):
+                    u[i][k] = u[i][k] - f * u[j][k]
         ra, rm = a[gk], m[gk]
-        rows_a, rows_m, inv, u = [], [], [], []
-        diag = jnp.ones((8, LANES), F32)
+        rows_a, rows_m = [], []
+        diag = u[0][0]
         for j in range(8):
-            pivot = down(col[j], j)
-            r = 1.0 / pivot
-            diag = jnp.where(sub == j, pivot, diag)
+            diag = jnp.where(sub == j, u[j][j], diag)
             row_a, row_m = down(ra, j), down(rm, j)
-            uj = [down(col[i], j) if i > j else None for i in range(8)]
-            f = jnp.where(sub > j, col[j] * r, 0.0)
+            rows_a.append(row_a)
+            rows_m.append(row_m)
+            if j == 7:
+                break
+            f = jnp.where(sub > j, col[j] * inv[j], 0.0)
             for i in range(j + 1, 8):
-                col[i] = col[i] - f * uj[i]
+                col[i] = col[i] - f * u[j][i]
             ra = ra - f * row_a
             rm = rm - f * row_m
-            rows_a.append(row_a)
-            rows_m.append(row_m)
-            inv.append(r)
-            u.append(uj)
         done.append(rm * lax.rsqrt(diag))
         for g in range(gk + 1, groups):
             c = [across(a[g], k0 + j) for j in range(8)]
@@ -269,50 +323,94 @@
     return jnp.concatenate(done, 0)
 
 
-def head_kernel(
-    offset_ref, place_ref, everything, obs_head, rows_out, cols_out, head_out, linv_out, fcols_out,
-    full, work,
+def turned(chunk):
+    return jnp.concatenate([chunk, jnp.zeros((LANES - ROWS, LANES), F32)], 0).T
+
+
+def head_stage(
+    place_ref, pieces, patterns, parts, cols_out, head_out, down_out, linv_out, fcols_out, obs_head, full, work,
+    count_vec, count_smem, sem,
 ):
-    blocks, _, slots = everything.shape
-    row_chunks = rows_out.shape[0] // LANES
     col_chunks = cols_out.shape[1] // LANES
     members_n = ROWS - 8
     grp, tile = place_ref[0], place_ref[1]
+    tiles = place_ref[3] + 1
+    sub = lax.broadcasted_iota(jnp.int32, (8, LANES), 0)
+    lane8 = lax.broadcasted_iota(jnp.int32, (8, LANES), 1)
     lane = lax.broadcasted_iota(jnp.int32, (ROWS, LANES), 1)
-    parts = slots // LANES
-
-    def pack(b, carry):
-        at = offset_ref[b]
-        chunk = lax.div(at, LANES)
-        shift = lax.rem(at, LANES)
-        early = lane < shift
-        last = full[chunk]
-        for j in range(parts):
-            now = pltpu.roll(everything[b, :, j * LANES : (j + 1) * LANES], shift, 1)
-            full[chunk + j] = jnp.where(early, last, now)
-            last = now
-        full[chunk + parts] = last
-        return carry
-
-    lax.fori_loop(0, blocks, pack, 0)
-
-    def turn(c, carry):
-        piece = jnp.concatenate([full[grp * row_chunks + c], jnp.zeros((LANES - ROWS, LANES), F32)], 0)
-        rows_out[pl.ds(pl.multiple_of(c * LANES, LANES), LANES), :] = piece.T
-        return carry
-
-    lax.fori_loop(0, row_chunks, turn, 0)
+    blocks = sum(len(p) for p in patterns)
+    unit = math.sqrt(members_n - 1.0) / LOC
+
+    def source(pattern):
+        return (grp ^ pattern[0]) * tiles + (tile ^ pattern[1])
+
+    for r in range(-(-blocks // LANES)):
+        counts = jnp.zeros((1, LANES), F32)
+        for piece, pattern in zip(pieces, patterns):
+            for k, one in enumerate(pattern):
+                at = (members_n + 3) * parts
+                here = lane8[:1] + r * LANES == source(one)
+                counts = jnp.where(here, piece[k, at : at + 1, :], counts)
+        count_vec[r : r + 1, :] = counts.astype(jnp.int32)
+    copy = pltpu.make_async_copy(count_vec, count_smem, sem)
+    copy.start()
+    copy.wait()
+
+    def add_up(b, total):
+        r, c = lax.div(b, LANES), lax.rem(b, LANES)
+        count = count_smem[r, c]
+        count_smem[r + count_smem.shape[0] // 2, c] = total
+        return total + count
+
+    lax.fori_loop(0, blocks, add_up, jnp.int32(0))
+
+    for piece, pattern in zip(pieces, patterns):
+        for k, one in enumerate(pattern):
+            src = source(one)
+            r, c = lax.div(src, LANES), lax.rem(src, LANES)
+            count = count_smem[r, c]
+            at = count_smem[r + count_smem.shape[0] // 2, c]
+            chunk = lax.div(at, LANES)
+            shift = lax.rem(at, LANES)
+            early = lane < shift
+            last = None
+            for j in range(parts + 1):
+                if j < parts:
+                    tail = jnp.zeros((8, LANES), F32)
+                    for d in range(3):
+                        e = (members_n + d) * parts + j
+                        tail = jnp.where(sub == d, piece[k, e : e + 1, :] * unit, tail)
+                    now = jnp.concatenate([piece[k, j * members_n : (j + 1) * members_n, :], tail], 0)
+                    now = pltpu.roll(now, shift, 1)
+                    moved = now if j == 0 else jnp.where(early, last, now)
+                else:
+                    moved = last
+                live = lane < shift + count - j * LANES
+                if j == 0:
+                    live = live & (lane >= shift)
+                last = now
+                full[chunk + j] = jnp.where(live, moved, full[chunk + j])
+
+            @pl.when((lax.rem(src, tiles) == 0) & (src * parts < tiles * PANELS))
+            def _(piece=piece, k=k, src=src):
+                holder = lax.div(src, tiles)
+                for j in range(min(parts, PANELS)):
+                    e = (members_n + 4) * parts + j
+                    full[full.shape[0] - 1, pl.ds(holder * min(parts, PANELS) + j, 1), :] = piece[
+                        k, e : e + 1, :
+                    ]
+
+    for j in range(PANELS):
+        obs_head[:, j * LANES : (j + 1) * LANES] = full[full.shape[0] - 1, j : j + 1, :]
+
     for c in range(col_chunks):
         cols_out[:, c * LANES : (c + 1) * LANES] = full[tile * col_chunks + c]
     for c in range(PANELS):
         head_out[:, c * LANES : (c + 1) * LANES] = full[c]
+        down_out[c * LANES : (c + 1) * LANES, :] = turned(full[c])
 
     head = head_out[...]
-    down = []
-    for c in range(PANELS):
-        piece = jnp.concatenate([full[c], jnp.zeros((LANES - ROWS, LANES), F32)], 0)
-        down.append(piece.T)
-    down = jnp.concatenate(down, 0)
+    down = down_out[...]
     rid = lax.broadcasted_iota(jnp.int32, (HEAD, HEAD), 0)
     cid = lax.broadcasted_iota(jnp.int32, (HEAD, HEAD), 1)
     same = rid == cid
@@ -329,14 +427,16 @@
                         q * PANEL + 8 * g : q * PANEL + 8 * g + 8, q * PANEL : (q + 1) * PANEL
                     ]
         inverse = eliminate([work[HEAD + 8 * g : HEAD + 8 * g + 8, :PANEL] for g in range(16)])
-        done = jnp.dot(inverse, work[pl.ds(at, PANEL), :], precision=HIGH, preferred_element_type=F32)
-        work[pl.ds(at, PANEL), :] = done
+        wide = pl.ds(at, HEAD + PANEL)
+        done = jnp.dot(inverse, work[pl.ds(at, PANEL), wide], precision=HIGH, preferred_element_type=F32)
+        work[pl.ds(at, PANEL), wide] = done
         for q in range(PANELS - 1):
             @pl.when(p == q)
             def _(q=q):
                 rest = (q + 1) * PANEL
-                upper = done[:, rest:HEAD]
-                work[rest:HEAD, :] = work[rest:HEAD, :] - lax.dot_general(
+                upper = done[:, PANEL : HEAD - q * PANEL]
+                some = slice(q * PANEL, HEAD + rest)
+                work[rest:HEAD, some] = work[rest:HEAD, some] - lax.dot_general(
                     upper, done, (((0,), (0,)), ((), ())), precision=HIGH, preferred_element_type=F32
                 )
         return carry
@@ -372,31 +472,55 @@
     lax.fori_loop(0, cols_out.shape[1] // width, some_cols, jnp.broadcast_to(noise_down, (HEAD, width)))
 
 
-def final_kernel(place_ref, rows, cols, head, linv, fcols, obs_head, obs, trailing, factor, keep):
+def final_kernel(place_ref, *refs, patterns, parts):
+    pieces = refs[: len(patterns)]
+    obs, trailing, factor = refs[len(patterns) : len(patterns) + 3]
+    (
+        cols, head, down, linv, fcols, obs_head, full, work, count_vec, count_smem, sem, keep, lefts, factors,
+    ) = refs[len(patterns) + 3 :]
     members_n = ROWS - 8
     step = pl.program_id(0)
     grp, tile = place_ref[0], place_ref[1]
-    height = rows.shape[0]
+    height, col_span = trailing.shape
     steps = pl.num_programs(0)
-    col_span = cols.shape[1]
     first_row = (grp * steps + step) * height
     first_col = tile * col_span
-    left = rows[...]
-    rid = lax.broadcasted_iota(jnp.int32, (height, HEAD), 0) + first_row
-    cid = lax.broadcasted_iota(jnp.int32, (height, HEAD), 1)
-    cross = taper_cov(left, head[...], members_n) + jnp.where(rid == cid, obs_head[...], 0.0)
-    hi, lo = split(cross)
-    f = lax.dot_general(
-        jnp.concatenate([hi, lo, hi], 1), linv[...], (((1,), (1,)), ((), ())), preferred_element_type=F32
-    )
-    f = jnp.where(rid >= lax.div(cid, PANEL) * PANEL, f, 0.0)
-    keep[pl.ds(pl.multiple_of(step * height, height), height), :] = f
-    hi, lo = split(f)
-    f3 = jnp.concatenate([hi, hi, lo], 1)
+    chunks = height // LANES
+
+    def prepare(at, slot):
+        first = (grp * steps + at) * height
+        left = jnp.concatenate([turned(full[lax.div(first, LANES) + c]) for c in range(chunks)], 0)
+        lefts[slot] = left
+        rid = lax.broadcasted_iota(jnp.int32, (height, HEAD), 0) + first
+        cid = lax.broadcasted_iota(jnp.int32, (height, HEAD), 1)
+        cross = taper_cov(left, head[...], members_n) + jnp.where(rid == cid, obs_head[...], 0.0)
+        hi, lo = split(cross)
+        f = lax.dot_general(
+            jnp.concatenate([hi, lo, hi], 1), linv[...], (((1,), (1,)), ((), ())),
+            preferred_element_type=F32,
+        )
+        f = jnp.where(rid >= lax.div(cid, PANEL) * PANEL, f, 0.0)
+        keep[pl.ds(pl.multiple_of(at * height, height), height), :] = f
+        hi, lo = split(f)
+        factors[slot, :, :HEAD] = hi
+        factors[slot, :, HEAD : 2 * HEAD] = hi
+        factors[slot, :, 2 * HEAD :] = lo
+
+    @pl.when(step == 0)
+    def _():
+        head_stage(
+            place_ref, pieces, patterns, parts, cols, head, down, linv, fcols, obs_head, full, work,
+            count_vec, count_smem, sem,
+        )
+        prepare(0, 0)
+
+    slot = lax.rem(step, 2)
+    left = lefts[slot]
+    f3 = factors[slot]
+    prepare(jnp.minimum(step + 1, steps - 1), 1 - slot)
     width = min(512, col_span)
     for c in range(0, col_span, width):
-        part = cols[:, c : c + width]
-        value = taper_cov(left, part, members_n)
+        value = taper_cov(left, cols[:, c : c + width], members_n)
         trailing[:, c : c + width] = value - jnp.dot(
             f3, fcols[:, c : c + width], preferred_element_type=F32
         )
@@ -414,6 +538,45 @@
     def _():
         share = factor.shape[0]
         factor[...] = keep[pl.ds(pl.multiple_of(tile * share, share), share), :]
+
+
+def gather(unit, grp_size, tile_size):
+    def swap(piece, dg, dt):
+        value, pattern = piece
+        pairs = [
+            (g * tile_size + t, (g ^ dg) * tile_size + (t ^ dt))
+            for g in range(grp_size)
+            for t in range(tile_size)
+        ]
+        return lax.ppermute(value, ("grp", "tile"), pairs), [(p ^ dg, q ^ dt) for p, q in pattern]
+
+    def join(*some):
+        return jnp.concatenate([v for v, _ in some], 0), sum([p for _, p in some], [])
+
+    a = (unit[None], [(0, 0)])
+    if (grp_size, tile_size) == (4, 8):
+        b, c, d = swap(a, 0, 2), swap(a, 0, 4), swap(a, 0, 6)
+        a = join(a, swap(a, 0, 1))
+        ya = swap(a, 2, 0)
+        b = join(b, swap(b, 2, 0))
+        xb = swap(b, 0, 1)
+        c = join(c, swap(c, 0, 1))
+        yc = swap(c, 2, 0)
+        d = join(d, swap(d, 2, 0))
+        xd = swap(d, 0, 1)
+        pieces = [a, b, ya, xb, c, d, yc, xd]
+        pieces = pieces + [swap(p, 1, 0) for p in pieces]
+    else:
+        bit = 1
+        while bit < tile_size:
+            a = join(a, swap(a, 0, bit))
+            bit *= 2
+        bit = 1
+        while bit < grp_size:
+            a = join(a, swap(a, bit, 0))
+            bit *= 2
+        pieces = [a]
+    return [v for v, _ in pieces], [p for _, p in pieces]
 
 
 def spec(space=pltpu.VMEM):
@@ -432,15 +595,18 @@
     blocks = grp_size * tile_size
     place = jnp.stack([grp, tile, jnp.int32(grp_size - 1), jnp.int32(tile_size - 1)]).astype(jnp.int32)
 
-    diffusion = diffuse_rate * turb_energy * turb_energy / dissipation
-
-    def cut(xs, ys):
-        return jnp.concatenate([members[:, xs, ys], courant[:, xs, ys], diffusion[None, xs, ys]], 0)
-
-    every = slice(None)
-    x_first, x_last = cut(slice(0, 2), every), cut(slice(6, 8), every)
-    y_first = jnp.swapaxes(cut(every, slice(0, 2)), 1, 2)
-    y_last = jnp.swapaxes(cut(every, slice(6, 8)), 1, 2)
+    face = jax.ShapeDtypeStruct((members_n + 4, 2, 8, LANES), F32)
+    x_first, x_last, y_first, y_last = pl.pallas_call(
+        cut_kernel,
+        out_shape=[face] * 4,
+        in_specs=[spec()] * 4,
+        out_specs=[spec()] * 4,
+        scratch_shapes=[pltpu.VMEM((1, 64, LANES), F32)],
+        name="cut",
+    )(
+        members.reshape(members_n, 64, LANES), courant.reshape(3, 64, LANES),
+        turb_energy.reshape(64, LANES), dissipation.reshape(64, LANES),
+    )
 
     def move(value, dg, dt):
         pairs = []
@@ -452,77 +618,68 @@
 
     xlo, xhi = move(x_last, 1, 0), move(x_first, -1, 0)
     ylo, yhi = move(y_last, 0, 1), move(y_first, 0, -1)
-    c_ll, c_lh = move(cut(7, 7), 1, 1), move(cut(7, 0), 1, -1)
-    c_hl, c_hh = move(cut(0, 7), -1, 1), move(cut(0, 0), -1, -1)
+    edge = jax.ShapeDtypeStruct((2 * (members_n + 4), LANES), F32)
+    edge_last, edge_first = pl.pallas_call(
+        edge_kernel,
+        out_shape=[edge] * 2,
+        in_specs=[spec()] * 2,
+        out_specs=[spec()] * 2,
+        name="edges",
+    )(xlo, xhi)
+    edge_lo, edge_hi = move(edge_last, 0, 1), move(edge_first, 0, -1)
 
     obs_at = jnp.minimum(grp * slots, obs_var.shape[0] - slots)
     obs_part = lax.dynamic_slice_in_dim(obs_var, obs_at, slots, 0)[None]
 
+    parts = slots // LANES
     message = pl.pallas_call(
         forecast_kernel,
-        out_shape=jax.ShapeDtypeStruct((ROWS, slots), F32),
-        in_specs=[spec(pltpu.SMEM)] * 2 + [spec()] * 17,
+        out_shape=jax.ShapeDtypeStruct((-(-(members_n + 5) * parts // 8) * 8, LANES), F32),
+        in_specs=[spec(pltpu.SMEM)] * 2 + [spec()] * 15,
         out_specs=spec(),
         scratch_shapes=[pltpu.VMEM((12, 7, 8, LANES), F32), pltpu.VMEM((members_n, 64, LANES), F32)],
         compiler_params=pltpu.CompilerParams(vmem_limit_bytes=VMEM_LIMIT),
         name="forecast",
     )(
         place, sensor_count, members, courant, turb_energy, dissipation, xlo, xhi, ylo, yhi,
-        y_first, y_last, c_ll, c_lh, c_hl, c_hh, sensor_cells, sensor_frac, obs_part,
+        y_first, y_last, edge_lo, edge_hi, sensor_cells, sensor_frac, obs_part,
     )
 
-    everything = lax.all_gather(message, ("grp", "tile"), axis=0)
-    counts = everything[:, members_n + 3, 0].astype(jnp.int32)
-    offsets = jnp.cumsum(counts) - counts
-    holders = -(-HEAD // slots)
-    obs_head = everything[: holders * tile_size : tile_size, members_n + 4].reshape(1, -1)[:, :HEAD]
+    pieces, patterns = gather(message, grp_size, tile_size)
 
     row_span = NS // grp_size
     col_span = NS // tile_size
-    rows, cols, head, linv, fcols = pl.pallas_call(
-        head_kernel,
-        out_shape=[
-            jax.ShapeDtypeStruct((row_span, LANES), F32),
-            jax.ShapeDtypeStruct((ROWS, col_span), F32),
-            jax.ShapeDtypeStruct((ROWS, HEAD), F32),
-            jax.ShapeDtypeStruct((HEAD, 3 * HEAD), BF16),
-            jax.ShapeDtypeStruct((3 * HEAD, col_span), BF16),
-        ],
-        in_specs=[spec(pltpu.SMEM)] * 2 + [spec()] * 2,
-        out_specs=[spec()] * 5,
-        scratch_shapes=[
-            pltpu.VMEM((NS // LANES + slots // LANES + 1, ROWS, LANES), F32),
-            pltpu.VMEM((HEAD + PANEL, 2 * HEAD), F32),
-        ],
-        compiler_params=pltpu.CompilerParams(vmem_limit_bytes=VMEM_LIMIT),
-        name="head",
-    )(offsets, place, everything, obs_head)
-
+    count_rows = -(-grp_size * tile_size // LANES)
     height = 256
     share = row_span // tile_size
-    whole = lambda shape: pl.BlockSpec(shape, lambda i: (0, 0))
     trailing, factor = pl.pallas_call(
-        final_kernel,
+        functools.partial(final_kernel, patterns=patterns, parts=parts),
         grid=(row_span // height,),
         out_shape=[
             jax.ShapeDtypeStruct((row_span, col_span), F32),
             jax.ShapeDtypeStruct((share, HEAD), F32),
         ],
-        in_specs=[
-            spec(pltpu.SMEM),
-            pl.BlockSpec((height, LANES), lambda i: (i, 0)),
-            whole((ROWS, col_span)),
-            whole((ROWS, HEAD)),
-            whole((HEAD, 3 * HEAD)),
-            whole((3 * HEAD, col_span)),
-            whole((1, HEAD)),
-            whole((1, col_span)),
+        in_specs=[spec(pltpu.SMEM)] + [spec()] * (len(pieces) + 1),
+        out_specs=[pl.BlockSpec((height, col_span), lambda i: (i, 0)), pl.BlockSpec((share, HEAD), lambda i: (0, 0))],
+        scratch_shapes=[
+            pltpu.VMEM((ROWS, col_span), F32),
+            pltpu.VMEM((ROWS, HEAD), F32),
+            pltpu.VMEM((HEAD, LANES), F32),
+            pltpu.VMEM((HEAD, 3 * HEAD), BF16),
+            pltpu.VMEM((3 * HEAD, col_span), BF16),
+            pltpu.VMEM((1, HEAD), F32),
+            pltpu.VMEM((NS // LANES + parts + 2, ROWS, LANES), F32),
+            pltpu.VMEM((HEAD + PANEL, 2 * HEAD), F32),
+            pltpu.VMEM((2 * count_rows, LANES), jnp.int32),
+            pltpu.SMEM((2 * count_rows, LANES), jnp.int32),
+            pltpu.SemaphoreType.DMA,
+            pltpu.VMEM((row_span, HEAD), F32),
+            pltpu.VMEM((2, height, LANES), F32),
+            pltpu.VMEM((2, height, 3 * HEAD), BF16),
         ],
-        out_specs=[pl.BlockSpec((height, col_span), lambda i: (i, 0)), whole((share, HEAD))],
-        scratch_shapes=[pltpu.VMEM((row_span, HEAD), F32)],
         compiler_params=pltpu.CompilerParams(vmem_limit_bytes=VMEM_LIMIT),
-        name="final",
-    )(place, rows, cols, head, linv, fcols, obs_head, obs_var[None])
+        name="panels",
+    )(place, *pieces, obs_var[None])
     return trailing, factor
 
 

time: 239 us -> 171 us (0.72)
  waiting for transfers between devices: 81 us -> 23.7 us
  starting transfers between devices: 18.7 us -> 34.2 us
  between operations: 15.1 us -> 1.82 us
  local copies, waits for them, and re-layouts: 9.53 us -> 4.11 us
  Pallas kernels: 109 us -> 105 us
  other arithmetic: 4.66 us -> 1.53 us
    all_gather x1 -> x0, waiting for transfers between devices: 71.6 us -> none  [per_device(): everything = lax.all_gather(message, ('grp', 'tile'), axis=0)]
    ppermute x0 -> x19, waiting for transfers between devices: none -> 21.1 us  [swap(): lax.ppermute(value, ('grp', 'tile'), pairs)]
    ppermute x0 -> x19, starting transfers between devices: none -> 19.2 us  [swap(): lax.ppermute(value, ('grp', 'tile'), pairs)]
    slice x7 -> x0, local copies, waits for them, and re-layouts: 7.07 us -> none  [the longest x3 3.99 us: cut(): members[:, xs, ys]]
    ppermute x8 -> x6, waiting for transfers between devices: 9.35 us -> 2.55 us  [move(): return lax.ppermute(value, ('grp', 'tile'), pairs)]
    pallas_call x3 -> x4, Pallas kernels: 109 us -> 105 us  [the longest x1 93 us: per_device(): pl.pallas_call(functools.partial(final_kernel, patterns=patterns, parts=p...]
    ppermute x8 -> x6, starting transfers between devices: 18.6 us -> 15 us  [move(): return lax.ppermute(value, ('grp', 'tile'), pairs)]
    convert_element_type x2 -> x0, other arithmetic: 2.49 us -> none  [per_device(): counts = everything[:, members_n + 3, 0].astype(jnp.int32)]
  transfers between devices with their start and end apart: 9 -> 25, of which waited for: 2 -> 12; matrix products, arithmetic and copies ran while one was open for 3% -> 2% of each run, Pallas kernels for 0% -> 1%
where the time goes in v2:
time: 171 us; the launch traced here: 170 us
  Pallas kernels  105 us (61%)
  starting transfers between devices  34.2 us (20%)
  waiting for transfers between devices  23.7 us (14%)
  local copies, waits for them, and re-layouts  4.11 us (2%)
  between operations  1.82 us (1%)
    pallas_call x1, Pallas kernels, per_device(): pl.pallas_call(functools.partial(final_kernel, patterns=patterns, parts=p...  93 us
    ppermute x19, waiting for transfers between devices, swap(): lax.ppermute(value, ('grp', 'tile'), pairs)  21.1 us
    ppermute x19, starting transfers between devices, swap(): lax.ppermute(value, ('grp', 'tile'), pairs)  19.2 us
    ppermute x6, starting transfers between devices, move(): return lax.ppermute(value, ('grp', 'tile'), pairs)  15 us
    pallas_call x1, Pallas kernels, per_device(): pl.pallas_call(forecast_kernel, out_shape=jax.ShapeDtypeStruct((-(-(membe...  7.53 us
  transfers between devices with their start and end apart: 25, of which 12 were waited for; matrix products, arithmetic and copies ran while one was open for 2% of the time, Pallas kernels for 1%

profile of v2, /device:TPU:0, one launch (start us, length us, event | category | flops | bytes accessed | tf_op | source)
XLA Modules:
  0.0 170.2 jit_solution(3137582052452656890)
XLA Ops:
  0.6 2.6 %cut.1 = (f32[36,2,8,128]{3,2,1,0:T(8,128)}, f32[36,2,8,128]{3,2,1,0:T(8,128)}, f32[36,2,8,128]{3,2,1,0:T(8,128)}, f32[36,2,8,128]{3,2,1,0:T(8,128)}) custom-call(f32[32,64,128]{2,1,0:T(8,128)} %bitcast.9, f32[3,64,128]{2,1,0:T(8,128)} %bitcast.15, f32[64,128]{1,0:T(8,128)} %bitcast.16, f32[64,128]{1,0:T(8,128)} %bitcast.17), custom_call_target="tpu_custom_call" | custom-call | tf_op jit(solution)/shard_map/cut/pallas_call | solution.py:599
  3.2 2.4 %collective-permute-start = (f32[36,2,8,128]{3,2,1,0:T(8,128)}, f32[36,2,8,128]{3,2,1,0:T(8,128)S(1)}, u32[]{:S(2)}, u32[]{:S(2)}) collective-permute-start(f32[36,2,8,128]{3,2,1,0:T(8,128)} %get-tuple-element.8), channel_id=1, source_target_pairs={{0,8},{1,9},{2,10},{3,11},{4,12},{5,13},{6,14},{7,15},{8,16},{9,17... | collective-permute-start | bytes 884744 | tf_op jit(solution)/shard_map/ppermute | solution.py:617
  5.5 1.3 collective-permute-start.1
  6.8 4.2 %collective-permute-start.2 = (f32[36,2,8,128]{3,2,1,0:T(8,128)}, f32[36,2,8,128]{3,2,1,0:T(8,128)S(1)}, u32[]{:S(2)}, u32[]{:S(2)}) collective-permute-start(f32[36,2,8,128]{3,2,1,0:T(8,128)} %get-tuple-element.10.own_hi), channel_id=1, source_target_pairs={{0,1},{1,2},{2,3},{3,4},{4,5},{5,6},{6,7},{8,9},{9,10},{10,11},{11... | collective-permute-start | bytes 884744 | tf_op jit(solution)/shard_map/ppermute | solution.py:617
  11.1 1.3 collective-permute-start.3
  12.4 0.0 collective-permute-done.xlo
  12.4 0.0 copy-start.1
  12.4 0.0 collective-permute-done.1.xhi
  12.4 0.7 copy-done.1
  13.1 0.7 copy-done.2
  13.8 1.8 %edges.1 = (f32[72,128]{1,0:T(8,128)}, f32[72,128]{1,0:T(8,128)}) custom-call(f32[36,2,8,128]{3,2,1,0:T(8,128)} %copy-done.1, f32[36,2,8,128]{3,2,1,0:T(8,128)} %copy-done.2), custom_call_target="tpu_custom_call" | custom-call | tf_op jit(solution)/shard_map/edges/pallas_call | solution.py:622
  15.6 4.5 %collective-permute-start.4 = (f32[72,128]{1,0:T(8,128)}, f32[72,128]{1,0:T(8,128)S(1)}, u32[]{:S(2)}, u32[]{:S(2)}) collective-permute-start(f32[72,128]{1,0:T(8,128)} %get-tuple-element.12), channel_id=1, source_target_pairs={{0,1},{1,2},{2,3},{3,4},{4,5},{5,6},{6,7},{8,9},{9,10},{10,11},{11... | collective-permute-start | bytes 110600 | tf_op jit(solution)/shard_map/ppermute | solution.py:617
  20.2 1.3 collective-permute-start.5
  21.5 0.6 pad_add_fusion.place_ref
  22.7 1.4 dynamic_slice.3
  24.1 0.0 collective-permute-done.2.ylo
  24.1 0.3 collective-permute-done.4.edge_lo
  24.4 2.3 %collective-permute-done.5.edge_hi = f32[72,128]{1,0:T(8,128)S(1)} collective-permute-done((f32[72,128]{1,0:T(8,128)}, f32[72,128]{1,0:T(8,128)S(1)}, u32[]{:S(2)}, u32[]{:S(2)}) %collective-permute-start.5) | collective-permute-done | bytes 36896 | tf_op jit(solution)/shard_map/ppermute | solution.py:617
  26.7 0.6 copy-done.21
  27.3 7.5 %forecast.1 = f32[296,128]{1,0:T(8,128)} custom-call(s32[4]{0:T(128)} %pad_add_fusion.place_ref, s32[1]{0:T(128)S(6)} %copy.13.count_ref, f32[32,8,8,128]{3,2,1,0:T(8,128)} %mem.1, f32[3,8,8,128]{3,2,1,0:T(8,128)} %cour.1, f32[8,8,128]{2,1,0:T(8,128)} %turb.1, f32[8,8,128]{2,1,0:T(8,128)} %diss.1, f32[36,2,8,128]{3,2,1,0:T(8,128)} %copy-done.1, ...), custom_call_target="tpu_custom_call" | custom-call | tf_op jit(solution)/shard_map/forecast/pallas_call | solution.py:635
  34.8 2.9 %collective-permute-start.6 = (f32[1,296,128]{2,1,0:T(8,128)}, f32[1,296,128]{2,1,0:T(8,128)S(1)}, u32[]{:S(2)}, u32[]{:S(2)}) collective-permute-start(f32[1,296,128]{2,1,0:T(8,128)} %bitcast.10), channel_id=1, source_target_pairs={{0,1},{1,0},{2,3},{3,2},{4,5},{5,4},{6,7},{7,6},{8,9},{9,8},{10,11... | collective-permute-start | bytes 454664 | tf_op jit(solution)/shard_map/ppermute | solution.py:551
  37.7 2.5 %collective-permute-start.13 = (f32[1,296,128]{2,1,0:T(8,128)}, f32[1,296,128]{2,1,0:T(8,128)S(1)}, u32[]{:S(2)}, u32[]{:S(2)}) collective-permute-start(f32[1,296,128]{2,1,0:T(8,128)} %bitcast.11), channel_id=1, source_target_pairs={{0,6},{1,7},{2,4},{3,5},{4,2},{5,3},{6,0},{7,1},{8,14},{9,15},{10,... | collective-permute-start | bytes 454664 | tf_op jit(solution)/shard_map/ppermute | solution.py:551
  40.2 0.7 collective-permute-start.7
  40.9 1.2 collective-permute-start.11
  42.1 0.3 collective-permute-done.6
  42.5 0.9 pad_maximum_fusion.refs_0_
  43.4 0.1 collective-permute-start.17
  43.5 3.8 %collective-permute-start.9 = (f32[2,296,128]{2,1,0:T(8,128)S(1)}, f32[2,296,128]{2,1,0:T(8,128)S(1)}, u32[]{:S(2)}, u32[]{:S(2)}) collective-permute-start(f32[2,296,128]{2,1,0:T(8,128)S(1)} %pad_maximum_fusion.refs_0_), channel_id=1, source_target_pairs={{0,16},{1,17},{2,18},{3,19},{4,20},{5,21},{6,22},{7,23},{8,24},{9,... | collective-permute-start | bytes 909320 | tf_op jit(solution)/shard_map/ppermute | solution.py:551
  47.3 2.4 %collective-permute-start.14 = (f32[1,296,128]{2,1,0:T(8,128)S(1)}, f32[1,296,128]{2,1,0:T(8,128)S(1)}, u32[]{:S(2)}, u32[]{:S(2)}) collective-permute-start(f32[1,296,128]{2,1,0:T(8,128)S(1)} %collective-permute-done.13), channel_id=1, source_target_pairs={{0,16},{1,17},{2,18},{3,19},{4,20},{5,21},{6,22},{7,23},{8,24},{9,... | collective-permute-start | bytes 454664 | tf_op jit(solution)/shard_map/ppermute | solution.py:551
  49.6 0.3 collective-permute-done.7
  49.9 1.2 collective-permute-start.8
  51.1 3.6 %collective-permute-done.11 = f32[1,296,128]{2,1,0:T(8,128)S(1)} collective-permute-done((f32[1,296,128]{2,1,0:T(8,128)}, f32[1,296,128]{2,1,0:T(8,128)S(1)}, u32[]{:S(2)}, u32[]{:S(2)}) %collective-permute-start.11) | collective-permute-done | bytes 151584 | tf_op jit(solution)/shard_map/ppermute | solution.py:551
  54.7 0.6 collective-permute-start.12
  55.3 3.2 %collective-permute-done.14 = f32[1,296,128]{2,1,0:T(8,128)S(1)} collective-permute-done((f32[1,296,128]{2,1,0:T(8,128)S(1)}, f32[1,296,128]{2,1,0:T(8,128)S(1)}, u32[]{:S(2)}, u32[]{:S(2)}) %collective-permute-start.14) | collective-permute-done | bytes 151584 | tf_op jit(solution)/shard_map/ppermute | solution.py:551
  58.6 0.1 collective-permute-start.22
  58.6 1.2 collective-permute-done.12
  59.9 0.6 collective-permute-start.16
  60.5 1.1 collective-permute-done.8
  61.5 0.0 collective-permute-start.21
  61.6 1.8 %collective-permute-start.15 = (f32[2,296,128]{2,1,0:T(8,128)S(1)}, f32[2,296,128]{2,1,0:T(8,128)S(1)}, u32[]{:S(2)}, u32[]{:S(2)}) collective-permute-start(f32[2,296,128]{2,1,0:T(8,128)S(1)} %constant_dynamic-update-slice_fusion.2.refs_4_), channel_id=1, source_target_pairs={{0,16},{1,17},{2,18},{3,19},{4,20},{5,21},{6,22},{7,23},{8,24},{9,... | collective-permute-start | bytes 909320 | tf_op jit(solution)/shard_map/ppermute | solution.py:551
  63.4 1.0 collective-permute-start.10
  64.4 5.6 %collective-permute-done.16.refs_7_ = f32[2,296,128]{2,1,0:T(8,128)S(1)} collective-permute-done((f32[2,296,128]{2,1,0:T(8,128)S(1)}, f32[2,296,128]{2,1,0:T(8,128)S(1)}, u32[]{:S(2)}, u32[]{:S(2)}) %collective-permute-start.16) | collective-permute-done | bytes 303136 | tf_op jit(solution)/shard_map/ppermute | solution.py:551
  70.0 0.5 collective-permute-start.24
  70.5 0.7 collective-permute-done.15.refs_6_
  71.3 3.5 %collective-permute-done.10.refs_3_ = f32[2,296,128]{2,1,0:T(8,128)S(1)} collective-permute-done((f32[2,296,128]{2,1,0:T(8,128)S(1)}, f32[2,296,128]{2,1,0:T(8,128)S(1)}, u32[]{:S(2)}, u32[]{:S(2)}) %collective-permute-start.10) | collective-permute-done | bytes 303136 | tf_op jit(solution)/shard_map/ppermute | solution.py:551
  74.8 1.5 collective-permute-done.20.refs_11_
  76.5 0.6 copy-done.17
  77.0 93.0 %panels.1 = (f32[4096,2048]{1,0:T(8,128)}, f32[512,512]{1,0:T(8,128)}) custom-call(s32[4]{0:T(128)} %pad_add_fusion.place_ref, f32[2,296,128]{2,1,0:T(8,128)} %copy-done, f32[2,296,128]{2,1,0:T(8,128)} %copy-done.3, f32[2,296,128]{2,1,0:T(8,128)} %copy-done.7, f32[2,296,128]{2,1,0:T(8,128)} %copy-done.12, f32[2,296,128]{2,1,0:T(8,128)} %copy-done.4, ...), custom_call_target="tpu_custom_call" | custom-call | tf_op jit(solution)/shard_map/panels/pallas_call | solution.py:655
  (59 shorter events, 0.2 us)
Async XLA Ops:
  3.2 9.2 %collective-permute-start = (f32[36,2,8,128]{3,2,1,0:T(8,128)}, f32[36,2,8,128]{3,2,1,0:T(8,128)S(1)}, u32[]{:S(2)}, u32[]{:S(2)}) collective-permute-start(f32[36,2,8,128]{3,2,1,0:T(8,128)} %get-tuple-element.8), channel_id=1, source_target_pairs={{0,8},{1,9},{2,10},{3,11},{4,12},{5,13},{6,14},{7,15},{8,16},{9,17... | collective-permute-start | bytes 884744 | tf_op jit(solution)/shard_map/ppermute | solution.py:617
  5.5 6.9 %collective-permute-start.1 = (f32[36,2,8,128]{3,2,1,0:T(8,128)}, f32[36,2,8,128]{3,2,1,0:T(8,128)S(1)}, u32[]{:S(2)}, u32[]{:S(2)}) collective-permute-start(f32[36,2,8,128]{3,2,1,0:T(8,128)} %get-tuple-element.9), channel_id=1, source_target_pairs={{8,0},{9,1},{10,2},{11,3},{12,4},{13,5},{14,6},{15,7},{16,8},{17,9... | collective-permute-start | bytes 884744 | tf_op jit(solution)/shard_map/ppermute | solution.py:617
  6.8 17.2 %collective-permute-start.2 = (f32[36,2,8,128]{3,2,1,0:T(8,128)}, f32[36,2,8,128]{3,2,1,0:T(8,128)S(1)}, u32[]{:S(2)}, u32[]{:S(2)}) collective-permute-start(f32[36,2,8,128]{3,2,1,0:T(8,128)} %get-tuple-element.10.own_hi), channel_id=1, source_target_pairs={{0,1},{1,2},{2,3},{3,4},{4,5},{5,6},{6,7},{8,9},{9,10},{10,11},{11... | collective-permute-start | bytes 884744 | tf_op jit(solution)/shard_map/ppermute | solution.py:617
  11.1 13.0 %collective-permute-start.3 = (f32[36,2,8,128]{3,2,1,0:T(8,128)}, f32[36,2,8,128]{3,2,1,0:T(8,128)S(1)}, u32[]{:S(2)}, u32[]{:S(2)}) collective-permute-start(f32[36,2,8,128]{3,2,1,0:T(8,128)} %get-tuple-element.11.own_lo), channel_id=1, source_target_pairs={{1,0},{2,1},{3,2},{4,3},{5,4},{6,5},{7,6},{9,8},{10,9},{11,10},{12... | collective-permute-start | bytes 884744 | tf_op jit(solution)/shard_map/ppermute | solution.py:617
  12.4 0.7 copy-start.1
  13.1 0.7 copy-start.2
  15.6 8.8 %collective-permute-start.4 = (f32[72,128]{1,0:T(8,128)}, f32[72,128]{1,0:T(8,128)S(1)}, u32[]{:S(2)}, u32[]{:S(2)}) collective-permute-start(f32[72,128]{1,0:T(8,128)} %get-tuple-element.12), channel_id=1, source_target_pairs={{0,1},{1,2},{2,3},{3,4},{4,5},{5,6},{6,7},{8,9},{9,10},{10,11},{11... | collective-permute-start | bytes 110600 | tf_op jit(solution)/shard_map/ppermute | solution.py:617
  20.2 6.5 %collective-permute-start.5 = (f32[72,128]{1,0:T(8,128)}, f32[72,128]{1,0:T(8,128)S(1)}, u32[]{:S(2)}, u32[]{:S(2)}) collective-permute-start(f32[72,128]{1,0:T(8,128)} %get-tuple-element.13), channel_id=1, source_target_pairs={{1,0},{2,1},{3,2},{4,3},{5,4},{6,5},{7,6},{9,8},{10,9},{11,10},{12... | collective-permute-start | bytes 110600 | tf_op jit(solution)/shard_map/ppermute | solution.py:617
  24.1 2.6 %copy-start.18 = (f32[36,2,8,128]{3,2,1,0:T(8,128)}, f32[36,2,8,128]{3,2,1,0:T(8,128)S(1)}, u32[]{:S(2)}) copy-start(f32[36,2,8,128]{3,2,1,0:T(8,128)S(1)} %collective-permute-done.2.ylo) | copy-start | bytes 884740
  24.1 2.6 %copy-start.19 = (f32[36,2,8,128]{3,2,1,0:T(8,128)}, f32[36,2,8,128]{3,2,1,0:T(8,128)S(1)}, u32[]{:S(2)}) copy-start(f32[36,2,8,128]{3,2,1,0:T(8,128)S(1)} %collective-permute-done.3.yhi) | copy-start | bytes 884740
  24.4 2.3 %copy-start.20 = (f32[72,128]{1,0:T(8,128)}, f32[72,128]{1,0:T(8,128)S(1)}, u32[]{:S(2)}) copy-start(f32[72,128]{1,0:T(8,128)S(1)} %collective-permute-done.4.edge_lo) | copy-start | bytes 110596
  26.7 0.6 copy-start.21
  34.8 7.6 %collective-permute-start.6 = (f32[1,296,128]{2,1,0:T(8,128)}, f32[1,296,128]{2,1,0:T(8,128)S(1)}, u32[]{:S(2)}, u32[]{:S(2)}) collective-permute-start(f32[1,296,128]{2,1,0:T(8,128)} %bitcast.10), channel_id=1, source_target_pairs={{0,1},{1,0},{2,3},{3,2},{4,5},{5,4},{6,7},{7,6},{8,9},{9,8},{10,11... | collective-permute-start | bytes 454664 | tf_op jit(solution)/shard_map/ppermute | solution.py:551
  37.7 9.5 %collective-permute-start.13 = (f32[1,296,128]{2,1,0:T(8,128)}, f32[1,296,128]{2,1,0:T(8,128)S(1)}, u32[]{:S(2)}, u32[]{:S(2)}) collective-permute-start(f32[1,296,128]{2,1,0:T(8,128)} %bitcast.11), channel_id=1, source_target_pairs={{0,6},{1,7},{2,4},{3,5},{4,2},{5,3},{6,0},{7,1},{8,14},{9,15},{10,... | collective-permute-start | bytes 454664 | tf_op jit(solution)/shard_map/ppermute | solution.py:551
  40.2 9.7 %collective-permute-start.7 = (f32[1,296,128]{2,1,0:T(8,128)}, f32[1,296,128]{2,1,0:T(8,128)S(1)}, u32[]{:S(2)}, u32[]{:S(2)}) collective-permute-start(f32[1,296,128]{2,1,0:T(8,128)} %bitcast.12), channel_id=1, source_target_pairs={{0,2},{1,3},{2,0},{3,1},{4,6},{5,7},{6,4},{7,5},{8,10},{9,11},{10,... | collective-permute-start | bytes 454664 | tf_op jit(solution)/shard_map/ppermute | solution.py:551
  40.9 13.8 %collective-permute-start.11 = (f32[1,296,128]{2,1,0:T(8,128)}, f32[1,296,128]{2,1,0:T(8,128)S(1)}, u32[]{:S(2)}, u32[]{:S(2)}) collective-permute-start(f32[1,296,128]{2,1,0:T(8,128)} %bitcast.13), channel_id=1, source_target_pairs={{0,4},{1,5},{2,6},{3,7},{4,0},{5,1},{6,2},{7,3},{8,12},{9,13},{10,... | collective-permute-start | bytes 454664 | tf_op jit(solution)/shard_map/ppermute | solution.py:551
  43.4 32.9 %copy-start = (f32[2,296,128]{2,1,0:T(8,128)}, f32[2,296,128]{2,1,0:T(8,128)S(1)}, u32[]{:S(2)}) copy-start(f32[2,296,128]{2,1,0:T(8,128)S(1)} %pad_maximum_fusion.refs_0_) | copy-start | bytes 909316
  43.4 18.2 %collective-permute-start.17 = (f32[2,296,128]{2,1,0:T(8,128)S(1)}, f32[2,296,128]{2,1,0:T(8,128)S(1)}, u32[]{:S(2)}, u32[]{:S(2)}) collective-permute-start(f32[2,296,128]{2,1,0:T(8,128)S(1)} %pad_maximum_fusion.refs_0_), channel_id=1, source_target_pairs={{0,8},{1,9},{2,10},{3,11},{4,12},{5,13},{6,14},{7,15},{8,0},{9,1},... | collective-permute-start | bytes 909320 | tf_op jit(solution)/shard_map/ppermute | solution.py:551
  43.5 19.9 %collective-permute-start.9 = (f32[2,296,128]{2,1,0:T(8,128)S(1)}, f32[2,296,128]{2,1,0:T(8,128)S(1)}, u32[]{:S(2)}, u32[]{:S(2)}) collective-permute-start(f32[2,296,128]{2,1,0:T(8,128)S(1)} %pad_maximum_fusion.refs_0_), channel_id=1, source_target_pairs={{0,16},{1,17},{2,18},{3,19},{4,20},{5,21},{6,22},{7,23},{8,24},{9,... | collective-permute-start | bytes 909320 | tf_op jit(solution)/shard_map/ppermute | solution.py:551
  47.3 11.3 %collective-permute-start.14 = (f32[1,296,128]{2,1,0:T(8,128)S(1)}, f32[1,296,128]{2,1,0:T(8,128)S(1)}, u32[]{:S(2)}, u32[]{:S(2)}) collective-permute-start(f32[1,296,128]{2,1,0:T(8,128)S(1)} %collective-permute-done.13), channel_id=1, source_target_pairs={{0,16},{1,17},{2,18},{3,19},{4,20},{5,21},{6,22},{7,23},{8,24},{9,... | collective-permute-start | bytes 454664 | tf_op jit(solution)/shard_map/ppermute | solution.py:551
  49.9 11.6 %collective-permute-start.8 = (f32[1,296,128]{2,1,0:T(8,128)S(1)}, f32[1,296,128]{2,1,0:T(8,128)S(1)}, u32[]{:S(2)}, u32[]{:S(2)}) collective-permute-start(f32[1,296,128]{2,1,0:T(8,128)S(1)} %collective-permute-done.7), channel_id=1, source_target_pairs={{0,16},{1,17},{2,18},{3,19},{4,20},{5,21},{6,22},{7,23},{8,24},{9,... | collective-permute-start | bytes 454664 | tf_op jit(solution)/shard_map/ppermute | solution.py:551
  54.7 5.2 %collective-permute-start.12 = (f32[1,296,128]{2,1,0:T(8,128)S(1)}, f32[1,296,128]{2,1,0:T(8,128)S(1)}, u32[]{:S(2)}, u32[]{:S(2)}) collective-permute-start(f32[1,296,128]{2,1,0:T(8,128)S(1)} %collective-permute-done.11), channel_id=1, source_target_pairs={{0,1},{1,0},{2,3},{3,2},{4,5},{5,4},{6,7},{7,6},{8,9},{9,8},{10,11... | collective-permute-start | bytes 454664 | tf_op jit(solution)/shard_map/ppermute | solution.py:551
  58.6 17.8 %copy-start.5 = (f32[2,296,128]{2,1,0:T(8,128)}, f32[2,296,128]{2,1,0:T(8,128)S(1)}, u32[]{:S(2)}) copy-start(f32[2,296,128]{2,1,0:T(8,128)S(1)} %constant_dynamic-update-slice_fusion.4.refs_5_) | copy-start | bytes 909316
  58.6 5.8 %collective-permute-start.22 = (f32[2,296,128]{2,1,0:T(8,128)S(1)}, f32[2,296,128]{2,1,0:T(8,128)S(1)}, u32[]{:S(2)}, u32[]{:S(2)}) collective-permute-start(f32[2,296,128]{2,1,0:T(8,128)S(1)} %constant_dynamic-update-slice_fusion.4.refs_5_), channel_id=1, source_target_pairs={{0,8},{1,9},{2,10},{3,11},{4,12},{5,13},{6,14},{7,15},{8,0},{9,1},... | collective-permute-start | bytes 909320 | tf_op jit(solution)/shard_map/ppermute | solution.py:551
  59.9 10.1 %collective-permute-start.16 = (f32[2,296,128]{2,1,0:T(8,128)S(1)}, f32[2,296,128]{2,1,0:T(8,128)S(1)}, u32[]{:S(2)}, u32[]{:S(2)}) collective-permute-start(f32[2,296,128]{2,1,0:T(8,128)S(1)} %constant_dynamic-update-slice_fusion.4.refs_5_), channel_id=1, source_target_pairs={{0,1},{1,0},{2,3},{3,2},{4,5},{5,4},{6,7},{7,6},{8,9},{9,8},{10,11... | collective-permute-start | bytes 909320 | tf_op jit(solution)/shard_map/ppermute | solution.py:551
  60.5 15.9 %copy-start.4 = (f32[2,296,128]{2,1,0:T(8,128)}, f32[2,296,128]{2,1,0:T(8,128)S(1)}, u32[]{:S(2)}) copy-start(f32[2,296,128]{2,1,0:T(8,128)S(1)} %constant_dynamic-update-slice_fusion.2.refs_4_) | copy-start | bytes 909316
  61.5 8.5 %collective-permute-start.21 = (f32[2,296,128]{2,1,0:T(8,128)S(1)}, f32[2,296,128]{2,1,0:T(8,128)S(1)}, u32[]{:S(2)}, u32[]{:S(2)}) collective-permute-start(f32[2,296,128]{2,1,0:T(8,128)S(1)} %constant_dynamic-update-slice_fusion.2.refs_4_), channel_id=1, source_target_pairs={{0,8},{1,9},{2,10},{3,11},{4,12},{5,13},{6,14},{7,15},{8,0},{9,1},... | collective-permute-start | bytes 909320 | tf_op jit(solution)/shard_map/ppermute | solution.py:551
  61.5 14.8 %copy-start.3 = (f32[2,296,128]{2,1,0:T(8,128)}, f32[2,296,128]{2,1,0:T(8,128)S(1)}, u32[]{:S(2)}) copy-start(f32[2,296,128]{2,1,0:T(8,128)S(1)} %constant_dynamic-update-slice_fusion.refs_1_) | copy-start | bytes 909316
  61.6 14.8 %copy-start.6 = (f32[2,296,128]{2,1,0:T(8,128)}, f32[2,296,128]{2,1,0:T(8,128)S(1)}, u32[]{:S(2)}) copy-start(f32[2,296,128]{2,1,0:T(8,128)S(1)} %collective-permute-done.17.refs_8_) | copy-start | bytes 909316
  61.6 9.7 %collective-permute-start.15 = (f32[2,296,128]{2,1,0:T(8,128)S(1)}, f32[2,296,128]{2,1,0:T(8,128)S(1)}, u32[]{:S(2)}, u32[]{:S(2)}) collective-permute-start(f32[2,296,128]{2,1,0:T(8,128)S(1)} %constant_dynamic-update-slice_fusion.2.refs_4_), channel_id=1, source_target_pairs={{0,16},{1,17},{2,18},{3,19},{4,20},{5,21},{6,22},{7,23},{8,24},{9,... | collective-permute-start | bytes 909320 | tf_op jit(solution)/shard_map/ppermute | solution.py:551
  63.4 13.0 %copy-start.7 = (f32[2,296,128]{2,1,0:T(8,128)}, f32[2,296,128]{2,1,0:T(8,128)S(1)}, u32[]{:S(2)}) copy-start(f32[2,296,128]{2,1,0:T(8,128)S(1)} %collective-permute-done.9.refs_2_) | copy-start | bytes 909316
  63.4 11.3 %collective-permute-start.10 = (f32[2,296,128]{2,1,0:T(8,128)S(1)}, f32[2,296,128]{2,1,0:T(8,128)S(1)}, u32[]{:S(2)}, u32[]{:S(2)}) collective-permute-start(f32[2,296,128]{2,1,0:T(8,128)S(1)} %constant_dynamic-update-slice_fusion.refs_1_), channel_id=1, source_target_pairs={{0,1},{1,0},{2,3},{3,2},{4,5},{5,4},{6,7},{7,6},{8,9},{9,8},{10,11... | collective-permute-start | bytes 909320 | tf_op jit(solution)/shard_map/ppermute | solution.py:551
  64.4 12.0 %copy-start.8 = (f32[2,296,128]{2,1,0:T(8,128)}, f32[2,296,128]{2,1,0:T(8,128)S(1)}, u32[]{:S(2)}) copy-start(f32[2,296,128]{2,1,0:T(8,128)S(1)} %collective-permute-done.22.refs_13_) | copy-start | bytes 909316
  64.4 10.3 %collective-permute-start.18 = (f32[2,296,128]{2,1,0:T(8,128)S(1)}, f32[2,296,128]{2,1,0:T(8,128)S(1)}, u32[]{:S(2)}, u32[]{:S(2)}) collective-permute-start(f32[2,296,128]{2,1,0:T(8,128)S(1)} %constant_dynamic-update-slice_fusion.refs_1_), channel_id=1, source_target_pairs={{0,8},{1,9},{2,10},{3,11},{4,12},{5,13},{6,14},{7,15},{8,0},{9,1},... | collective-permute-start | bytes 909320 | tf_op jit(solution)/shard_map/ppermute | solution.py:551
  70.0 6.4 %copy-start.9 = (f32[2,296,128]{2,1,0:T(8,128)}, f32[2,296,128]{2,1,0:T(8,128)S(1)}, u32[]{:S(2)}) copy-start(f32[2,296,128]{2,1,0:T(8,128)S(1)} %collective-permute-done.16.refs_7_) | copy-start | bytes 909316
  70.0 4.8 %collective-permute-start.19 = (f32[2,296,128]{2,1,0:T(8,128)S(1)}, f32[2,296,128]{2,1,0:T(8,128)S(1)}, u32[]{:S(2)}, u32[]{:S(2)}) collective-permute-start(f32[2,296,128]{2,1,0:T(8,128)S(1)} %collective-permute-done.9.refs_2_), channel_id=1, source_target_pairs={{0,8},{1,9},{2,10},{3,11},{4,12},{5,13},{6,14},{7,15},{8,0},{9,1},... | collective-permute-start | bytes 909320 | tf_op jit(solution)/shard_map/ppermute | solution.py:551
  70.0 6.4 %copy-start.10 = (f32[2,296,128]{2,1,0:T(8,128)}, f32[2,296,128]{2,1,0:T(8,128)S(1)}, u32[]{:S(2)}) copy-start(f32[2,296,128]{2,1,0:T(8,128)S(1)} %collective-permute-done.21.refs_12_) | copy-start | bytes 909316
  70.0 4.8 %collective-permute-start.24 = (f32[2,296,128]{2,1,0:T(8,128)S(1)}, f32[2,296,128]{2,1,0:T(8,128)S(1)}, u32[]{:S(2)}, u32[]{:S(2)}) collective-permute-start(f32[2,296,128]{2,1,0:T(8,128)S(1)} %collective-permute-done.16.refs_7_), channel_id=1, source_target_pairs={{0,8},{1,9},{2,10},{3,11},{4,12},{5,13},{6,14},{7,15},{8,0},{9,1},... | collective-permute-start | bytes 909320 | tf_op jit(solution)/shard_map/ppermute | solution.py:551
  71.3 5.1 %copy-start.11 = (f32[2,296,128]{2,1,0:T(8,128)}, f32[2,296,128]{2,1,0:T(8,128)S(1)}, u32[]{:S(2)}) copy-start(f32[2,296,128]{2,1,0:T(8,128)S(1)} %collective-permute-done.15.refs_6_) | copy-start | bytes 909316
  71.3 3.5 %collective-permute-start.23 = (f32[2,296,128]{2,1,0:T(8,128)S(1)}, f32[2,296,128]{2,1,0:T(8,128)S(1)}, u32[]{:S(2)}, u32[]{:S(2)}) collective-permute-start(f32[2,296,128]{2,1,0:T(8,128)S(1)} %collective-permute-done.15.refs_6_), channel_id=1, source_target_pairs={{0,8},{1,9},{2,10},{3,11},{4,12},{5,13},{6,14},{7,15},{8,0},{9,1},... | collective-permute-start | bytes 909320 | tf_op jit(solution)/shard_map/ppermute | solution.py:551
  74.7 1.7 copy-start.12
  74.7 1.6 collective-permute-start.20
  74.7 1.7 copy-start.13
  74.8 1.7 copy-start.14
  74.8 1.7 copy-start.15
  74.8 1.6 copy-start.16
  76.3 0.7 copy-start.17

commit v3 on v2

--- a/solution.py
+++ b/solution.py
@@ -270,7 +270,7 @@
     return cov * pl.reciprocal(dist, approx=True)
 
 
-def eliminate(a):
+def eliminate(a, beside):
     groups = len(a)
     sub = lax.broadcasted_iota(jnp.int32, (8, LANES), 0)
     lane = lax.broadcasted_iota(jnp.int32, (8, LANES), 1)
@@ -288,8 +288,11 @@
         col = [across(a[gk], k0 + j) for j in range(8)]
         u = [[down(col[j], i) if i >= j else None for i in range(8)] for j in range(8)]
         inv = []
+        todo = beside(gk)
         for j in range(8):
             inv.append(pl.reciprocal(u[j][j], approx=True))
+            for piece in todo[j * len(todo) // 8 : (j + 1) * len(todo) // 8]:
+                piece()
             for i in range(j + 1, 8):
                 f = u[j][i] * inv[j]
                 for k in range(i, 8):
@@ -328,8 +331,8 @@
 
 
 def head_stage(
-    place_ref, pieces, patterns, parts, cols_out, head_out, down_out, linv_out, fcols_out, obs_head, full, work,
-    count_vec, count_smem, sem,
+    place_ref, pieces, patterns, parts, cols_out, head_out, down_out, linv_a, linv_b, fcols_out, obs_head, full,
+    work, count_vec, count_smem, sem, lefts, rows_cross, cols_cross, obs_down,
 ):
     col_chunks = cols_out.shape[1] // LANES
     members_n = ROWS - 8
@@ -414,6 +417,16 @@
     rid = lax.broadcasted_iota(jnp.int32, (HEAD, HEAD), 0)
     cid = lax.broadcasted_iota(jnp.int32, (HEAD, HEAD), 1)
     same = rid == cid
+    noise = jnp.sum(jnp.where(same, obs_head[...], 0.0), axis=1, keepdims=True)
+    obs_down[...] = jnp.broadcast_to(noise, obs_down.shape)
+    span = lefts.shape[0]
+    col_span = cols_out.shape[1]
+    some = span // (PANELS * 16)
+    per_chunk = LANES // some
+    row_iota = lax.broadcasted_iota(jnp.int32, (16, HEAD), 0)
+    head_iota = lax.broadcasted_iota(jnp.int32, (16, HEAD), 1)
+    down_iota = lax.broadcasted_iota(jnp.int32, (8, HEAD), 0)
+    col_iota = lax.broadcasted_iota(jnp.int32, (8, HEAD), 1)
     work[:HEAD, :HEAD] = taper_cov(down, head, members_n) + jnp.where(same, obs_head[...], 0.0)
     work[:HEAD, HEAD:] = jnp.where(same, 1.0, 0.0).astype(F32)
 
@@ -426,7 +439,34 @@
                     work[HEAD + 8 * g : HEAD + 8 * g + 8, :PANEL] = work[
                         q * PANEL + 8 * g : q * PANEL + 8 * g + 8, q * PANEL : (q + 1) * PANEL
                     ]
-        inverse = eliminate([work[HEAD + 8 * g : HEAD + 8 * g + 8, :PANEL] for g in range(16)])
+        def beside(g):
+            part = p * 16 + g
+            if g % per_chunk == 0:
+                c = lax.div(part, per_chunk)
+                lefts[pl.ds(pl.multiple_of(c * LANES, LANES), LANES), :] = turned(
+                    full[grp * (span // LANES) + c]
+                )
+            def some_rows(r):
+                at = pl.multiple_of(part * some + r, 16)
+                cross = taper_cov(lefts[pl.ds(at, 16), :], head_out[...], members_n)
+                same = row_iota + (grp * span + at) == head_iota
+                hi, lo = split(cross + jnp.where(same, obs_head[...], 0.0))
+                rows_cross[pl.ds(at, 16), :HEAD] = hi
+                rows_cross[pl.ds(at, 16), HEAD:] = lo
+
+            def some_lanes(c):
+                at = pl.multiple_of(part * 8, 8)
+                cross = taper_cov(down_out[pl.ds(at, 8), :], cols_out[:, c : c + HEAD], members_n)
+                same = down_iota + at == col_iota + (tile * col_span + c)
+                cols_cross[pl.ds(at, 8), c : c + HEAD] = cross + jnp.where(
+                    same, obs_down[pl.ds(at, 8), :1], 0.0
+                )
+
+            return [functools.partial(some_rows, r) for r in range(0, some, 16)] + [
+                functools.partial(some_lanes, c) for c in range(0, col_span, HEAD)
+            ]
+
+        inverse = eliminate([work[HEAD + 8 * g : HEAD + 8 * g + 8, :PANEL] for g in range(16)], beside)
         wide = pl.ds(at, HEAD + PANEL)
         done = jnp.dot(inverse, work[pl.ds(at, PANEL), wide], precision=HIGH, preferred_element_type=F32)
         work[pl.ds(at, PANEL), wide] = done
@@ -442,41 +482,40 @@
         return carry
 
     lax.fori_loop(0, PANELS, panel, 0)
-    linv = work[:HEAD, HEAD:]
-    hi, lo = split(linv)
-    linv_out[:, :HEAD] = hi
-    linv_out[:, HEAD : 2 * HEAD] = hi
-    linv_out[:, 2 * HEAD :] = lo
-    left = jnp.concatenate([hi, lo, hi], 1)
-    width = 256
-    pr = lax.broadcasted_iota(jnp.int32, (HEAD, width), 0)
-    pc = lax.broadcasted_iota(jnp.int32, (HEAD, width), 1)
+    half = HEAD // 2
+    for out, rows, depth in ((linv_a, slice(0, half), half), (linv_b, slice(half, HEAD), HEAD)):
+        hi, lo = split(work[rows, HEAD : HEAD + depth])
+        out[:, :depth] = hi
+        out[:, depth : 2 * depth] = hi
+        out[:, 2 * depth :] = lo
+    width = min(512, col_span)
+    pr = lax.broadcasted_iota(jnp.int32, (half, width), 0)
+    pc = lax.broadcasted_iota(jnp.int32, (half, width), 1)
 
     def some_cols(c, carry):
         at = pl.multiple_of(c * width, width)
-        first = tile * col_chunks * LANES + c * width
-        right = cols_out[:, pl.ds(at, width)]
-        ids = pc + first
-        cross = taper_cov(down, right, members_n)
-        cross = cross + jnp.where(pr == ids, carry, 0.0)
-        hi, lo = split(cross)
-        f = jnp.dot(left, jnp.concatenate([hi, hi, lo], 0), preferred_element_type=F32)
-        f = jnp.where(ids >= lax.div(pr, PANEL) * PANEL, f, 0.0)
-        hi, lo = split(f)
-        fcols_out[:HEAD, pl.ds(at, width)] = hi
-        fcols_out[HEAD : 2 * HEAD, pl.ds(at, width)] = lo
-        fcols_out[2 * HEAD :, pl.ds(at, width)] = hi
+        hi, lo = split(cols_cross[:, pl.ds(at, width)])
+        for out, first, depth in ((linv_a, 0, half), (linv_b, half, HEAD)):
+            f = jnp.dot(
+                out[...], jnp.concatenate([hi[:depth], lo[:depth], hi[:depth]], 0), preferred_element_type=F32
+            )
+            ids = pc + (tile * col_span + c * width)
+            f = jnp.where(ids >= lax.div(pr + first, PANEL) * PANEL, f, 0.0)
+            f_hi, f_lo = split(f)
+            fcols_out[first : first + half, pl.ds(at, width)] = f_hi
+            fcols_out[HEAD + first : HEAD + first + half, pl.ds(at, width)] = f_lo
+            fcols_out[2 * HEAD + first : 2 * HEAD + first + half, pl.ds(at, width)] = f_hi
         return carry
 
-    noise_down = jnp.sum(jnp.where(same, obs_head[...], 0.0), axis=1, keepdims=True)
-    lax.fori_loop(0, cols_out.shape[1] // width, some_cols, jnp.broadcast_to(noise_down, (HEAD, width)))
+    lax.fori_loop(0, col_span // width, some_cols, 0, unroll=True)
 
 
 def final_kernel(place_ref, *refs, patterns, parts):
     pieces = refs[: len(patterns)]
     obs, trailing, factor = refs[len(patterns) : len(patterns) + 3]
     (
-        cols, head, down, linv, fcols, obs_head, full, work, count_vec, count_smem, sem, keep, lefts, factors,
+        cols, head, down, linv_a, linv_b, fcols, obs_head, full, work, count_vec, count_smem, sem, keep, lefts,
+        rows_cross, cols_cross, obs_down, factors,
     ) = refs[len(patterns) + 3 :]
     members_n = ROWS - 8
     step = pl.program_id(0)
@@ -485,45 +524,59 @@
     steps = pl.num_programs(0)
     first_row = (grp * steps + step) * height
     first_col = tile * col_span
-    chunks = height // LANES
+    share = factor.shape[0]
+    half = HEAD // 2
 
     def prepare(at, slot):
         first = (grp * steps + at) * height
-        left = jnp.concatenate([turned(full[lax.div(first, LANES) + c]) for c in range(chunks)], 0)
-        lefts[slot] = left
-        rid = lax.broadcasted_iota(jnp.int32, (height, HEAD), 0) + first
-        cid = lax.broadcasted_iota(jnp.int32, (height, HEAD), 1)
-        cross = taper_cov(left, head[...], members_n) + jnp.where(rid == cid, obs_head[...], 0.0)
-        hi, lo = split(cross)
-        f = lax.dot_general(
-            jnp.concatenate([hi, lo, hi], 1), linv[...], (((1,), (1,)), ((), ())),
-            preferred_element_type=F32,
-        )
-        f = jnp.where(rid >= lax.div(cid, PANEL) * PANEL, f, 0.0)
-        keep[pl.ds(pl.multiple_of(at * height, height), height), :] = f
-        hi, lo = split(f)
-        factors[slot, :, :HEAD] = hi
-        factors[slot, :, HEAD : 2 * HEAD] = hi
-        factors[slot, :, 2 * HEAD :] = lo
+        here = pl.ds(pl.multiple_of(at * height, height), height)
+        rid = lax.broadcasted_iota(jnp.int32, (height, half), 0) + first
+        cid = lax.broadcasted_iota(jnp.int32, (height, half), 1)
+        for linv, begin, depth in ((linv_a, 0, half), (linv_b, half, HEAD)):
+            hi, lo = rows_cross[here, :depth], rows_cross[here, HEAD : HEAD + depth]
+            f = lax.dot_general(
+                jnp.concatenate([hi, lo, hi], 1), linv[...], (((1,), (1,)), ((), ())),
+                preferred_element_type=F32,
+            )
+            f = jnp.where(rid >= lax.div(cid + begin, PANEL) * PANEL, f, 0.0)
+            keep[:, begin : begin + half] = f
+            hi, lo = split(f)
+            factors[slot, :, begin : begin + half] = hi
+            factors[slot, :, HEAD + begin : HEAD + begin + half] = hi
+            factors[slot, :, 2 * HEAD + begin : 2 * HEAD + begin + half] = lo
+
+    def share_out(at):
+        start = at * height - tile * share
+        if share >= height:
+            @pl.when((start >= 0) & (start < share))
+            def _():
+                factor[pl.ds(pl.multiple_of(start, height), height), :] = keep[...]
+        else:
+            @pl.when((start <= 0) & (start > -height))
+            def _():
+                factor[...] = keep[pl.ds(pl.multiple_of(-start, share), share), :]
 
     @pl.when(step == 0)
     def _():
         head_stage(
-            place_ref, pieces, patterns, parts, cols, head, down, linv, fcols, obs_head, full, work,
-            count_vec, count_smem, sem,
+            place_ref, pieces, patterns, parts, cols, head, down, linv_a, linv_b, fcols, obs_head, full, work,
+            count_vec, count_smem, sem, lefts, rows_cross, cols_cross, obs_down,
         )
         prepare(0, 0)
+        share_out(0)
 
     slot = lax.rem(step, 2)
-    left = lefts[slot]
+    left = lefts[pl.ds(pl.multiple_of(step * height, height), height), :]
     f3 = factors[slot]
-    prepare(jnp.minimum(step + 1, steps - 1), 1 - slot)
+    following = jnp.minimum(step + 1, steps - 1)
     width = min(512, col_span)
     for c in range(0, col_span, width):
         value = taper_cov(left, cols[:, c : c + width], members_n)
         trailing[:, c : c + width] = value - jnp.dot(
             f3, fcols[:, c : c + width], preferred_element_type=F32
         )
+
+    prepare(following, 1 - slot)
 
     @pl.when((first_row < first_col + col_span) & (first_col < first_row + height))
     def _():
@@ -534,10 +587,7 @@
                 rid == cid, obs[:, c : c + width], 0.0
             )
 
-    @pl.when(step == steps - 1)
-    def _():
-        share = factor.shape[0]
-        factor[...] = keep[pl.ds(pl.multiple_of(tile * share, share), share), :]
+    share_out(following)
 
 
 def gather(unit, grp_size, tile_size):
@@ -665,7 +715,8 @@
             pltpu.VMEM((ROWS, col_span), F32),
             pltpu.VMEM((ROWS, HEAD), F32),
             pltpu.VMEM((HEAD, LANES), F32),
-            pltpu.VMEM((HEAD, 3 * HEAD), BF16),
+            pltpu.VMEM((HEAD // 2, 3 * HEAD // 2), BF16),
+            pltpu.VMEM((HEAD // 2, 3 * HEAD), BF16),
             pltpu.VMEM((3 * HEAD, col_span), BF16),
             pltpu.VMEM((1, HEAD), F32),
             pltpu.VMEM((NS // LANES + parts + 2, ROWS, LANES), F32),
@@ -673,8 +724,11 @@
             pltpu.VMEM((2 * count_rows, LANES), jnp.int32),
             pltpu.SMEM((2 * count_rows, LANES), jnp.int32),
             pltpu.SemaphoreType.DMA,
-            pltpu.VMEM((row_span, HEAD), F32),
-            pltpu.VMEM((2, height, LANES), F32),
+            pltpu.VMEM((height, HEAD), F32),
+            pltpu.VMEM((row_span, LANES), F32),
+            pltpu.VMEM((row_span, 2 * HEAD), BF16),
+            pltpu.VMEM((HEAD, col_span), F32),
+            pltpu.VMEM((HEAD, LANES), F32),
             pltpu.VMEM((2, height, 3 * HEAD), BF16),
         ],
         compiler_params=pltpu.CompilerParams(vmem_limit_bytes=VMEM_LIMIT),

time: 171 us -> 162 us (0.947)
  Pallas kernels: 105 us -> 96 us
    pallas_call x1, Pallas kernels: 93 us -> 84.1 us  [per_device(): pl.pallas_call(functools.partial(final_kernel, patterns=patterns, parts=p...]
where the time goes in v3:
time: 162 us; the launch traced here: 161 us
  Pallas kernels  96 us (59%)
  starting transfers between devices  34.2 us (21%)
  waiting for transfers between devices  23.7 us (15%)
  local copies, waits for them, and re-layouts  4.11 us (3%)
  between operations  1.82 us (1%)
    pallas_call x1, Pallas kernels, per_device(): pl.pallas_call(functools.partial(final_kernel, patterns=patterns, parts=p...  84.1 us
    ppermute x19, waiting for transfers between devices, swap(): lax.ppermute(value, ('grp', 'tile'), pairs)  21.1 us
    ppermute x19, starting transfers between devices, swap(): lax.ppermute(value, ('grp', 'tile'), pairs)  19.2 us
    ppermute x6, starting transfers between devices, move(): return lax.ppermute(value, ('grp', 'tile'), pairs)  15 us
    pallas_call x1, Pallas kernels, per_device(): pl.pallas_call(forecast_kernel, out_shape=jax.ShapeDtypeStruct((-(-(membe...  7.53 us
  transfers between devices with their start and end apart: 25, of which 12 were waited for; matrix products, arithmetic and copies ran while one was open for 2% of the time, Pallas kernels for 1%

profile of v3, /device:TPU:0, one launch (start us, length us, event | category | flops | bytes accessed | tf_op | source)
XLA Modules:
  0.0 161.3 jit_solution(9858753766932017333)
XLA Ops:
  0.6 2.6 %cut.1 = (f32[36,2,8,128]{3,2,1,0:T(8,128)}, f32[36,2,8,128]{3,2,1,0:T(8,128)}, f32[36,2,8,128]{3,2,1,0:T(8,128)}, f32[36,2,8,128]{3,2,1,0:T(8,128)}) custom-call(f32[32,64,128]{2,1,0:T(8,128)} %bitcast.9, f32[3,64,128]{2,1,0:T(8,128)} %bitcast.15, f32[64,128]{1,0:T(8,128)} %bitcast.16, f32[64,128]{1,0:T(8,128)} %bitcast.17), custom_call_target="tpu_custom_call" | custom-call | tf_op jit(solution)/shard_map/cut/pallas_call | solution.py:649
  3.2 2.4 %collective-permute-start = (f32[36,2,8,128]{3,2,1,0:T(8,128)}, f32[36,2,8,128]{3,2,1,0:T(8,128)S(1)}, u32[]{:S(2)}, u32[]{:S(2)}) collective-permute-start(f32[36,2,8,128]{3,2,1,0:T(8,128)} %get-tuple-element.8), channel_id=1, source_target_pairs={{0,8},{1,9},{2,10},{3,11},{4,12},{5,13},{6,14},{7,15},{8,16},{9,17... | collective-permute-start | bytes 884744 | tf_op jit(solution)/shard_map/ppermute | solution.py:667
  5.5 1.3 collective-permute-start.1
  6.8 4.2 %collective-permute-start.2 = (f32[36,2,8,128]{3,2,1,0:T(8,128)}, f32[36,2,8,128]{3,2,1,0:T(8,128)S(1)}, u32[]{:S(2)}, u32[]{:S(2)}) collective-permute-start(f32[36,2,8,128]{3,2,1,0:T(8,128)} %get-tuple-element.10.own_hi), channel_id=1, source_target_pairs={{0,1},{1,2},{2,3},{3,4},{4,5},{5,6},{6,7},{8,9},{9,10},{10,11},{11... | collective-permute-start | bytes 884744 | tf_op jit(solution)/shard_map/ppermute | solution.py:667
  11.1 1.3 collective-permute-start.3
  12.4 0.0 collective-permute-done.xlo
  12.4 0.0 copy-start.1
  12.4 0.7 copy-done.1
  13.1 0.7 copy-done.2
  13.8 1.8 %edges.1 = (f32[72,128]{1,0:T(8,128)}, f32[72,128]{1,0:T(8,128)}) custom-call(f32[36,2,8,128]{3,2,1,0:T(8,128)} %copy-done.1, f32[36,2,8,128]{3,2,1,0:T(8,128)} %copy-done.2), custom_call_target="tpu_custom_call" | custom-call | tf_op jit(solution)/shard_map/edges/pallas_call | solution.py:672
  15.6 4.5 %collective-permute-start.4 = (f32[72,128]{1,0:T(8,128)}, f32[72,128]{1,0:T(8,128)S(1)}, u32[]{:S(2)}, u32[]{:S(2)}) collective-permute-start(f32[72,128]{1,0:T(8,128)} %get-tuple-element.12), channel_id=1, source_target_pairs={{0,1},{1,2},{2,3},{3,4},{4,5},{5,6},{6,7},{8,9},{9,10},{10,11},{11... | collective-permute-start | bytes 110600 | tf_op jit(solution)/shard_map/ppermute | solution.py:667
  20.2 1.3 collective-permute-start.5
  21.5 0.6 pad_add_fusion.place_ref
  22.7 1.4 dynamic_slice.3
  24.1 0.0 collective-permute-done.2.ylo
  24.1 0.0 collective-permute-done.3.yhi
  24.1 0.3 collective-permute-done.4.edge_lo
  24.4 2.3 %collective-permute-done.5.edge_hi = f32[72,128]{1,0:T(8,128)S(1)} collective-permute-done((f32[72,128]{1,0:T(8,128)}, f32[72,128]{1,0:T(8,128)S(1)}, u32[]{:S(2)}, u32[]{:S(2)}) %collective-permute-start.5) | collective-permute-done | bytes 36896 | tf_op jit(solution)/shard_map/ppermute | solution.py:667
  26.7 0.6 copy-done.21
  27.3 7.5 %forecast.1 = f32[296,128]{1,0:T(8,128)} custom-call(s32[4]{0:T(128)} %pad_add_fusion.place_ref, s32[1]{0:T(128)S(6)} %copy.13.count_ref, f32[32,8,8,128]{3,2,1,0:T(8,128)} %mem.1, f32[3,8,8,128]{3,2,1,0:T(8,128)} %cour.1, f32[8,8,128]{2,1,0:T(8,128)} %turb.1, f32[8,8,128]{2,1,0:T(8,128)} %diss.1, f32[36,2,8,128]{3,2,1,0:T(8,128)} %copy-done.1, ...), custom_call_target="tpu_custom_call" | custom-call | tf_op jit(solution)/shard_map/forecast/pallas_call | solution.py:685
  34.8 2.9 %collective-permute-start.6 = (f32[1,296,128]{2,1,0:T(8,128)}, f32[1,296,128]{2,1,0:T(8,128)S(1)}, u32[]{:S(2)}, u32[]{:S(2)}) collective-permute-start(f32[1,296,128]{2,1,0:T(8,128)} %bitcast.10), channel_id=1, source_target_pairs={{0,1},{1,0},{2,3},{3,2},{4,5},{5,4},{6,7},{7,6},{8,9},{9,8},{10,11... | collective-permute-start | bytes 454664 | tf_op jit(solution)/shard_map/ppermute | solution.py:601
  37.7 2.5 %collective-permute-start.13 = (f32[1,296,128]{2,1,0:T(8,128)}, f32[1,296,128]{2,1,0:T(8,128)S(1)}, u32[]{:S(2)}, u32[]{:S(2)}) collective-permute-start(f32[1,296,128]{2,1,0:T(8,128)} %bitcast.11), channel_id=1, source_target_pairs={{0,6},{1,7},{2,4},{3,5},{4,2},{5,3},{6,0},{7,1},{8,14},{9,15},{10,... | collective-permute-start | bytes 454664 | tf_op jit(solution)/shard_map/ppermute | solution.py:601
  40.2 0.7 collective-permute-start.7
  40.9 1.2 collective-permute-start.11
  42.1 0.3 collective-permute-done.6
  42.5 0.9 pad_maximum_fusion.refs_0_
  43.4 0.1 collective-permute-start.17
  43.5 3.8 %collective-permute-start.9 = (f32[2,296,128]{2,1,0:T(8,128)S(1)}, f32[2,296,128]{2,1,0:T(8,128)S(1)}, u32[]{:S(2)}, u32[]{:S(2)}) collective-permute-start(f32[2,296,128]{2,1,0:T(8,128)S(1)} %pad_maximum_fusion.refs_0_), channel_id=1, source_target_pairs={{0,16},{1,17},{2,18},{3,19},{4,20},{5,21},{6,22},{7,23},{8,24},{9,... | collective-permute-start | bytes 909320 | tf_op jit(solution)/shard_map/ppermute | solution.py:601
  47.3 0.0 collective-permute-done.13
  47.3 2.4 %collective-permute-start.14 = (f32[1,296,128]{2,1,0:T(8,128)S(1)}, f32[1,296,128]{2,1,0:T(8,128)S(1)}, u32[]{:S(2)}, u32[]{:S(2)}) collective-permute-start(f32[1,296,128]{2,1,0:T(8,128)S(1)} %collective-permute-done.13), channel_id=1, source_target_pairs={{0,16},{1,17},{2,18},{3,19},{4,20},{5,21},{6,22},{7,23},{8,24},{9,... | collective-permute-start | bytes 454664 | tf_op jit(solution)/shard_map/ppermute | solution.py:601
  49.6 0.3 collective-permute-done.7
  49.9 1.2 collective-permute-start.8
  51.1 3.6 %collective-permute-done.11 = f32[1,296,128]{2,1,0:T(8,128)S(1)} collective-permute-done((f32[1,296,128]{2,1,0:T(8,128)}, f32[1,296,128]{2,1,0:T(8,128)S(1)}, u32[]{:S(2)}, u32[]{:S(2)}) %collective-permute-start.11) | collective-permute-done | bytes 151584 | tf_op jit(solution)/shard_map/ppermute | solution.py:601
  54.7 0.6 collective-permute-start.12
  55.3 3.2 %collective-permute-done.14 = f32[1,296,128]{2,1,0:T(8,128)S(1)} collective-permute-done((f32[1,296,128]{2,1,0:T(8,128)S(1)}, f32[1,296,128]{2,1,0:T(8,128)S(1)}, u32[]{:S(2)}, u32[]{:S(2)}) %collective-permute-start.14) | collective-permute-done | bytes 151584 | tf_op jit(solution)/shard_map/ppermute | solution.py:601
  58.6 0.1 collective-permute-start.22
  58.6 1.2 collective-permute-done.12
  59.9 0.6 collective-permute-start.16
  60.5 1.1 collective-permute-done.8
  61.6 1.8 %collective-permute-start.15 = (f32[2,296,128]{2,1,0:T(8,128)S(1)}, f32[2,296,128]{2,1,0:T(8,128)S(1)}, u32[]{:S(2)}, u32[]{:S(2)}) collective-permute-start(f32[2,296,128]{2,1,0:T(8,128)S(1)} %constant_dynamic-update-slice_fusion.2.refs_4_), channel_id=1, source_target_pairs={{0,16},{1,17},{2,18},{3,19},{4,20},{5,21},{6,22},{7,23},{8,24},{9,... | collective-permute-start | bytes 909320 | tf_op jit(solution)/shard_map/ppermute | solution.py:601
  63.4 1.0 collective-permute-start.10
  64.4 5.6 %collective-permute-done.16.refs_7_ = f32[2,296,128]{2,1,0:T(8,128)S(1)} collective-permute-done((f32[2,296,128]{2,1,0:T(8,128)S(1)}, f32[2,296,128]{2,1,0:T(8,128)S(1)}, u32[]{:S(2)}, u32[]{:S(2)}) %collective-permute-start.16) | collective-permute-done | bytes 303136 | tf_op jit(solution)/shard_map/ppermute | solution.py:601
  70.0 0.5 collective-permute-start.24
  70.5 0.7 collective-permute-done.15.refs_6_
  71.3 3.5 %collective-permute-done.10.refs_3_ = f32[2,296,128]{2,1,0:T(8,128)S(1)} collective-permute-done((f32[2,296,128]{2,1,0:T(8,128)S(1)}, f32[2,296,128]{2,1,0:T(8,128)S(1)}, u32[]{:S(2)}, u32[]{:S(2)}) %collective-permute-start.10) | collective-permute-done | bytes 303136 | tf_op jit(solution)/shard_map/ppermute | solution.py:601
  74.8 1.5 collective-permute-done.20.refs_11_
  76.5 0.6 copy-done.17
  77.0 84.1 %panels.1 = (f32[4096,2048]{1,0:T(8,128)}, f32[512,512]{1,0:T(8,128)}) custom-call(s32[4]{0:T(128)} %pad_add_fusion.place_ref, f32[2,296,128]{2,1,0:T(8,128)} %copy-done, f32[2,296,128]{2,1,0:T(8,128)} %copy-done.3, f32[2,296,128]{2,1,0:T(8,128)} %copy-done.7, f32[2,296,128]{2,1,0:T(8,128)} %copy-done.12, f32[2,296,128]{2,1,0:T(8,128)} %copy-done.4, ...), custom_call_target="tpu_custom_call" | custom-call | tf_op jit(solution)/shard_map/panels/pallas_call | solution.py:705
  (59 shorter events, 0.2 us)
Async XLA Ops:
  3.2 9.2 %collective-permute-start = (f32[36,2,8,128]{3,2,1,0:T(8,128)}, f32[36,2,8,128]{3,2,1,0:T(8,128)S(1)}, u32[]{:S(2)}, u32[]{:S(2)}) collective-permute-start(f32[36,2,8,128]{3,2,1,0:T(8,128)} %get-tuple-element.8), channel_id=1, source_target_pairs={{0,8},{1,9},{2,10},{3,11},{4,12},{5,13},{6,14},{7,15},{8,16},{9,17... | collective-permute-start | bytes 884744 | tf_op jit(solution)/shard_map/ppermute | solution.py:667
  5.5 6.9 %collective-permute-start.1 = (f32[36,2,8,128]{3,2,1,0:T(8,128)}, f32[36,2,8,128]{3,2,1,0:T(8,128)S(1)}, u32[]{:S(2)}, u32[]{:S(2)}) collective-permute-start(f32[36,2,8,128]{3,2,1,0:T(8,128)} %get-tuple-element.9), channel_id=1, source_target_pairs={{8,0},{9,1},{10,2},{11,3},{12,4},{13,5},{14,6},{15,7},{16,8},{17,9... | collective-permute-start | bytes 884744 | tf_op jit(solution)/shard_map/ppermute | solution.py:667
  6.8 17.2 %collective-permute-start.2 = (f32[36,2,8,128]{3,2,1,0:T(8,128)}, f32[36,2,8,128]{3,2,1,0:T(8,128)S(1)}, u32[]{:S(2)}, u32[]{:S(2)}) collective-permute-start(f32[36,2,8,128]{3,2,1,0:T(8,128)} %get-tuple-element.10.own_hi), channel_id=1, source_target_pairs={{0,1},{1,2},{2,3},{3,4},{4,5},{5,6},{6,7},{8,9},{9,10},{10,11},{11... | collective-permute-start | bytes 884744 | tf_op jit(solution)/shard_map/ppermute | solution.py:667
  11.1 13.0 %collective-permute-start.3 = (f32[36,2,8,128]{3,2,1,0:T(8,128)}, f32[36,2,8,128]{3,2,1,0:T(8,128)S(1)}, u32[]{:S(2)}, u32[]{:S(2)}) collective-permute-start(f32[36,2,8,128]{3,2,1,0:T(8,128)} %get-tuple-element.11.own_lo), channel_id=1, source_target_pairs={{1,0},{2,1},{3,2},{4,3},{5,4},{6,5},{7,6},{9,8},{10,9},{11,10},{12... | collective-permute-start | bytes 884744 | tf_op jit(solution)/shard_map/ppermute | solution.py:667
  12.4 0.7 copy-start.1
  13.1 0.7 copy-start.2
  15.6 8.8 %collective-permute-start.4 = (f32[72,128]{1,0:T(8,128)}, f32[72,128]{1,0:T(8,128)S(1)}, u32[]{:S(2)}, u32[]{:S(2)}) collective-permute-start(f32[72,128]{1,0:T(8,128)} %get-tuple-element.12), channel_id=1, source_target_pairs={{0,1},{1,2},{2,3},{3,4},{4,5},{5,6},{6,7},{8,9},{9,10},{10,11},{11... | collective-permute-start | bytes 110600 | tf_op jit(solution)/shard_map/ppermute | solution.py:667
  20.2 6.5 %collective-permute-start.5 = (f32[72,128]{1,0:T(8,128)}, f32[72,128]{1,0:T(8,128)S(1)}, u32[]{:S(2)}, u32[]{:S(2)}) collective-permute-start(f32[72,128]{1,0:T(8,128)} %get-tuple-element.13), channel_id=1, source_target_pairs={{1,0},{2,1},{3,2},{4,3},{5,4},{6,5},{7,6},{9,8},{10,9},{11,10},{12... | collective-permute-start | bytes 110600 | tf_op jit(solution)/shard_map/ppermute | solution.py:667
  24.1 2.6 %copy-start.18 = (f32[36,2,8,128]{3,2,1,0:T(8,128)}, f32[36,2,8,128]{3,2,1,0:T(8,128)S(1)}, u32[]{:S(2)}) copy-start(f32[36,2,8,128]{3,2,1,0:T(8,128)S(1)} %collective-permute-done.2.ylo) | copy-start | bytes 884740
  24.1 2.6 %copy-start.19 = (f32[36,2,8,128]{3,2,1,0:T(8,128)}, f32[36,2,8,128]{3,2,1,0:T(8,128)S(1)}, u32[]{:S(2)}) copy-start(f32[36,2,8,128]{3,2,1,0:T(8,128)S(1)} %collective-permute-done.3.yhi) | copy-start | bytes 884740
  24.4 2.3 %copy-start.20 = (f32[72,128]{1,0:T(8,128)}, f32[72,128]{1,0:T(8,128)S(1)}, u32[]{:S(2)}) copy-start(f32[72,128]{1,0:T(8,128)S(1)} %collective-permute-done.4.edge_lo) | copy-start | bytes 110596
  26.7 0.6 copy-start.21
  34.8 7.6 %collective-permute-start.6 = (f32[1,296,128]{2,1,0:T(8,128)}, f32[1,296,128]{2,1,0:T(8,128)S(1)}, u32[]{:S(2)}, u32[]{:S(2)}) collective-permute-start(f32[1,296,128]{2,1,0:T(8,128)} %bitcast.10), channel_id=1, source_target_pairs={{0,1},{1,0},{2,3},{3,2},{4,5},{5,4},{6,7},{7,6},{8,9},{9,8},{10,11... | collective-permute-start | bytes 454664 | tf_op jit(solution)/shard_map/ppermute | solution.py:601
  37.7 9.5 %collective-permute-start.13 = (f32[1,296,128]{2,1,0:T(8,128)}, f32[1,296,128]{2,1,0:T(8,128)S(1)}, u32[]{:S(2)}, u32[]{:S(2)}) collective-permute-start(f32[1,296,128]{2,1,0:T(8,128)} %bitcast.11), channel_id=1, source_target_pairs={{0,6},{1,7},{2,4},{3,5},{4,2},{5,3},{6,0},{7,1},{8,14},{9,15},{10,... | collective-permute-start | bytes 454664 | tf_op jit(solution)/shard_map/ppermute | solution.py:601
  40.2 9.7 %collective-permute-start.7 = (f32[1,296,128]{2,1,0:T(8,128)}, f32[1,296,128]{2,1,0:T(8,128)S(1)}, u32[]{:S(2)}, u32[]{:S(2)}) collective-permute-start(f32[1,296,128]{2,1,0:T(8,128)} %bitcast.12), channel_id=1, source_target_pairs={{0,2},{1,3},{2,0},{3,1},{4,6},{5,7},{6,4},{7,5},{8,10},{9,11},{10,... | collective-permute-start | bytes 454664 | tf_op jit(solution)/shard_map/ppermute | solution.py:601
  40.9 13.8 %collective-permute-start.11 = (f32[1,296,128]{2,1,0:T(8,128)}, f32[1,296,128]{2,1,0:T(8,128)S(1)}, u32[]{:S(2)}, u32[]{:S(2)}) collective-permute-start(f32[1,296,128]{2,1,0:T(8,128)} %bitcast.13), channel_id=1, source_target_pairs={{0,4},{1,5},{2,6},{3,7},{4,0},{5,1},{6,2},{7,3},{8,12},{9,13},{10,... | collective-permute-start | bytes 454664 | tf_op jit(solution)/shard_map/ppermute | solution.py:601
  43.4 32.9 %copy-start = (f32[2,296,128]{2,1,0:T(8,128)}, f32[2,296,128]{2,1,0:T(8,128)S(1)}, u32[]{:S(2)}) copy-start(f32[2,296,128]{2,1,0:T(8,128)S(1)} %pad_maximum_fusion.refs_0_) | copy-start | bytes 909316
  43.4 18.2 %collective-permute-start.17 = (f32[2,296,128]{2,1,0:T(8,128)S(1)}, f32[2,296,128]{2,1,0:T(8,128)S(1)}, u32[]{:S(2)}, u32[]{:S(2)}) collective-permute-start(f32[2,296,128]{2,1,0:T(8,128)S(1)} %pad_maximum_fusion.refs_0_), channel_id=1, source_target_pairs={{0,8},{1,9},{2,10},{3,11},{4,12},{5,13},{6,14},{7,15},{8,0},{9,1},... | collective-permute-start | bytes 909320 | tf_op jit(solution)/shard_map/ppermute | solution.py:601
  43.5 19.9 %collective-permute-start.9 = (f32[2,296,128]{2,1,0:T(8,128)S(1)}, f32[2,296,128]{2,1,0:T(8,128)S(1)}, u32[]{:S(2)}, u32[]{:S(2)}) collective-permute-start(f32[2,296,128]{2,1,0:T(8,128)S(1)} %pad_maximum_fusion.refs_0_), channel_id=1, source_target_pairs={{0,16},{1,17},{2,18},{3,19},{4,20},{5,21},{6,22},{7,23},{8,24},{9,... | collective-permute-start | bytes 909320 | tf_op jit(solution)/shard_map/ppermute | solution.py:601
  47.3 11.3 %collective-permute-start.14 = (f32[1,296,128]{2,1,0:T(8,128)S(1)}, f32[1,296,128]{2,1,0:T(8,128)S(1)}, u32[]{:S(2)}, u32[]{:S(2)}) collective-permute-start(f32[1,296,128]{2,1,0:T(8,128)S(1)} %collective-permute-done.13), channel_id=1, source_target_pairs={{0,16},{1,17},{2,18},{3,19},{4,20},{5,21},{6,22},{7,23},{8,24},{9,... | collective-permute-start | bytes 454664 | tf_op jit(solution)/shard_map/ppermute | solution.py:601
  49.9 11.6 %collective-permute-start.8 = (f32[1,296,128]{2,1,0:T(8,128)S(1)}, f32[1,296,128]{2,1,0:T(8,128)S(1)}, u32[]{:S(2)}, u32[]{:S(2)}) collective-permute-start(f32[1,296,128]{2,1,0:T(8,128)S(1)} %collective-permute-done.7), channel_id=1, source_target_pairs={{0,16},{1,17},{2,18},{3,19},{4,20},{5,21},{6,22},{7,23},{8,24},{9,... | collective-permute-start | bytes 454664 | tf_op jit(solution)/shard_map/ppermute | solution.py:601
  54.7 5.2 %collective-permute-start.12 = (f32[1,296,128]{2,1,0:T(8,128)S(1)}, f32[1,296,128]{2,1,0:T(8,128)S(1)}, u32[]{:S(2)}, u32[]{:S(2)}) collective-permute-start(f32[1,296,128]{2,1,0:T(8,128)S(1)} %collective-permute-done.11), channel_id=1, source_target_pairs={{0,1},{1,0},{2,3},{3,2},{4,5},{5,4},{6,7},{7,6},{8,9},{9,8},{10,11... | collective-permute-start | bytes 454664 | tf_op jit(solution)/shard_map/ppermute | solution.py:601
  58.6 17.8 %copy-start.5 = (f32[2,296,128]{2,1,0:T(8,128)}, f32[2,296,128]{2,1,0:T(8,128)S(1)}, u32[]{:S(2)}) copy-start(f32[2,296,128]{2,1,0:T(8,128)S(1)} %constant_dynamic-update-slice_fusion.4.refs_5_) | copy-start | bytes 909316
  58.6 5.8 %collective-permute-start.22 = (f32[2,296,128]{2,1,0:T(8,128)S(1)}, f32[2,296,128]{2,1,0:T(8,128)S(1)}, u32[]{:S(2)}, u32[]{:S(2)}) collective-permute-start(f32[2,296,128]{2,1,0:T(8,128)S(1)} %constant_dynamic-update-slice_fusion.4.refs_5_), channel_id=1, source_target_pairs={{0,8},{1,9},{2,10},{3,11},{4,12},{5,13},{6,14},{7,15},{8,0},{9,1},... | collective-permute-start | bytes 909320 | tf_op jit(solution)/shard_map/ppermute | solution.py:601
  59.9 10.1 %collective-permute-start.16 = (f32[2,296,128]{2,1,0:T(8,128)S(1)}, f32[2,296,128]{2,1,0:T(8,128)S(1)}, u32[]{:S(2)}, u32[]{:S(2)}) collective-permute-start(f32[2,296,128]{2,1,0:T(8,128)S(1)} %constant_dynamic-update-slice_fusion.4.refs_5_), channel_id=1, source_target_pairs={{0,1},{1,0},{2,3},{3,2},{4,5},{5,4},{6,7},{7,6},{8,9},{9,8},{10,11... | collective-permute-start | bytes 909320 | tf_op jit(solution)/shard_map/ppermute | solution.py:601
  60.5 15.9 %copy-start.4 = (f32[2,296,128]{2,1,0:T(8,128)}, f32[2,296,128]{2,1,0:T(8,128)S(1)}, u32[]{:S(2)}) copy-start(f32[2,296,128]{2,1,0:T(8,128)S(1)} %constant_dynamic-update-slice_fusion.2.refs_4_) | copy-start | bytes 909316
  61.5 8.5 %collective-permute-start.21 = (f32[2,296,128]{2,1,0:T(8,128)S(1)}, f32[2,296,128]{2,1,0:T(8,128)S(1)}, u32[]{:S(2)}, u32[]{:S(2)}) collective-permute-start(f32[2,296,128]{2,1,0:T(8,128)S(1)} %constant_dynamic-update-slice_fusion.2.refs_4_), channel_id=1, source_target_pairs={{0,8},{1,9},{2,10},{3,11},{4,12},{5,13},{6,14},{7,15},{8,0},{9,1},... | collective-permute-start | bytes 909320 | tf_op jit(solution)/shard_map/ppermute | solution.py:601
  61.5 14.8 %copy-start.3 = (f32[2,296,128]{2,1,0:T(8,128)}, f32[2,296,128]{2,1,0:T(8,128)S(1)}, u32[]{:S(2)}) copy-start(f32[2,296,128]{2,1,0:T(8,128)S(1)} %constant_dynamic-update-slice_fusion.refs_1_) | copy-start | bytes 909316
  61.6 14.8 %copy-start.6 = (f32[2,296,128]{2,1,0:T(8,128)}, f32[2,296,128]{2,1,0:T(8,128)S(1)}, u32[]{:S(2)}) copy-start(f32[2,296,128]{2,1,0:T(8,128)S(1)} %collective-permute-done.17.refs_8_) | copy-start | bytes 909316
  61.6 9.7 %collective-permute-start.15 = (f32[2,296,128]{2,1,0:T(8,128)S(1)}, f32[2,296,128]{2,1,0:T(8,128)S(1)}, u32[]{:S(2)}, u32[]{:S(2)}) collective-permute-start(f32[2,296,128]{2,1,0:T(8,128)S(1)} %constant_dynamic-update-slice_fusion.2.refs_4_), channel_id=1, source_target_pairs={{0,16},{1,17},{2,18},{3,19},{4,20},{5,21},{6,22},{7,23},{8,24},{9,... | collective-permute-start | bytes 909320 | tf_op jit(solution)/shard_map/ppermute | solution.py:601
  63.4 13.0 %copy-start.7 = (f32[2,296,128]{2,1,0:T(8,128)}, f32[2,296,128]{2,1,0:T(8,128)S(1)}, u32[]{:S(2)}) copy-start(f32[2,296,128]{2,1,0:T(8,128)S(1)} %collective-permute-done.9.refs_2_) | copy-start | bytes 909316
  63.4 11.3 %collective-permute-start.10 = (f32[2,296,128]{2,1,0:T(8,128)S(1)}, f32[2,296,128]{2,1,0:T(8,128)S(1)}, u32[]{:S(2)}, u32[]{:S(2)}) collective-permute-start(f32[2,296,128]{2,1,0:T(8,128)S(1)} %constant_dynamic-update-slice_fusion.refs_1_), channel_id=1, source_target_pairs={{0,1},{1,0},{2,3},{3,2},{4,5},{5,4},{6,7},{7,6},{8,9},{9,8},{10,11... | collective-permute-start | bytes 909320 | tf_op jit(solution)/shard_map/ppermute | solution.py:601
  64.4 12.0 %copy-start.8 = (f32[2,296,128]{2,1,0:T(8,128)}, f32[2,296,128]{2,1,0:T(8,128)S(1)}, u32[]{:S(2)}) copy-start(f32[2,296,128]{2,1,0:T(8,128)S(1)} %collective-permute-done.22.refs_13_) | copy-start | bytes 909316
  64.4 10.3 %collective-permute-start.18 = (f32[2,296,128]{2,1,0:T(8,128)S(1)}, f32[2,296,128]{2,1,0:T(8,128)S(1)}, u32[]{:S(2)}, u32[]{:S(2)}) collective-permute-start(f32[2,296,128]{2,1,0:T(8,128)S(1)} %constant_dynamic-update-slice_fusion.refs_1_), channel_id=1, source_target_pairs={{0,8},{1,9},{2,10},{3,11},{4,12},{5,13},{6,14},{7,15},{8,0},{9,1},... | collective-permute-start | bytes 909320 | tf_op jit(solution)/shard_map/ppermute | solution.py:601
  70.0 6.4 %copy-start.9 = (f32[2,296,128]{2,1,0:T(8,128)}, f32[2,296,128]{2,1,0:T(8,128)S(1)}, u32[]{:S(2)}) copy-start(f32[2,296,128]{2,1,0:T(8,128)S(1)} %collective-permute-done.16.refs_7_) | copy-start | bytes 909316
  70.0 4.8 %collective-permute-start.19 = (f32[2,296,128]{2,1,0:T(8,128)S(1)}, f32[2,296,128]{2,1,0:T(8,128)S(1)}, u32[]{:S(2)}, u32[]{:S(2)}) collective-permute-start(f32[2,296,128]{2,1,0:T(8,128)S(1)} %collective-permute-done.9.refs_2_), channel_id=1, source_target_pairs={{0,8},{1,9},{2,10},{3,11},{4,12},{5,13},{6,14},{7,15},{8,0},{9,1},... | collective-permute-start | bytes 909320 | tf_op jit(solution)/shard_map/ppermute | solution.py:601
  70.0 6.4 %copy-start.10 = (f32[2,296,128]{2,1,0:T(8,128)}, f32[2,296,128]{2,1,0:T(8,128)S(1)}, u32[]{:S(2)}) copy-start(f32[2,296,128]{2,1,0:T(8,128)S(1)} %collective-permute-done.21.refs_12_) | copy-start | bytes 909316
  70.0 4.8 %collective-permute-start.24 = (f32[2,296,128]{2,1,0:T(8,128)S(1)}, f32[2,296,128]{2,1,0:T(8,128)S(1)}, u32[]{:S(2)}, u32[]{:S(2)}) collective-permute-start(f32[2,296,128]{2,1,0:T(8,128)S(1)} %collective-permute-done.16.refs_7_), channel_id=1, source_target_pairs={{0,8},{1,9},{2,10},{3,11},{4,12},{5,13},{6,14},{7,15},{8,0},{9,1},... | collective-permute-start | bytes 909320 | tf_op jit(solution)/shard_map/ppermute | solution.py:601
  71.3 5.1 %copy-start.11 = (f32[2,296,128]{2,1,0:T(8,128)}, f32[2,296,128]{2,1,0:T(8,128)S(1)}, u32[]{:S(2)}) copy-start(f32[2,296,128]{2,1,0:T(8,128)S(1)} %collective-permute-done.15.refs_6_) | copy-start | bytes 909316
  71.3 3.5 %collective-permute-start.23 = (f32[2,296,128]{2,1,0:T(8,128)S(1)}, f32[2,296,128]{2,1,0:T(8,128)S(1)}, u32[]{:S(2)}, u32[]{:S(2)}) collective-permute-start(f32[2,296,128]{2,1,0:T(8,128)S(1)} %collective-permute-done.15.refs_6_), channel_id=1, source_target_pairs={{0,8},{1,9},{2,10},{3,11},{4,12},{5,13},{6,14},{7,15},{8,0},{9,1},... | collective-permute-start | bytes 909320 | tf_op jit(solution)/shard_map/ppermute | solution.py:601
  74.7 1.7 %copy-start.12 = (f32[2,296,128]{2,1,0:T(8,128)}, f32[2,296,128]{2,1,0:T(8,128)S(1)}, u32[]{:S(2)}) copy-start(f32[2,296,128]{2,1,0:T(8,128)S(1)} %collective-permute-done.10.refs_3_) | copy-start | bytes 909316
  74.7 1.6 collective-permute-start.20
  74.7 1.7 %copy-start.13 = (f32[2,296,128]{2,1,0:T(8,128)}, f32[2,296,128]{2,1,0:T(8,128)S(1)}, u32[]{:S(2)}) copy-start(f32[2,296,128]{2,1,0:T(8,128)S(1)} %collective-permute-done.18.refs_9_) | copy-start | bytes 909316
  74.8 1.7 %copy-start.14 = (f32[2,296,128]{2,1,0:T(8,128)}, f32[2,296,128]{2,1,0:T(8,128)S(1)}, u32[]{:S(2)}) copy-start(f32[2,296,128]{2,1,0:T(8,128)S(1)} %collective-permute-done.19.refs_10_) | copy-start | bytes 909316
  74.8 1.7 %copy-start.15 = (f32[2,296,128]{2,1,0:T(8,128)}, f32[2,296,128]{2,1,0:T(8,128)S(1)}, u32[]{:S(2)}) copy-start(f32[2,296,128]{2,1,0:T(8,128)S(1)} %collective-permute-done.24.refs_15_) | copy-start | bytes 909316
  74.8 1.6 %copy-start.16 = (f32[2,296,128]{2,1,0:T(8,128)}, f32[2,296,128]{2,1,0:T(8,128)S(1)}, u32[]{:S(2)}) copy-start(f32[2,296,128]{2,1,0:T(8,128)S(1)} %collective-permute-done.23.refs_14_) | copy-start | bytes 909316
  76.3 0.7 copy-start.17

commit v4 on v3

--- a/solution.py
+++ b/solution.py
@@ -15,6 +15,7 @@
 LOC = 8
 HEAD = PANEL * PANELS
 ROWS = 40
+DEPTH = 80
 LANES = 128
 
 diffuse_rate = 0.06
@@ -51,7 +52,7 @@
         one(mem, i, i)
         return carry
 
-    lax.fori_loop(0, members_n, members_loop, 0)
+    lax.fori_loop(0, members_n, members_loop, 0, unroll=4)
     for d in range(3):
         one(cour, d, members_n + d)
     one(diff, 0, members_n + 3)
@@ -258,16 +259,49 @@
         out[used:, :] = jnp.zeros((out.shape[0] - used, LANES), F32)
 
 
-def taper_cov(left, right, members_n):
-    cov = jnp.dot(
-        left[:, :members_n].astype(BF16), right[:members_n].astype(BF16), preferred_element_type=F32
-    )
+def taper_cov(left, right):
+    some = left[:, :DEPTH].astype(BF16)
+    cov = jnp.dot(some, right[:DEPTH], preferred_element_type=F32)
+    dist = jnp.dot(some, right[DEPTH:], preferred_element_type=F32)
+    return cov * pl.reciprocal(dist, approx=True)
+
+
+def taper_tile(left, right, places):
+    members_n = ROWS - 8
+    cov = jnp.dot(left[:, :DEPTH].astype(BF16), right[:DEPTH], preferred_element_type=F32)
     dist = members_n - 1.0
     for d in range(3):
-        at = members_n + d
-        gap = left[:, at : at + 1] - right[at : at + 1, :]
+        gap = left[:, DEPTH + d : DEPTH + d + 1] - places[d : d + 1, :]
         dist = dist + gap * gap
     return cov * pl.reciprocal(dist, approx=True)
+
+
+def thirds(value):
+    first = value.astype(BF16).astype(F32)
+    rest = value - first
+    second = rest.astype(BF16).astype(F32)
+    return first, second, (rest - second).astype(BF16).astype(F32)
+
+
+def sides(chunk, centers):
+    members_n = ROWS - 8
+    sub = lax.broadcasted_iota(jnp.int32, (8, LANES), 0)
+    place = jnp.where(sub == 0, centers[0], jnp.where(sub == 1, centers[1], centers[2]))
+    at = jnp.where(sub < 3, chunk[members_n:] - place, 0.0)
+    square = at * at
+    norm = square[0:1] + square[1:2] + square[2:3]
+    norm = jnp.broadcast_to(norm, (8, LANES))
+    p1, p2, p3 = thirds(at)
+
+    def rows(value):
+        first, second, third = thirds(value)
+        return jnp.where(sub == 3, first, jnp.where(sub == 4, second, jnp.where(sub == 5, third, 0.0)))
+
+    ones = jnp.where((sub > 2) & (sub < 6), 1.0, 0.0)
+    left = [chunk[:members_n], p1 + rows(norm), p1 + ones, p2, p2, p1, p3, at]
+    q1, q2, q3 = -2.0 * p1, -2.0 * p2, -2.0 * p3
+    right = [q1 + ones, q2 + rows(norm + (members_n - 1.0)), q1, q2, q3, q1]
+    return jnp.concatenate(left, 0), jnp.concatenate(right, 0), at
 
 
 def eliminate(a, beside):
@@ -283,9 +317,10 @@
     def across(v, k):
         return jnp.broadcast_to(v[:, k : k + 1], (8, LANES))
 
+    ahead = None
     for gk in range(groups):
         k0 = 8 * gk
-        col = [across(a[gk], k0 + j) for j in range(8)]
+        col = ahead or [across(a[gk], k0 + j) for j in range(8)]
         u = [[down(col[j], i) if i >= j else None for i in range(8)] for j in range(8)]
         inv = []
         todo = beside(gk)
@@ -316,10 +351,15 @@
         for g in range(gk + 1, groups):
             c = [across(a[g], k0 + j) for j in range(8)]
             ag, mg = a[g], m[g]
+            if g == gk + 1:
+                ahead = [across(ag, k0 + 8 + j) for j in range(8)]
             for j in range(8):
                 f = c[j] * inv[j]
                 for i in range(j + 1, 8):
                     c[i] = c[i] - f * u[j][i]
+                if g == gk + 1:
+                    for i in range(8):
+                        ahead[i] = ahead[i] - f * down(c[j], i)
                 ag = ag - f * rows_a[j]
                 mg = mg - f * rows_m[j]
             a[g], m[g] = ag, mg
@@ -327,11 +367,11 @@
 
 
 def turned(chunk):
-    return jnp.concatenate([chunk, jnp.zeros((LANES - ROWS, LANES), F32)], 0).T
+    return jnp.concatenate([chunk, jnp.zeros((LANES - DEPTH - 8, LANES), F32)], 0).T
 
 
 def head_stage(
-    place_ref, pieces, patterns, parts, cols_out, head_out, down_out, linv_a, linv_b, fcols_out, obs_head, full,
+    place_ref, pieces, patterns, parts, cols_out, col_places, head_out, down_out, linv_a, linv_b, fcols_out, obs_head, full,
     work, count_vec, count_smem, sem, lefts, rows_cross, cols_cross, obs_down,
 ):
     col_chunks = cols_out.shape[1] // LANES
@@ -406,11 +446,28 @@
     for j in range(PANELS):
         obs_head[:, j * LANES : (j + 1) * LANES] = full[full.shape[0] - 1, j : j + 1, :]
 
-    for c in range(col_chunks):
-        cols_out[:, c * LANES : (c + 1) * LANES] = full[tile * col_chunks + c]
+    centers = [
+        (place_ref[2] + 1).astype(F32) * (4.0 * unit), tiles.astype(F32) * (4.0 * unit), LANES * 0.5 * unit
+    ]
+
+    def across_side(out, places, c, chunk):
+        lanes = pl.ds(pl.multiple_of(c * LANES, LANES), LANES)
+        _, right, at = sides(chunk, centers)
+        right = right.astype(BF16)
+        if places is not None:
+            places[:, lanes] = at
+        out[:members_n, lanes] = chunk[:members_n].astype(BF16)
+        out[members_n : DEPTH + members_n, lanes] = jnp.zeros((DEPTH, LANES), BF16)
+        out[DEPTH + members_n :, lanes] = right
+
+    def across_cols(c, carry):
+        across_side(cols_out, col_places, c, full[tile * col_chunks + c])
+        return carry
+
+    lax.fori_loop(0, col_chunks, across_cols, 0, unroll=4)
     for c in range(PANELS):
-        head_out[:, c * LANES : (c + 1) * LANES] = full[c]
-        down_out[c * LANES : (c + 1) * LANES, :] = turned(full[c])
+        across_side(head_out, None, c, full[c])
+        down_out[c * LANES : (c + 1) * LANES, :] = turned(sides(full[c], centers)[0])
 
     head = head_out[...]
     down = down_out[...]
@@ -427,7 +484,7 @@
     head_iota = lax.broadcasted_iota(jnp.int32, (16, HEAD), 1)
     down_iota = lax.broadcasted_iota(jnp.int32, (8, HEAD), 0)
     col_iota = lax.broadcasted_iota(jnp.int32, (8, HEAD), 1)
-    work[:HEAD, :HEAD] = taper_cov(down, head, members_n) + jnp.where(same, obs_head[...], 0.0)
+    work[:HEAD, :HEAD] = taper_cov(down, head) + jnp.where(same, obs_head[...], 0.0)
     work[:HEAD, HEAD:] = jnp.where(same, 1.0, 0.0).astype(F32)
 
     def panel(p, carry):
@@ -444,11 +501,11 @@
             if g % per_chunk == 0:
                 c = lax.div(part, per_chunk)
                 lefts[pl.ds(pl.multiple_of(c * LANES, LANES), LANES), :] = turned(
-                    full[grp * (span // LANES) + c]
+                    sides(full[grp * (span // LANES) + c], centers)[0]
                 )
             def some_rows(r):
                 at = pl.multiple_of(part * some + r, 16)
-                cross = taper_cov(lefts[pl.ds(at, 16), :], head_out[...], members_n)
+                cross = taper_cov(lefts[pl.ds(at, 16), :], head_out[...])
                 same = row_iota + (grp * span + at) == head_iota
                 hi, lo = split(cross + jnp.where(same, obs_head[...], 0.0))
                 rows_cross[pl.ds(at, 16), :HEAD] = hi
@@ -456,7 +513,7 @@
 
             def some_lanes(c):
                 at = pl.multiple_of(part * 8, 8)
-                cross = taper_cov(down_out[pl.ds(at, 8), :], cols_out[:, c : c + HEAD], members_n)
+                cross = taper_cov(down_out[pl.ds(at, 8), :], cols_out[:, c : c + HEAD])
                 same = down_iota + at == col_iota + (tile * col_span + c)
                 cols_cross[pl.ds(at, 8), c : c + HEAD] = cross + jnp.where(
                     same, obs_down[pl.ds(at, 8), :1], 0.0
@@ -514,7 +571,7 @@
     pieces = refs[: len(patterns)]
     obs, trailing, factor = refs[len(patterns) : len(patterns) + 3]
     (
-        cols, head, down, linv_a, linv_b, fcols, obs_head, full, work, count_vec, count_smem, sem, keep, lefts,
+        cols, col_places, head, down, linv_a, linv_b, fcols, obs_head, full, work, count_vec, count_smem, sem, keep, lefts,
         rows_cross, cols_cross, obs_down, factors,
     ) = refs[len(patterns) + 3 :]
     members_n = ROWS - 8
@@ -559,7 +616,7 @@
     @pl.when(step == 0)
     def _():
         head_stage(
-            place_ref, pieces, patterns, parts, cols, head, down, linv_a, linv_b, fcols, obs_head, full, work,
+            place_ref, pieces, patterns, parts, cols, col_places, head, down, linv_a, linv_b, fcols, obs_head, full, work,
             count_vec, count_smem, sem, lefts, rows_cross, cols_cross, obs_down,
         )
         prepare(0, 0)
@@ -571,7 +628,7 @@
     following = jnp.minimum(step + 1, steps - 1)
     width = min(512, col_span)
     for c in range(0, col_span, width):
-        value = taper_cov(left, cols[:, c : c + width], members_n)
+        value = taper_tile(left, cols[:, c : c + width], col_places[:, c : c + width])
         trailing[:, c : c + width] = value - jnp.dot(
             f3, fcols[:, c : c + width], preferred_element_type=F32
         )
@@ -712,8 +769,9 @@
         in_specs=[spec(pltpu.SMEM)] + [spec()] * (len(pieces) + 1),
         out_specs=[pl.BlockSpec((height, col_span), lambda i: (i, 0)), pl.BlockSpec((share, HEAD), lambda i: (0, 0))],
         scratch_shapes=[
-            pltpu.VMEM((ROWS, col_span), F32),
-            pltpu.VMEM((ROWS, HEAD), F32),
+            pltpu.VMEM((2 * DEPTH, col_span), BF16),
+            pltpu.VMEM((8, col_span), F32),
+            pltpu.VMEM((2 * DEPTH, HEAD), BF16),
             pltpu.VMEM((HEAD, LANES), F32),
             pltpu.VMEM((HEAD // 2, 3 * HEAD // 2), BF16),
             pltpu.VMEM((HEAD // 2, 3 * HEAD), BF16),

time: 162 us -> 158 us (0.975)
  Pallas kernels: 96 us -> 92 us
    pallas_call x1, Pallas kernels: 84.1 us -> 80.2 us  [per_device(): pl.pallas_call(functools.partial(final_kernel, patterns=patterns, parts=p...]
where the time goes in v4:
time: 158 us; the launch traced here: 157 us
  Pallas kernels  92 us (58%)
  starting transfers between devices  34.2 us (22%)
  waiting for transfers between devices  23.7 us (15%)
  local copies, waits for them, and re-layouts  4.11 us (3%)
  between operations  1.82 us (1%)
    pallas_call x1, Pallas kernels, per_device(): pl.pallas_call(functools.partial(final_kernel, patterns=patterns, parts=p...  80.2 us
    ppermute x19, waiting for transfers between devices, swap(): lax.ppermute(value, ('grp', 'tile'), pairs)  21.1 us
    ppermute x19, starting transfers between devices, swap(): lax.ppermute(value, ('grp', 'tile'), pairs)  19.2 us
    ppermute x6, starting transfers between devices, move(): return lax.ppermute(value, ('grp', 'tile'), pairs)  15 us
    pallas_call x1, Pallas kernels, per_device(): pl.pallas_call(forecast_kernel, out_shape=jax.ShapeDtypeStruct((-(-(membe...  7.53 us
  transfers between devices with their start and end apart: 25, of which 12 were waited for; matrix products, arithmetic and copies ran while one was open for 2% of the time, Pallas kernels for 1%

profile of v4, /device:TPU:0, one launch (start us, length us, event | category | flops | bytes accessed | tf_op | source)
XLA Modules:
  0.0 157.3 jit_solution(4260627830427738196)
XLA Ops:
  0.6 2.4 %cut.1 = (f32[36,2,8,128]{3,2,1,0:T(8,128)}, f32[36,2,8,128]{3,2,1,0:T(8,128)}, f32[36,2,8,128]{3,2,1,0:T(8,128)}, f32[36,2,8,128]{3,2,1,0:T(8,128)}) custom-call(f32[32,64,128]{2,1,0:T(8,128)} %bitcast.9, f32[3,64,128]{2,1,0:T(8,128)} %bitcast.15, f32[64,128]{1,0:T(8,128)} %bitcast.16, f32[64,128]{1,0:T(8,128)} %bitcast.17), custom_call_target="tpu_custom_call" | custom-call | tf_op jit(solution)/shard_map/cut/pallas_call | solution.py:706
  3.1 2.4 %collective-permute-start = (f32[36,2,8,128]{3,2,1,0:T(8,128)}, f32[36,2,8,128]{3,2,1,0:T(8,128)S(1)}, u32[]{:S(2)}, u32[]{:S(2)}) collective-permute-start(f32[36,2,8,128]{3,2,1,0:T(8,128)} %get-tuple-element.8), channel_id=1, source_target_pairs={{0,8},{1,9},{2,10},{3,11},{4,12},{5,13},{6,14},{7,15},{8,16},{9,17... | collective-permute-start | bytes 884744 | tf_op jit(solution)/shard_map/ppermute | solution.py:724
  5.4 1.3 collective-permute-start.1
  6.7 4.2 %collective-permute-start.2 = (f32[36,2,8,128]{3,2,1,0:T(8,128)}, f32[36,2,8,128]{3,2,1,0:T(8,128)S(1)}, u32[]{:S(2)}, u32[]{:S(2)}) collective-permute-start(f32[36,2,8,128]{3,2,1,0:T(8,128)} %get-tuple-element.10.own_hi), channel_id=1, source_target_pairs={{0,1},{1,2},{2,3},{3,4},{4,5},{5,6},{6,7},{8,9},{9,10},{10,11},{11... | collective-permute-start | bytes 884744 | tf_op jit(solution)/shard_map/ppermute | solution.py:724
  11.0 1.3 collective-permute-start.3
  12.3 0.0 copy-start.1
  12.3 0.0 collective-permute-done.1.xhi
  12.3 0.7 copy-done.1
  13.0 0.7 copy-done.2
  13.7 1.8 %edges.1 = (f32[72,128]{1,0:T(8,128)}, f32[72,128]{1,0:T(8,128)}) custom-call(f32[36,2,8,128]{3,2,1,0:T(8,128)} %copy-done.1, f32[36,2,8,128]{3,2,1,0:T(8,128)} %copy-done.2), custom_call_target="tpu_custom_call" | custom-call | tf_op jit(solution)/shard_map/edges/pallas_call | solution.py:729
  15.5 4.5 %collective-permute-start.4 = (f32[72,128]{1,0:T(8,128)}, f32[72,128]{1,0:T(8,128)S(1)}, u32[]{:S(2)}, u32[]{:S(2)}) collective-permute-start(f32[72,128]{1,0:T(8,128)} %get-tuple-element.12), channel_id=1, source_target_pairs={{0,1},{1,2},{2,3},{3,4},{4,5},{5,6},{6,7},{8,9},{9,10},{10,11},{11... | collective-permute-start | bytes 110600 | tf_op jit(solution)/shard_map/ppermute | solution.py:724
  20.1 1.3 collective-permute-start.5
  21.4 0.6 pad_add_fusion.place_ref
  22.6 1.4 dynamic_slice.3
  24.0 0.3 collective-permute-done.4.edge_lo
  24.3 2.3 %collective-permute-done.5.edge_hi = f32[72,128]{1,0:T(8,128)S(1)} collective-permute-done((f32[72,128]{1,0:T(8,128)}, f32[72,128]{1,0:T(8,128)S(1)}, u32[]{:S(2)}, u32[]{:S(2)}) %collective-permute-start.5) | collective-permute-done | bytes 36896 | tf_op jit(solution)/shard_map/ppermute | solution.py:724
  26.6 0.6 copy-done.21
  27.2 7.5 %forecast.1 = f32[296,128]{1,0:T(8,128)} custom-call(s32[4]{0:T(128)} %pad_add_fusion.place_ref, s32[1]{0:T(128)S(6)} %copy.13.count_ref, f32[32,8,8,128]{3,2,1,0:T(8,128)} %mem.1, f32[3,8,8,128]{3,2,1,0:T(8,128)} %cour.1, f32[8,8,128]{2,1,0:T(8,128)} %turb.1, f32[8,8,128]{2,1,0:T(8,128)} %diss.1, f32[36,2,8,128]{3,2,1,0:T(8,128)} %copy-done.1, ...), custom_call_target="tpu_custom_call" | custom-call | tf_op jit(solution)/shard_map/forecast/pallas_call | solution.py:742
  34.7 2.9 %collective-permute-start.6 = (f32[1,296,128]{2,1,0:T(8,128)}, f32[1,296,128]{2,1,0:T(8,128)S(1)}, u32[]{:S(2)}, u32[]{:S(2)}) collective-permute-start(f32[1,296,128]{2,1,0:T(8,128)} %bitcast.10), channel_id=1, source_target_pairs={{0,1},{1,0},{2,3},{3,2},{4,5},{5,4},{6,7},{7,6},{8,9},{9,8},{10,11... | collective-permute-start | bytes 454664 | tf_op jit(solution)/shard_map/ppermute | solution.py:658
  37.6 2.5 %collective-permute-start.13 = (f32[1,296,128]{2,1,0:T(8,128)}, f32[1,296,128]{2,1,0:T(8,128)S(1)}, u32[]{:S(2)}, u32[]{:S(2)}) collective-permute-start(f32[1,296,128]{2,1,0:T(8,128)} %bitcast.11), channel_id=1, source_target_pairs={{0,6},{1,7},{2,4},{3,5},{4,2},{5,3},{6,0},{7,1},{8,14},{9,15},{10,... | collective-permute-start | bytes 454664 | tf_op jit(solution)/shard_map/ppermute | solution.py:658
  40.1 0.7 collective-permute-start.7
  40.8 1.2 collective-permute-start.11
  42.0 0.3 collective-permute-done.6
  42.3 0.9 pad_maximum_fusion.refs_0_
  43.3 0.1 collective-permute-start.17
  43.4 3.8 %collective-permute-start.9 = (f32[2,296,128]{2,1,0:T(8,128)S(1)}, f32[2,296,128]{2,1,0:T(8,128)S(1)}, u32[]{:S(2)}, u32[]{:S(2)}) collective-permute-start(f32[2,296,128]{2,1,0:T(8,128)S(1)} %pad_maximum_fusion.refs_0_), channel_id=1, source_target_pairs={{0,16},{1,17},{2,18},{3,19},{4,20},{5,21},{6,22},{7,23},{8,24},{9,... | collective-permute-start | bytes 909320 | tf_op jit(solution)/shard_map/ppermute | solution.py:658
  47.2 2.3 %collective-permute-start.14 = (f32[1,296,128]{2,1,0:T(8,128)S(1)}, f32[1,296,128]{2,1,0:T(8,128)S(1)}, u32[]{:S(2)}, u32[]{:S(2)}) collective-permute-start(f32[1,296,128]{2,1,0:T(8,128)S(1)} %collective-permute-done.13), channel_id=1, source_target_pairs={{0,16},{1,17},{2,18},{3,19},{4,20},{5,21},{6,22},{7,23},{8,24},{9,... | collective-permute-start | bytes 454664 | tf_op jit(solution)/shard_map/ppermute | solution.py:658
  49.5 0.3 collective-permute-done.7
  49.8 1.2 collective-permute-start.8
  51.0 3.6 %collective-permute-done.11 = f32[1,296,128]{2,1,0:T(8,128)S(1)} collective-permute-done((f32[1,296,128]{2,1,0:T(8,128)}, f32[1,296,128]{2,1,0:T(8,128)S(1)}, u32[]{:S(2)}, u32[]{:S(2)}) %collective-permute-start.11) | collective-permute-done | bytes 151584 | tf_op jit(solution)/shard_map/ppermute | solution.py:658
  54.6 0.6 collective-permute-start.12
  55.2 3.3 %collective-permute-done.14 = f32[1,296,128]{2,1,0:T(8,128)S(1)} collective-permute-done((f32[1,296,128]{2,1,0:T(8,128)S(1)}, f32[1,296,128]{2,1,0:T(8,128)S(1)}, u32[]{:S(2)}, u32[]{:S(2)}) %collective-permute-start.14) | collective-permute-done | bytes 151584 | tf_op jit(solution)/shard_map/ppermute | solution.py:658
  58.5 0.1 collective-permute-start.22
  58.5 1.2 collective-permute-done.12
  59.8 0.6 collective-permute-start.16
  60.4 1.1 collective-permute-done.8
  61.4 0.0 collective-permute-start.21
  61.5 0.0 collective-permute-done.17.refs_8_
  61.5 1.8 %collective-permute-start.15 = (f32[2,296,128]{2,1,0:T(8,128)S(1)}, f32[2,296,128]{2,1,0:T(8,128)S(1)}, u32[]{:S(2)}, u32[]{:S(2)}) collective-permute-start(f32[2,296,128]{2,1,0:T(8,128)S(1)} %constant_dynamic-update-slice_fusion.2.refs_4_), channel_id=1, source_target_pairs={{0,16},{1,17},{2,18},{3,19},{4,20},{5,21},{6,22},{7,23},{8,24},{9,... | collective-permute-start | bytes 909320 | tf_op jit(solution)/shard_map/ppermute | solution.py:658
  63.3 0.0 collective-permute-done.9.refs_2_
  63.3 1.0 collective-permute-start.10
  64.3 5.6 %collective-permute-done.16.refs_7_ = f32[2,296,128]{2,1,0:T(8,128)S(1)} collective-permute-done((f32[2,296,128]{2,1,0:T(8,128)S(1)}, f32[2,296,128]{2,1,0:T(8,128)S(1)}, u32[]{:S(2)}, u32[]{:S(2)}) %collective-permute-start.16) | collective-permute-done | bytes 303136 | tf_op jit(solution)/shard_map/ppermute | solution.py:658
  69.9 0.5 collective-permute-start.24
  70.4 0.7 collective-permute-done.15.refs_6_
  71.2 3.5 %collective-permute-done.10.refs_3_ = f32[2,296,128]{2,1,0:T(8,128)S(1)} collective-permute-done((f32[2,296,128]{2,1,0:T(8,128)S(1)}, f32[2,296,128]{2,1,0:T(8,128)S(1)}, u32[]{:S(2)}, u32[]{:S(2)}) %collective-permute-start.10) | collective-permute-done | bytes 303136 | tf_op jit(solution)/shard_map/ppermute | solution.py:658
  74.7 1.5 collective-permute-done.20.refs_11_
  76.4 0.6 copy-done.17
  76.9 80.2 %panels.1 = (f32[4096,2048]{1,0:T(8,128)}, f32[512,512]{1,0:T(8,128)}) custom-call(s32[4]{0:T(128)} %pad_add_fusion.place_ref, f32[2,296,128]{2,1,0:T(8,128)} %copy-done, f32[2,296,128]{2,1,0:T(8,128)} %copy-done.3, f32[2,296,128]{2,1,0:T(8,128)} %copy-done.7, f32[2,296,128]{2,1,0:T(8,128)} %copy-done.12, f32[2,296,128]{2,1,0:T(8,128)} %copy-done.4, ...), custom_call_target="tpu_custom_call" | custom-call | tf_op jit(solution)/shard_map/panels/pallas_call | solution.py:762
  (59 shorter events, 0.2 us)
Async XLA Ops:
  3.1 9.2 %collective-permute-start = (f32[36,2,8,128]{3,2,1,0:T(8,128)}, f32[36,2,8,128]{3,2,1,0:T(8,128)S(1)}, u32[]{:S(2)}, u32[]{:S(2)}) collective-permute-start(f32[36,2,8,128]{3,2,1,0:T(8,128)} %get-tuple-element.8), channel_id=1, source_target_pairs={{0,8},{1,9},{2,10},{3,11},{4,12},{5,13},{6,14},{7,15},{8,16},{9,17... | collective-permute-start | bytes 884744 | tf_op jit(solution)/shard_map/ppermute | solution.py:724
  5.4 6.9 %collective-permute-start.1 = (f32[36,2,8,128]{3,2,1,0:T(8,128)}, f32[36,2,8,128]{3,2,1,0:T(8,128)S(1)}, u32[]{:S(2)}, u32[]{:S(2)}) collective-permute-start(f32[36,2,8,128]{3,2,1,0:T(8,128)} %get-tuple-element.9), channel_id=1, source_target_pairs={{8,0},{9,1},{10,2},{11,3},{12,4},{13,5},{14,6},{15,7},{16,8},{17,9... | collective-permute-start | bytes 884744 | tf_op jit(solution)/shard_map/ppermute | solution.py:724
  6.7 17.2 %collective-permute-start.2 = (f32[36,2,8,128]{3,2,1,0:T(8,128)}, f32[36,2,8,128]{3,2,1,0:T(8,128)S(1)}, u32[]{:S(2)}, u32[]{:S(2)}) collective-permute-start(f32[36,2,8,128]{3,2,1,0:T(8,128)} %get-tuple-element.10.own_hi), channel_id=1, source_target_pairs={{0,1},{1,2},{2,3},{3,4},{4,5},{5,6},{6,7},{8,9},{9,10},{10,11},{11... | collective-permute-start | bytes 884744 | tf_op jit(solution)/shard_map/ppermute | solution.py:724
  11.0 13.0 %collective-permute-start.3 = (f32[36,2,8,128]{3,2,1,0:T(8,128)}, f32[36,2,8,128]{3,2,1,0:T(8,128)S(1)}, u32[]{:S(2)}, u32[]{:S(2)}) collective-permute-start(f32[36,2,8,128]{3,2,1,0:T(8,128)} %get-tuple-element.11.own_lo), channel_id=1, source_target_pairs={{1,0},{2,1},{3,2},{4,3},{5,4},{6,5},{7,6},{9,8},{10,9},{11,10},{12... | collective-permute-start | bytes 884744 | tf_op jit(solution)/shard_map/ppermute | solution.py:724
  12.3 0.7 copy-start.1
  13.0 0.7 copy-start.2
  15.5 8.8 %collective-permute-start.4 = (f32[72,128]{1,0:T(8,128)}, f32[72,128]{1,0:T(8,128)S(1)}, u32[]{:S(2)}, u32[]{:S(2)}) collective-permute-start(f32[72,128]{1,0:T(8,128)} %get-tuple-element.12), channel_id=1, source_target_pairs={{0,1},{1,2},{2,3},{3,4},{4,5},{5,6},{6,7},{8,9},{9,10},{10,11},{11... | collective-permute-start | bytes 110600 | tf_op jit(solution)/shard_map/ppermute | solution.py:724
  20.1 6.5 %collective-permute-start.5 = (f32[72,128]{1,0:T(8,128)}, f32[72,128]{1,0:T(8,128)S(1)}, u32[]{:S(2)}, u32[]{:S(2)}) collective-permute-start(f32[72,128]{1,0:T(8,128)} %get-tuple-element.13), channel_id=1, source_target_pairs={{1,0},{2,1},{3,2},{4,3},{5,4},{6,5},{7,6},{9,8},{10,9},{11,10},{12... | collective-permute-start | bytes 110600 | tf_op jit(solution)/shard_map/ppermute | solution.py:724
  24.0 2.6 %copy-start.18 = (f32[36,2,8,128]{3,2,1,0:T(8,128)}, f32[36,2,8,128]{3,2,1,0:T(8,128)S(1)}, u32[]{:S(2)}) copy-start(f32[36,2,8,128]{3,2,1,0:T(8,128)S(1)} %collective-permute-done.2.ylo) | copy-start | bytes 884740
  24.0 2.6 %copy-start.19 = (f32[36,2,8,128]{3,2,1,0:T(8,128)}, f32[36,2,8,128]{3,2,1,0:T(8,128)S(1)}, u32[]{:S(2)}) copy-start(f32[36,2,8,128]{3,2,1,0:T(8,128)S(1)} %collective-permute-done.3.yhi) | copy-start | bytes 884740
  24.3 2.3 %copy-start.20 = (f32[72,128]{1,0:T(8,128)}, f32[72,128]{1,0:T(8,128)S(1)}, u32[]{:S(2)}) copy-start(f32[72,128]{1,0:T(8,128)S(1)} %collective-permute-done.4.edge_lo) | copy-start | bytes 110596
  26.5 0.6 copy-start.21
  34.7 7.6 %collective-permute-start.6 = (f32[1,296,128]{2,1,0:T(8,128)}, f32[1,296,128]{2,1,0:T(8,128)S(1)}, u32[]{:S(2)}, u32[]{:S(2)}) collective-permute-start(f32[1,296,128]{2,1,0:T(8,128)} %bitcast.10), channel_id=1, source_target_pairs={{0,1},{1,0},{2,3},{3,2},{4,5},{5,4},{6,7},{7,6},{8,9},{9,8},{10,11... | collective-permute-start | bytes 454664 | tf_op jit(solution)/shard_map/ppermute | solution.py:658
  37.6 9.6 %collective-permute-start.13 = (f32[1,296,128]{2,1,0:T(8,128)}, f32[1,296,128]{2,1,0:T(8,128)S(1)}, u32[]{:S(2)}, u32[]{:S(2)}) collective-permute-start(f32[1,296,128]{2,1,0:T(8,128)} %bitcast.11), channel_id=1, source_target_pairs={{0,6},{1,7},{2,4},{3,5},{4,2},{5,3},{6,0},{7,1},{8,14},{9,15},{10,... | collective-permute-start | bytes 454664 | tf_op jit(solution)/shard_map/ppermute | solution.py:658
  40.1 9.7 %collective-permute-start.7 = (f32[1,296,128]{2,1,0:T(8,128)}, f32[1,296,128]{2,1,0:T(8,128)S(1)}, u32[]{:S(2)}, u32[]{:S(2)}) collective-permute-start(f32[1,296,128]{2,1,0:T(8,128)} %bitcast.12), channel_id=1, source_target_pairs={{0,2},{1,3},{2,0},{3,1},{4,6},{5,7},{6,4},{7,5},{8,10},{9,11},{10,... | collective-permute-start | bytes 454664 | tf_op jit(solution)/shard_map/ppermute | solution.py:658
  40.8 13.8 %collective-permute-start.11 = (f32[1,296,128]{2,1,0:T(8,128)}, f32[1,296,128]{2,1,0:T(8,128)S(1)}, u32[]{:S(2)}, u32[]{:S(2)}) collective-permute-start(f32[1,296,128]{2,1,0:T(8,128)} %bitcast.13), channel_id=1, source_target_pairs={{0,4},{1,5},{2,6},{3,7},{4,0},{5,1},{6,2},{7,3},{8,12},{9,13},{10,... | collective-permute-start | bytes 454664 | tf_op jit(solution)/shard_map/ppermute | solution.py:658
  43.3 33.0 %copy-start = (f32[2,296,128]{2,1,0:T(8,128)}, f32[2,296,128]{2,1,0:T(8,128)S(1)}, u32[]{:S(2)}) copy-start(f32[2,296,128]{2,1,0:T(8,128)S(1)} %pad_maximum_fusion.refs_0_) | copy-start | bytes 909316
  43.3 18.2 %collective-permute-start.17 = (f32[2,296,128]{2,1,0:T(8,128)S(1)}, f32[2,296,128]{2,1,0:T(8,128)S(1)}, u32[]{:S(2)}, u32[]{:S(2)}) collective-permute-start(f32[2,296,128]{2,1,0:T(8,128)S(1)} %pad_maximum_fusion.refs_0_), channel_id=1, source_target_pairs={{0,8},{1,9},{2,10},{3,11},{4,12},{5,13},{6,14},{7,15},{8,0},{9,1},... | collective-permute-start | bytes 909320 | tf_op jit(solution)/shard_map/ppermute | solution.py:658
  43.4 19.9 %collective-permute-start.9 = (f32[2,296,128]{2,1,0:T(8,128)S(1)}, f32[2,296,128]{2,1,0:T(8,128)S(1)}, u32[]{:S(2)}, u32[]{:S(2)}) collective-permute-start(f32[2,296,128]{2,1,0:T(8,128)S(1)} %pad_maximum_fusion.refs_0_), channel_id=1, source_target_pairs={{0,16},{1,17},{2,18},{3,19},{4,20},{5,21},{6,22},{7,23},{8,24},{9,... | collective-permute-start | bytes 909320 | tf_op jit(solution)/shard_map/ppermute | solution.py:658
  47.2 11.3 %collective-permute-start.14 = (f32[1,296,128]{2,1,0:T(8,128)S(1)}, f32[1,296,128]{2,1,0:T(8,128)S(1)}, u32[]{:S(2)}, u32[]{:S(2)}) collective-permute-start(f32[1,296,128]{2,1,0:T(8,128)S(1)} %collective-permute-done.13), channel_id=1, source_target_pairs={{0,16},{1,17},{2,18},{3,19},{4,20},{5,21},{6,22},{7,23},{8,24},{9,... | collective-permute-start | bytes 454664 | tf_op jit(solution)/shard_map/ppermute | solution.py:658
  49.8 11.6 %collective-permute-start.8 = (f32[1,296,128]{2,1,0:T(8,128)S(1)}, f32[1,296,128]{2,1,0:T(8,128)S(1)}, u32[]{:S(2)}, u32[]{:S(2)}) collective-permute-start(f32[1,296,128]{2,1,0:T(8,128)S(1)} %collective-permute-done.7), channel_id=1, source_target_pairs={{0,16},{1,17},{2,18},{3,19},{4,20},{5,21},{6,22},{7,23},{8,24},{9,... | collective-permute-start | bytes 454664 | tf_op jit(solution)/shard_map/ppermute | solution.py:658
  54.6 5.2 %collective-permute-start.12 = (f32[1,296,128]{2,1,0:T(8,128)S(1)}, f32[1,296,128]{2,1,0:T(8,128)S(1)}, u32[]{:S(2)}, u32[]{:S(2)}) collective-permute-start(f32[1,296,128]{2,1,0:T(8,128)S(1)} %collective-permute-done.11), channel_id=1, source_target_pairs={{0,1},{1,0},{2,3},{3,2},{4,5},{5,4},{6,7},{7,6},{8,9},{9,8},{10,11... | collective-permute-start | bytes 454664 | tf_op jit(solution)/shard_map/ppermute | solution.py:658
  58.5 17.8 %copy-start.5 = (f32[2,296,128]{2,1,0:T(8,128)}, f32[2,296,128]{2,1,0:T(8,128)S(1)}, u32[]{:S(2)}) copy-start(f32[2,296,128]{2,1,0:T(8,128)S(1)} %constant_dynamic-update-slice_fusion.4.refs_5_) | copy-start | bytes 909316
  58.5 5.8 %collective-permute-start.22 = (f32[2,296,128]{2,1,0:T(8,128)S(1)}, f32[2,296,128]{2,1,0:T(8,128)S(1)}, u32[]{:S(2)}, u32[]{:S(2)}) collective-permute-start(f32[2,296,128]{2,1,0:T(8,128)S(1)} %constant_dynamic-update-slice_fusion.4.refs_5_), channel_id=1, source_target_pairs={{0,8},{1,9},{2,10},{3,11},{4,12},{5,13},{6,14},{7,15},{8,0},{9,1},... | collective-permute-start | bytes 909320 | tf_op jit(solution)/shard_map/ppermute | solution.py:658
  59.8 10.1 %collective-permute-start.16 = (f32[2,296,128]{2,1,0:T(8,128)S(1)}, f32[2,296,128]{2,1,0:T(8,128)S(1)}, u32[]{:S(2)}, u32[]{:S(2)}) collective-permute-start(f32[2,296,128]{2,1,0:T(8,128)S(1)} %constant_dynamic-update-slice_fusion.4.refs_5_), channel_id=1, source_target_pairs={{0,1},{1,0},{2,3},{3,2},{4,5},{5,4},{6,7},{7,6},{8,9},{9,8},{10,11... | collective-permute-start | bytes 909320 | tf_op jit(solution)/shard_map/ppermute | solution.py:658
  60.4 15.9 %copy-start.4 = (f32[2,296,128]{2,1,0:T(8,128)}, f32[2,296,128]{2,1,0:T(8,128)S(1)}, u32[]{:S(2)}) copy-start(f32[2,296,128]{2,1,0:T(8,128)S(1)} %constant_dynamic-update-slice_fusion.2.refs_4_) | copy-start | bytes 909316
  61.4 8.5 %collective-permute-start.21 = (f32[2,296,128]{2,1,0:T(8,128)S(1)}, f32[2,296,128]{2,1,0:T(8,128)S(1)}, u32[]{:S(2)}, u32[]{:S(2)}) collective-permute-start(f32[2,296,128]{2,1,0:T(8,128)S(1)} %constant_dynamic-update-slice_fusion.2.refs_4_), channel_id=1, source_target_pairs={{0,8},{1,9},{2,10},{3,11},{4,12},{5,13},{6,14},{7,15},{8,0},{9,1},... | collective-permute-start | bytes 909320 | tf_op jit(solution)/shard_map/ppermute | solution.py:658
  61.4 14.8 %copy-start.3 = (f32[2,296,128]{2,1,0:T(8,128)}, f32[2,296,128]{2,1,0:T(8,128)S(1)}, u32[]{:S(2)}) copy-start(f32[2,296,128]{2,1,0:T(8,128)S(1)} %constant_dynamic-update-slice_fusion.refs_1_) | copy-start | bytes 909316
  61.5 14.8 %copy-start.6 = (f32[2,296,128]{2,1,0:T(8,128)}, f32[2,296,128]{2,1,0:T(8,128)S(1)}, u32[]{:S(2)}) copy-start(f32[2,296,128]{2,1,0:T(8,128)S(1)} %collective-permute-done.17.refs_8_) | copy-start | bytes 909316
  61.5 9.7 %collective-permute-start.15 = (f32[2,296,128]{2,1,0:T(8,128)S(1)}, f32[2,296,128]{2,1,0:T(8,128)S(1)}, u32[]{:S(2)}, u32[]{:S(2)}) collective-permute-start(f32[2,296,128]{2,1,0:T(8,128)S(1)} %constant_dynamic-update-slice_fusion.2.refs_4_), channel_id=1, source_target_pairs={{0,16},{1,17},{2,18},{3,19},{4,20},{5,21},{6,22},{7,23},{8,24},{9,... | collective-permute-start | bytes 909320 | tf_op jit(solution)/shard_map/ppermute | solution.py:658
  63.3 13.0 %copy-start.7 = (f32[2,296,128]{2,1,0:T(8,128)}, f32[2,296,128]{2,1,0:T(8,128)S(1)}, u32[]{:S(2)}) copy-start(f32[2,296,128]{2,1,0:T(8,128)S(1)} %collective-permute-done.9.refs_2_) | copy-start | bytes 909316
  63.3 11.3 %collective-permute-start.10 = (f32[2,296,128]{2,1,0:T(8,128)S(1)}, f32[2,296,128]{2,1,0:T(8,128)S(1)}, u32[]{:S(2)}, u32[]{:S(2)}) collective-permute-start(f32[2,296,128]{2,1,0:T(8,128)S(1)} %constant_dynamic-update-slice_fusion.refs_1_), channel_id=1, source_target_pairs={{0,1},{1,0},{2,3},{3,2},{4,5},{5,4},{6,7},{7,6},{8,9},{9,8},{10,11... | collective-permute-start | bytes 909320 | tf_op jit(solution)/shard_map/ppermute | solution.py:658
  64.3 12.0 %copy-start.8 = (f32[2,296,128]{2,1,0:T(8,128)}, f32[2,296,128]{2,1,0:T(8,128)S(1)}, u32[]{:S(2)}) copy-start(f32[2,296,128]{2,1,0:T(8,128)S(1)} %collective-permute-done.22.refs_13_) | copy-start | bytes 909316
  64.3 10.3 %collective-permute-start.18 = (f32[2,296,128]{2,1,0:T(8,128)S(1)}, f32[2,296,128]{2,1,0:T(8,128)S(1)}, u32[]{:S(2)}, u32[]{:S(2)}) collective-permute-start(f32[2,296,128]{2,1,0:T(8,128)S(1)} %constant_dynamic-update-slice_fusion.refs_1_), channel_id=1, source_target_pairs={{0,8},{1,9},{2,10},{3,11},{4,12},{5,13},{6,14},{7,15},{8,0},{9,1},... | collective-permute-start | bytes 909320 | tf_op jit(solution)/shard_map/ppermute | solution.py:658
  69.9 6.4 %copy-start.9 = (f32[2,296,128]{2,1,0:T(8,128)}, f32[2,296,128]{2,1,0:T(8,128)S(1)}, u32[]{:S(2)}) copy-start(f32[2,296,128]{2,1,0:T(8,128)S(1)} %collective-permute-done.16.refs_7_) | copy-start | bytes 909316
  69.9 4.8 %collective-permute-start.19 = (f32[2,296,128]{2,1,0:T(8,128)S(1)}, f32[2,296,128]{2,1,0:T(8,128)S(1)}, u32[]{:S(2)}, u32[]{:S(2)}) collective-permute-start(f32[2,296,128]{2,1,0:T(8,128)S(1)} %collective-permute-done.9.refs_2_), channel_id=1, source_target_pairs={{0,8},{1,9},{2,10},{3,11},{4,12},{5,13},{6,14},{7,15},{8,0},{9,1},... | collective-permute-start | bytes 909320 | tf_op jit(solution)/shard_map/ppermute | solution.py:658
  69.9 6.4 %copy-start.10 = (f32[2,296,128]{2,1,0:T(8,128)}, f32[2,296,128]{2,1,0:T(8,128)S(1)}, u32[]{:S(2)}) copy-start(f32[2,296,128]{2,1,0:T(8,128)S(1)} %collective-permute-done.21.refs_12_) | copy-start | bytes 909316
  69.9 4.8 %collective-permute-start.24 = (f32[2,296,128]{2,1,0:T(8,128)S(1)}, f32[2,296,128]{2,1,0:T(8,128)S(1)}, u32[]{:S(2)}, u32[]{:S(2)}) collective-permute-start(f32[2,296,128]{2,1,0:T(8,128)S(1)} %collective-permute-done.16.refs_7_), channel_id=1, source_target_pairs={{0,8},{1,9},{2,10},{3,11},{4,12},{5,13},{6,14},{7,15},{8,0},{9,1},... | collective-permute-start | bytes 909320 | tf_op jit(solution)/shard_map/ppermute | solution.py:658
  71.2 5.1 %copy-start.11 = (f32[2,296,128]{2,1,0:T(8,128)}, f32[2,296,128]{2,1,0:T(8,128)S(1)}, u32[]{:S(2)}) copy-start(f32[2,296,128]{2,1,0:T(8,128)S(1)} %collective-permute-done.15.refs_6_) | copy-start | bytes 909316
  71.2 3.5 %collective-permute-start.23 = (f32[2,296,128]{2,1,0:T(8,128)S(1)}, f32[2,296,128]{2,1,0:T(8,128)S(1)}, u32[]{:S(2)}, u32[]{:S(2)}) collective-permute-start(f32[2,296,128]{2,1,0:T(8,128)S(1)} %collective-permute-done.15.refs_6_), channel_id=1, source_target_pairs={{0,8},{1,9},{2,10},{3,11},{4,12},{5,13},{6,14},{7,15},{8,0},{9,1},... | collective-permute-start | bytes 909320 | tf_op jit(solution)/shard_map/ppermute | solution.py:658
  74.6 1.7 %copy-start.12 = (f32[2,296,128]{2,1,0:T(8,128)}, f32[2,296,128]{2,1,0:T(8,128)S(1)}, u32[]{:S(2)}) copy-start(f32[2,296,128]{2,1,0:T(8,128)S(1)} %collective-permute-done.10.refs_3_) | copy-start | bytes 909316
  74.6 1.6 %collective-permute-start.20 = (f32[2,296,128]{2,1,0:T(8,128)S(1)}, f32[2,296,128]{2,1,0:T(8,128)S(1)}, u32[]{:S(2)}, u32[]{:S(2)}) collective-permute-start(f32[2,296,128]{2,1,0:T(8,128)S(1)} %collective-permute-done.10.refs_3_), channel_id=1, source_target_pairs={{0,8},{1,9},{2,10},{3,11},{4,12},{5,13},{6,14},{7,15},{8,0},{9,1},... | collective-permute-start | bytes 909320 | tf_op jit(solution)/shard_map/ppermute | solution.py:658
  74.6 1.7 %copy-start.13 = (f32[2,296,128]{2,1,0:T(8,128)}, f32[2,296,128]{2,1,0:T(8,128)S(1)}, u32[]{:S(2)}) copy-start(f32[2,296,128]{2,1,0:T(8,128)S(1)} %collective-permute-done.18.refs_9_) | copy-start | bytes 909316
  74.7 1.7 %copy-start.14 = (f32[2,296,128]{2,1,0:T(8,128)}, f32[2,296,128]{2,1,0:T(8,128)S(1)}, u32[]{:S(2)}) copy-start(f32[2,296,128]{2,1,0:T(8,128)S(1)} %collective-permute-done.19.refs_10_) | copy-start | bytes 909316
  74.7 1.7 %copy-start.15 = (f32[2,296,128]{2,1,0:T(8,128)}, f32[2,296,128]{2,1,0:T(8,128)S(1)}, u32[]{:S(2)}) copy-start(f32[2,296,128]{2,1,0:T(8,128)S(1)} %collective-permute-done.24.refs_15_) | copy-start | bytes 909316
  74.7 1.6 %copy-start.16 = (f32[2,296,128]{2,1,0:T(8,128)}, f32[2,296,128]{2,1,0:T(8,128)S(1)}, u32[]{:S(2)}) copy-start(f32[2,296,128]{2,1,0:T(8,128)S(1)} %collective-permute-done.23.refs_14_) | copy-start | bytes 909316
  76.2 0.7 copy-start.17
